TPU v7x, 512 devices: a whole 4x8x8 slice. The times are simulated.
512 devices in a mesh: dp: 8 (over z_hi, core), lat: 64 (over x, z_lo, y).
Axes of the slice: x: 4, y: 8, z: 8 (z_hi: 4, z_lo: 2; z = z_hi * 2 + z_lo), core: 2. Of those that a mesh axis runs over, the one named last changes fastest.
Arguments:
- query_feats: bfloat16 [8, 128, 128, 1024], P('dp', 'lat'), may hold values from -32 to 32
- key_feats: bfloat16 [8, 128, 128, 1024], P('dp', 'lat'), may hold values from -6 to 6
- value_feats: bfloat16 [8, 128, 128, 1024], P('dp', 'lat'), may hold values from -6 to 6
- out_grad: bfloat16 [8, 128, 128, 1024], P('dp', 'lat'), may hold values from -6 to 6
- out_proj: bfloat16 [1024, 1024], P('lat'), may hold values from -0.1875 to 0.1875
- cycle_lo: int32 [128], replicated, may hold values from 0 to 125, as said below
- cycle_hi: int32 [128], replicated, may hold values from 2 to 127, as said below
- lon_half: int32 [128], replicated, may hold values from 1 to 64, as said below
Outputs:
- query_grad: bfloat16 [8, 128, 128, 1024], P('dp', 'lat')
- key_grad: bfloat16 [8, 128, 128, 1024], P('dp', 'lat')
- value_grad: bfloat16 [8, 128, 128, 1024], P('dp', 'lat')
- proj_grad: float32 [1024, 1024], P('lat')
Inputs may be any that keep to these rules, and one draw needn't show every extreme that they name: cycle_lo[i] is i minus 1 to 2, not below 0; within 4 cycles of either pole it is max(i - 2, 0). cycle_hi[i] is i plus 1 to 2, not above 127; within 4 cycles of either pole it is min(i + 2, 127). `lon_half`: 64, the whole cycle, within 4 cycles of either pole; at most 32 elsewhere.
All inputs are finite; a program needn't handle non-finite values.
Results may differ from a plain program's by a relative error of at most 0.015.
Values may be sent and summed in bfloat16 or wider, within the bound.
No kernel may reach another device: no remote copies, remote signals or barrier semaphores. Data moves between devices by JAX's collectives and lax.ppermute only.
A program may use at most 192 MiB of HBM per device.

v0:
```python
import math

import jax
import jax.numpy as jnp
from jax import lax
from jax.sharding import PartitionSpec as P

HEADS = 16
HEAD_DIM = 64
REACH = 2


def padded(value, sides, width):
    for axis, dim in sides:
        size, length = (lax.axis_size(axis), value.shape[dim])
        up = [(i, (i + 1) % size) for i in range(size - 1)]
        down = [(j, i) for i, j in up]
        last = lax.slice_in_dim(value, length - width, length, axis=dim)
        first = lax.slice_in_dim(value, 0, width, axis=dim)
        before = lax.ppermute(last, axis, up)
        after = lax.ppermute(first, axis, down)
        value = jnp.concatenate([before, value, after], axis=dim)
    return value


def shifted(value, axis, by):
    size = lax.axis_size(axis)
    pairs = [(i, i + by) for i in range(size) if 0 <= i + by < size]
    return lax.ppermute(value, axis, pairs)


def cycle_log_weight(cycles, total):
    latitude = (cycles.astype(jnp.float32) + 0.5) * (math.pi / total)
    return jnp.log(jnp.sin(latitude))


def attend(query_heads, key_heads, value_heads, grad_heads, allowed, log_weight):
    scaling = 1.0 / math.sqrt(HEAD_DIM)
    scores = (
        jnp.einsum("qhd,khd->hqk", query_heads, key_heads, preferred_element_type=jnp.float32)
        * scaling
    )
    scores = scores + log_weight[None, None, :]
    scores = jnp.where(allowed[None], scores, -jnp.inf)
    row_peak = jnp.max(scores, axis=-1, keepdims=True)
    unnormed = jnp.exp(scores - row_peak)
    attention = unnormed / jnp.sum(unnormed, axis=-1, keepdims=True)
    attention_low = attention.astype(jnp.bfloat16)
    attended = jnp.einsum(
        "hqk,khd->qhd", attention_low, value_heads, preferred_element_type=jnp.float32
    ).astype(jnp.bfloat16)
    row_dot = jnp.sum(grad_heads.astype(jnp.float32) * attended.astype(jnp.float32), axis=-1)
    prob_grad = jnp.einsum(
        "qhd,khd->hqk", grad_heads, value_heads, preferred_element_type=jnp.float32
    )
    score_grad = (attention * (prob_grad - row_dot.T[:, :, None]) * scaling).astype(jnp.bfloat16)
    query_part = jnp.einsum(
        "hqk,khd->qhd", score_grad, key_heads, preferred_element_type=jnp.float32
    )
    key_part = jnp.einsum(
        "hqk,qhd->khd", score_grad, query_heads, preferred_element_type=jnp.float32
    )
    value_part = jnp.einsum(
        "hqk,qhd->khd", attention_low, grad_heads, preferred_element_type=jnp.float32
    )
    return (attended, query_part, key_part, value_part)


def split_heads(matrix, groups):
    count = matrix.shape[0]
    return jnp.moveaxis(matrix.reshape(count, groups, HEADS // groups, HEAD_DIM), 1, 0)


def join_heads(stacked):
    groups, count, per_group, head_size = stacked.shape
    return jnp.moveaxis(stacked, 0, 1).reshape(count, groups * per_group * head_size)


def local(query_feats, key_feats, value_feats, out_grad, out_proj, cycle_lo, cycle_hi, lon_half):
    cycles_here = query_feats.shape[1]
    lon_count = query_feats.shape[2]
    width = query_feats.shape[3]
    query_rows = cycles_here * lon_count
    grad_flat = out_grad.reshape(query_rows, width)
    attn_grad = jnp.dot(
        grad_flat,
        lax.all_gather(out_proj, "lat", axis=0, tiled=True).T,
        preferred_element_type=jnp.float32,
    ).astype(jnp.bfloat16)
    total_cycles = cycle_lo.shape[0]
    first_cycle = lax.axis_index("lat") * cycles_here
    longitude = jnp.arange(lon_count, dtype=jnp.int32)
    lon_gap = jnp.abs(longitude[:, None] - longitude[None, :])
    lon_dist = jnp.minimum(lon_gap, lon_count - lon_gap)
    groups = HEADS // 4
    stacked = jnp.stack([key_feats[0], value_feats[0]])
    extended = padded(stacked, (("lat", 1),), REACH)
    ext_cycles = cycles_here + 2 * REACH
    key_count = ext_cycles * lon_count
    lower = lax.dynamic_slice_in_dim(cycle_lo, first_cycle, cycles_here)
    upper = lax.dynamic_slice_in_dim(cycle_hi, first_cycle, cycles_here)
    half = lax.dynamic_slice_in_dim(lon_half, first_cycle, cycles_here)
    cycle_ids = first_cycle - REACH + jnp.arange(ext_cycles, dtype=jnp.int32)
    cycle_ok = (cycle_ids[None, :] >= lower[:, None]) & (cycle_ids[None, :] <= upper[:, None])
    lon_ok = lon_dist[None, :, :] <= half[:, None, None]
    allowed = (cycle_ok[:, None, :, None] & lon_ok[:, :, None, :]).reshape(query_rows, key_count)
    cycle_weight = cycle_log_weight(jnp.clip(cycle_ids, 0, total_cycles - 1), total_cycles)
    log_weight = jnp.broadcast_to(cycle_weight[:, None], (ext_cycles, lon_count)).reshape(key_count)
    inputs = (
        split_heads(query_feats.reshape(query_rows, width), groups),
        split_heads(extended[0].reshape(key_count, width), groups),
        split_heads(extended[1].reshape(key_count, width), groups),
        split_heads(attn_grad, groups),
    )

    def per_group(items):
        return attend(items[0], items[1], items[2], items[3], allowed, log_weight)

    attended, query_part, key_part, value_part = lax.map(per_group, inputs)
    attended = join_heads(attended)
    query_part = join_heads(query_part)
    grads = jnp.stack([join_heads(key_part), join_heads(value_part)]).reshape(
        2, ext_cycles, lon_count, width
    )
    low_rim = grads[:, :REACH]
    high_rim = grads[:, REACH + cycles_here :]
    own = grads[:, REACH : REACH + cycles_here]
    from_below = shifted(high_rim.astype(jnp.bfloat16), "lat", 1).astype(high_rim.dtype)
    from_above = shifted(low_rim.astype(jnp.bfloat16), "lat", -1).astype(low_rim.dtype)
    own = own + from_below
    own = own + from_above
    query_grad = query_part.astype(jnp.bfloat16).reshape(1, cycles_here, lon_count, width)
    key_grad = own[0].astype(jnp.bfloat16)[None]
    value_grad = own[1].astype(jnp.bfloat16)[None]
    scaling = 1.0 / math.sqrt(lax.axis_size("dp") * total_cycles * lon_count)
    band_rows = lax.psum_scatter(
        jnp.dot(attended.T, grad_flat, preferred_element_type=jnp.float32),
        "lat",
        scatter_dimension=0,
        tiled=True,
    )
    summed = lax.psum(band_rows.astype(jnp.bfloat16), "dp").astype(jnp.float32)
    proj_grad = summed * scaling
    return (query_grad, key_grad, value_grad, proj_grad)


def solution(mesh):
    placed = (
        P("dp", "lat", None, None),
        P("dp", "lat", None, None),
        P("dp", "lat", None, None),
        P("dp", "lat", None, None),
        P("lat", None),
        P(),
        P(),
        P(),
    )
    return jax.shard_map(
        local,
        mesh=mesh,
        in_specs=placed,
        out_specs=(
            P("dp", "lat", None, None),
            P("dp", "lat", None, None),
            P("dp", "lat", None, None),
            P("lat", None),
        ),
        check_vma=False,
    )
```

profile of v0, /device:TPU:1, one launch (start us, length us, event | category | flops | bytes accessed | tf_op | source)
XLA Modules:
  0.0 724.8 jit_solution(13180394751480178918)
XLA Ops:
  10.1 1.3 collective-permute-start.1
  11.4 5.7 collective-permute-start
  19.3 1.3 copy.20
  21.2 10.0 %collective-permute-done.1 = bf16[2,2,128,1024]{3,2,1,0:T(8,128)(2,1)} collective-permute-done((bf16[2,2,128,1024]{3,2,1,0:T(8,128)(2,1)S(1)}, bf16[2,2,128,1024]{3,2,1,0:T(8,128)(2,1)}, u32[]{:S(2)}, u32[]{:S(2)}) %collective-permute-start.1) | collective-permute-done | bytes 1048608 | tf_op jit(solution)/shard_map/ppermute | solution.py:21
  32.4 1.7 pad_maximum_fusion
  34.1 2.1 fusion.61
  36.2 3.2 copy.21
  39.5 2.7 reshape_reshape_squeeze.7
  42.2 3.2 copy.19
  45.4 2.8 reshape_reshape_squeeze.6
  48.2 226.9 %all-gather.2.cloned.1.call-done = bf16[1024,1024]{1,0:T(8,128)(2,1)} async-done(((bf16[16,1024]{1,0:T(8,128)(2,1)}), bf16[1024,1024]{1,0:T(8,128)(2,1)}) %all-gather.2.cloned.1.call-update) | async-done | bytes 2097168 | tf_op jit(solution)/shard_map/all_gather | solution.py:87
  275.2 3.1 convolution_convert_fusion.1
  278.3 1.2 copy.22
  279.5 44.8 %while.17 = (s32[]{:T(128)}, bf16[4,256,4,64]{1,3,2,0:T(8,128)(2,1)}, bf16[4,256,4,64]{1,3,2,0:T(8,128)(2,1)}, f32[4,768,4,64]{1,3,2,0:T(8,128)}, f32[4,768,4,64...) while((s32[]{:T(128)}, ...), condition=%wide.region_4.5_spmd.clone, body=%wide.region_0.4_spmd.clone.sunk | while | flops 613940992 | bytes 47252764 | solution.py:119
  279.9 2.9 fusion.99
  282.9 2.3 fusion.100
  285.2 1.3 bitcast_dynamic-update-slice_fusion.2
  288.2 1.3 fusion.102
  289.5 1.3 fusion.103
  291.2 2.9 fusion.99
  294.1 2.3 fusion.100
  296.4 1.2 bitcast_dynamic-update-slice_fusion.2
  299.4 1.3 fusion.102
  300.7 1.3 fusion.103
  302.4 2.9 fusion.99
  305.3 2.3 fusion.100
  307.6 1.3 bitcast_dynamic-update-slice_fusion.2
  310.6 1.3 fusion.102
  311.9 1.3 fusion.103
  313.6 2.9 fusion.99
  316.5 2.3 fusion.100
  318.8 1.3 bitcast_dynamic-update-slice_fusion.2
  321.8 1.3 fusion.102
  323.1 1.3 fusion.103
  324.4 3.7 fusion.63
  328.1 4.6 stack.12
  332.7 4.6 stack.11
  337.3 2.6 constant_dynamic-update-slice_fusion.3
  341.8 2.5 copy-done.2
  344.3 2.5 fusion.60
  346.7 1.5 collective-permute-start.2
  348.2 1.5 collective-permute-start.3
  349.7 1.2 convert_element_type.66
  352.0 8.2 %collective-permute-done.2 = bf16[2,2,128,1024]{2,1,3,0:T(2,128)(2,1)S(1)} collective-permute-done((bf16[2,2,128,1024]{2,1,3,0:T(2,128)(2,1)}, bf16[2,2,128,1024]{2,1,3,0:T(2,128)(2,1)S(1)}, u32[]{:S(2)}, u32[]{:S(2)}) %collective-permute-start.2) | collective-permute-done | bytes 1048608 | tf_op jit(solution)/shard_map/ppermute | solution.py:29
  360.2 3.8 collective-permute-done.3
  364.0 4.5 fusion.54
  371.4 273.1 %reduce-scatter.2.cloned.1.call-done = f32[16,1024]{1,0:T(8,128)} async-done(((f32[1024,1024]{1,0:T(8,128)}), f32[16,1024]{1,0:T(8,128)}) %reduce-scatter.2.cloned.1.call-update) | async-done | bytes 65552 | tf_op jit(solution)/shard_map/reduce_scatter | solution.py:136
  645.4 71.9 %psum.7 = bf16[16,1024]{1,0:T(8,128)(2,1)S(1)} all-reduce(bf16[16,1024]{1,0:T(8,128)(2,1)S(1)} %convert_element_type.69), channel_id=1, replica_groups=mesh['dp'=8,'lat'=64] {'dp'}, use_global_device_ids=true, to_apply=%region_6.7 | all-reduce | flops 16384 | bytes 65536 | tf_op jit(solution)/shard_map/psum | solution.py:142
  (91 shorter events, 22.7 us)
Async XLA Ops:
  7.2 268.0 %copy-start = (bf16[1,2,128,1024]{3,2,1,0:T(8,128)(2,1)S(1)}, bf16[1,2,128,1024]{3,2,1,0:T(8,128)(2,1)}, u32[]{:S(2)}) copy-start(bf16[1,2,128,1024]{3,2,1,0:T(8,128)(2,1)} %param.13) | copy-start | bytes 1572868
  7.2 268.0 %all-gather.2.cloned.1.call-start = ((), (), s32[]{:S(2)}) async-start(), calls=%async_computation.1 | async-start | bytes 2129920 | tf_op jit(solution)/shard_map/all_gather | solution.py:87
  7.9 636.6 %reduce-scatter.2.cloned.1.call-start = ((), (), s32[]{:S(2)}) async-start(), calls=%async_computation.2 | async-start | bytes 4259840 | tf_op jit(solution)/shard_map/reduce_scatter | solution.py:136
  10.1 21.1 %collective-permute-start.1 = (bf16[2,2,128,1024]{3,2,1,0:T(8,128)(2,1)S(1)}, bf16[2,2,128,1024]{3,2,1,0:T(8,128)(2,1)}, u32[]{:S(2)}, u32[]{:S(2)}) collective-permute-start(bf16[2,2,128,1024]{3,2,1,0:T(8,128)(2,1)S(1)} %constant_dynamic-update-slice_fusion), channel_id=1, source_target_pairs={{1,0},{2,1},{3,2},{4,3},{5,4},{6,5},{7,6},{8,7},{9,8},{10,9},{11,1... | collective-permute-start | bytes 3145736 | tf_op jit(solution)/shard_map/ppermute | solution.py:21
  11.4 21.0 %collective-permute-start = (bf16[2,2,128,1024]{3,2,1,0:T(8,128)(2,1)S(1)}, bf16[2,2,128,1024]{3,2,1,0:T(8,128)(2,1)}, u32[]{:S(2)}, u32[]{:S(2)}) collective-permute-start(bf16[2,2,128,1024]{3,2,1,0:T(8,128)(2,1)S(1)} %constant_dynamic-update-slice_fusion), channel_id=1, source_target_pairs={{0,1},{1,2},{2,3},{3,4},{4,5},{5,6},{6,7},{7,8},{8,9},{9,10},{10,1... | collective-permute-start | bytes 3145736 | tf_op jit(solution)/shard_map/ppermute | solution.py:20
  48.2 231.3 %copy-start.4 = (bf16[768,4,4,64]{0,3,2,1:T(8,128)(2,1)S(1)}, bf16[768,4,4,64]{0,3,2,1:T(8,128)(2,1)}, u32[]{:S(2)}) copy-start(bf16[768,4,4,64]{0,3,2,1:T(8,128)(2,1)} %reshape_reshape_squeeze.7) | copy-start | bytes 4718596
  282.8 2.4 copy-start.5
  282.9 3.7 copy-start.1
  286.5 1.0 copy-start.6
  288.2 2.6 copy-start.7
  294.1 2.4 copy-start.5
  294.1 3.7 copy-start.1
  297.8 1.0 copy-start.6
  299.4 2.6 copy-start.7
  305.3 2.4 copy-start.5
  305.3 3.7 copy-start.1
  308.9 1.0 copy-start.6
  310.6 2.6 copy-start.7
  316.5 2.4 copy-start.5
  316.5 3.7 copy-start.1
  320.1 1.0 copy-start.6
  321.8 2.6 copy-start.7
  337.3 3.4 copy-start.3
  341.0 3.2 copy-start.2
  346.7 13.5 %collective-permute-start.2 = (bf16[2,2,128,1024]{2,1,3,0:T(2,128)(2,1)}, bf16[2,2,128,1024]{2,1,3,0:T(2,128)(2,1)S(1)}, u32[]{:S(2)}, u32[]{:S(2)}) collective-permute-start(bf16[2,2,128,1024]{2,1,3,0:T(2,128)(2,1)} %get-tuple-element.130), channel_id=1, source_target_pairs={{0,1},{1,2},{2,3},{3,4},{4,5},{5,6},{6,7},{7,8},{8,9},{9,10},{10,1... | collective-permute-start | bytes 3145736 | tf_op jit(solution)/shard_map/ppermute | solution.py:29
  348.2 15.8 %collective-permute-start.3 = (bf16[2,2,128,1024]{2,1,3,0:T(2,128)(2,1)}, bf16[2,2,128,1024]{2,1,3,0:T(2,128)(2,1)S(1)}, u32[]{:S(2)}, u32[]{:S(2)}) collective-permute-start(bf16[2,2,128,1024]{2,1,3,0:T(2,128)(2,1)} %get-tuple-element.131), channel_id=1, source_target_pairs={{1,0},{2,1},{3,2},{4,3},{5,4},{6,5},{7,6},{8,7},{9,8},{10,9},{11,1... | collective-permute-start | bytes 3145736 | tf_op jit(solution)/shard_map/ppermute | solution.py:29
Sparse Core Ops, SparseCore 0:
  10.1 265.0 all-gather.1
  328.3 316.2 reduce-scatter.1
where the time goes:
time: 726 us; the launch traced here: 725 us
  waiting for transfers between devices  524 us (72%)
  blocking collectives  71.9 us (10%)
  local copies, waits for them, and re-layouts  46 us (6%)
  matrix products  39.6 us (5%)
  other arithmetic  18.8 us (3%)
  between operations  14.2 us (2%)
  starting transfers between devices  9.99 us (1%)
    reduce_scatter x1, waiting for transfers between devices, local(): lax.psum_scatter(jnp.dot(attended.T, grad_flat, preferred_element_type=jn...  273 us
    all_gather x1, waiting for transfers between devices, local(): lax.all_gather(out_proj, 'lat', axis=0, tiled=True)  227 us
    psum x1, blocking collectives, local(): summed = lax.psum(band_rows.astype(jnp.bfloat16), 'dp').astype(jnp.float32)  71.9 us
  transfers between devices with their start and end apart: 6, of which 6 were waited for; matrix products, arithmetic and copies ran while one was open for 6% of the time, Pallas kernels for 0%

commit v1 on v0

v1 whole, which is shorter than its diff:
```python
import functools
import math

import jax
import jax.numpy as jnp
import numpy as np
from jax import lax
from jax.experimental import pallas as pl
from jax.experimental.pallas import tpu as pltpu
from jax.sharding import Mesh
from jax.sharding import PartitionSpec as P

HEADS = 16
HEAD_DIM = 64
REACH = 2
PAIR = 2 * HEAD_DIM
SCALE = 1.0 / math.sqrt(HEAD_DIM)
SPAN = 2 * REACH + 1
DP = ("zh", "core")
XZ = ("x", "zl")
LAT = ("x", "zl", "y")
BF = jnp.bfloat16
F32 = jnp.float32
VMEM_LIMIT = 48 * 1024 * 1024


def dot(a, b, dims):
    return lax.dot_general(a, b, (dims, ((), ())), preferred_element_type=F32)


def fill_bias(first, lo_ref, hi_ref, half_ref, logw_ref, bias_ref):
    cycles, _, lon = bias_ref.shape
    total = lo_ref.shape[0]
    key_lon = lax.broadcasted_iota(jnp.int32, (lon, lon), 0)
    query_lon = lax.broadcasted_iota(jnp.int32, (lon, lon), 1)
    gap = jnp.abs(key_lon - query_lon)
    dist = jnp.minimum(gap, lon - gap)
    for i in range(cycles):
        cycle = first + i
        lon_ok = dist <= half_ref[cycle]
        for c in range(SPAN):
            key_cycle = cycle - REACH + c
            ok = (key_cycle >= lo_ref[cycle]) & (key_cycle <= hi_ref[cycle])
            weight = logw_ref[jnp.clip(key_cycle, 0, total - 1)]
            value = jnp.where(ok, weight, -jnp.inf)
            bias_ref[i, c * lon : (c + 1) * lon, :] = jnp.where(lon_ok, value, -jnp.inf)


def head_masks(scale):
    lane = lax.broadcasted_iota(jnp.int32, (1, PAIR), 1)
    first = jnp.where(lane < HEAD_DIM, scale, 0.0).astype(F32)
    return first, scale - first


def both_heads(rows, scale):
    first, second = head_masks(scale)
    wide = rows.astype(F32)
    return jnp.concatenate([(wide * first).astype(BF), (wide * second).astype(BF)], axis=0)


def own_columns(both, lon):
    return jnp.concatenate([both[:HEAD_DIM, :lon], both[HEAD_DIM:, lon:]], axis=0).T


def forward_kernel(
    first_ref, lo_ref, hi_ref, half_ref, logw_ref,
    q_ref, kp_ref, ko_ref, kn_ref, vp_ref, vo_ref, vn_ref,
    out_ref, prob_ref, bias_ref,
):
    cycles, _, lon = bias_ref.shape

    @pl.when(pl.program_id(0) == 0)
    def _():
        fill_bias(first_ref[0], lo_ref, hi_ref, half_ref, logw_ref, bias_ref)

    keys = jnp.concatenate([kp_ref[0], ko_ref[...], kn_ref[0]], axis=0)
    values = jnp.concatenate([vp_ref[0], vo_ref[...], vn_ref[0]], axis=0)
    for i in range(cycles):
        window = slice(i * lon, (i + SPAN) * lon)
        rows = slice(i * lon, (i + 1) * lon)
        queries = both_heads(q_ref[rows, :], SCALE)
        scores = dot(keys[window], queries, ((1,), (1,)))
        bias = bias_ref[i]
        scores = scores + jnp.concatenate([bias, bias], axis=1)
        weights = jnp.exp(scores - jnp.max(scores, axis=0, keepdims=True))
        inverse = 1.0 / jnp.sum(weights, axis=0, keepdims=True)
        probs = (weights * inverse).astype(BF)
        prob_ref[0, i] = probs
        attended = dot(values[window], probs, ((0,), (0,)))
        out_ref[rows, :] = own_columns(attended, lon).astype(BF)


def backward_kernel(
    q_ref, g_ref, o_ref, prob_ref, kp_ref, ko_ref, kn_ref, vp_ref, vo_ref, vn_ref,
    dq_ref, low_ref, own_ref, high_ref,
):
    cycles = prob_ref.shape[1]
    lon = prob_ref.shape[2] // SPAN
    keys = jnp.concatenate([kp_ref[0], ko_ref[...], kn_ref[0]], axis=0)
    values = jnp.concatenate([vp_ref[0], vo_ref[...], vn_ref[0]], axis=0)
    parts = []
    for i in range(cycles):
        window = slice(i * lon, (i + SPAN) * lon)
        rows = slice(i * lon, (i + 1) * lon)
        queries = both_heads(q_ref[rows, :], SCALE)
        grads = both_heads(g_ref[rows, :], 1.0)
        product = (g_ref[rows, :].astype(F32) * o_ref[rows, :].astype(F32)).T
        row_dot = jnp.concatenate(
            [
                jnp.sum(product[:HEAD_DIM], axis=0, keepdims=True),
                jnp.sum(product[HEAD_DIM:], axis=0, keepdims=True),
            ],
            axis=1,
        )
        probs = prob_ref[0, i]
        prob_grad = dot(values[window], grads, ((1,), (1,)))
        score_grad = (probs.astype(F32) * (prob_grad - row_dot)).astype(BF)
        query_part = dot(keys[window], score_grad, ((0,), (0,)))
        dq_ref[rows, :] = (own_columns(query_part, lon) * SCALE).astype(BF)
        key_part = dot(score_grad, queries, ((1,), (0,)))
        value_part = dot(probs, grads, ((1,), (0,)))
        parts.append((key_part, value_part))
    for which in range(2):
        near, far = parts[0][which], parts[1][which]
        low_ref[which, :lon] = near[:lon].astype(BF)
        low_ref[which, lon:] = (near[lon : 2 * lon] + far[:lon]).astype(BF)
        own_ref[which] = (near[2 * lon : 4 * lon] + far[lon : 3 * lon]).astype(own_ref.dtype)
        high_ref[which, :lon] = (near[4 * lon :] + far[3 * lon : 4 * lon]).astype(BF)
        high_ref[which, lon:] = far[4 * lon :].astype(BF)


def forward(first, lo, hi, half, logw, q, k, v, below, above, lon):
    rows, width = q.shape
    cycles = rows // lon
    pairs = width // PAIR
    smem = pl.BlockSpec(memory_space=pltpu.SMEM)
    flat = pl.BlockSpec((rows, PAIR), lambda p: (0, p))
    key = pl.BlockSpec((1, rows, PAIR), lambda p: (0, 0, p))
    value = pl.BlockSpec((1, rows, PAIR), lambda p: (1, 0, p))
    return pl.pallas_call(
        forward_kernel,
        grid=(pairs,),
        in_specs=[smem] * 5 + [flat, key, flat, key, value, flat, value],
        out_specs=[flat, pl.BlockSpec((1, cycles, SPAN * lon, 2 * lon), lambda p: (p, 0, 0, 0))],
        out_shape=[
            jax.ShapeDtypeStruct((rows, width), BF),
            jax.ShapeDtypeStruct((pairs, cycles, SPAN * lon, 2 * lon), BF),
        ],
        scratch_shapes=[pltpu.VMEM((cycles, SPAN * lon, lon), F32)],
        compiler_params=pltpu.CompilerParams(vmem_limit_bytes=VMEM_LIMIT),
        cost_estimate=pl.CostEstimate(flops=4 * 10**9, bytes_accessed=12 * 10**6, transcendentals=3 * 10**6),
        name="attention_forward",
    )(first, lo, hi, half, logw, q, below, k, above, below, v, above)


def backward(q, g, o, probs, k, v, below, above, lon):
    rows, width = q.shape
    cycles = rows // lon
    pairs = width // PAIR
    flat = pl.BlockSpec((rows, PAIR), lambda p: (0, p))
    key = pl.BlockSpec((1, rows, PAIR), lambda p: (0, 0, p))
    value = pl.BlockSpec((1, rows, PAIR), lambda p: (1, 0, p))
    both = pl.BlockSpec((2, rows, PAIR), lambda p: (0, 0, p))
    prob = pl.BlockSpec((1, cycles, SPAN * lon, 2 * lon), lambda p: (p, 0, 0, 0))
    stacked = jax.ShapeDtypeStruct((2, rows, width), BF)
    return pl.pallas_call(
        backward_kernel,
        grid=(pairs,),
        in_specs=[flat, flat, flat, prob, key, flat, key, value, flat, value],
        out_specs=[flat, both, both, both],
        out_shape=[
            jax.ShapeDtypeStruct((rows, width), BF),
            stacked,
            jax.ShapeDtypeStruct((2, rows, width), F32),
            stacked,
        ],
        compiler_params=pltpu.CompilerParams(vmem_limit_bytes=VMEM_LIMIT),
        cost_estimate=pl.CostEstimate(flops=8 * 10**9, bytes_accessed=16 * 10**6, transcendentals=0),
        name="attention_backward",
    )(q, g, o, probs, below, k, above, below, v, above)


def lat_shift(value, by):
    size = lax.axis_size(LAT)
    pairs = [(i, i + by) for i in range(size) if 0 <= i + by < size]
    return lax.ppermute(value, LAT, pairs)


def core_swap(value):
    return lax.ppermute(value, "core", [(0, 1), (1, 0)])


def spread(value, axes):
    size = lax.axis_size(axes)
    return lax.all_to_all(
        jnp.broadcast_to(value[None], (size,) + value.shape), axes, 0, 0, tiled=True
    )


def scatter_sum(value, axes):
    size = lax.axis_size(axes)
    blocks = value.reshape((size, value.shape[0] // size) + value.shape[1:])
    received = lax.all_to_all(blocks, axes, 0, 0, tiled=True)
    return jnp.sum(received.astype(F32), axis=0)


def local(query_feats, key_feats, value_feats, out_grad, out_proj, cycle_lo, cycle_hi, lon_half):
    cycles, lon, width = query_feats.shape[1:]
    rows = cycles * lon
    total = cycle_lo.shape[0]
    half_width = width // 2
    q = query_feats.reshape(rows, width)
    k = key_feats.reshape(rows, width)
    v = value_feats.reshape(rows, width)
    grad_flat = out_grad.reshape(rows, width)
    core = lax.axis_index("core")
    mine, others = core * half_width, (1 - core) * half_width

    stacked = jnp.stack([k, v])
    below = lat_shift(stacked, 1)
    above = lat_shift(stacked, -1)

    proj = lax.dynamic_slice_in_dim(out_proj, mine, half_width, axis=1)
    proj = spread(proj, "y").reshape(-1, half_width)
    proj = spread(proj, XZ).reshape(-1, half_width)
    proj_other = core_swap(proj)
    grad_mine = lax.dynamic_slice_in_dim(grad_flat, mine, half_width, axis=1)
    grad_other = lax.dynamic_slice_in_dim(grad_flat, others, half_width, axis=1)

    latitude = (np.arange(total, dtype=np.float32) + np.float32(0.5)) * np.float32(math.pi / total)
    logw = jnp.asarray(np.log(np.sin(latitude)).astype(np.float32))
    first = (lax.axis_index(LAT) * cycles).astype(jnp.int32).reshape(1)
    attended, probs = forward(
        first, cycle_lo, cycle_hi, lon_half, logw, q, k, v, below, above, lon
    )

    sent = dot(attended, grad_other, ((0,), (0,))).astype(BF)
    received = core_swap(sent)

    attn_grad = dot(grad_mine, proj, ((1,), (1,))) + dot(grad_other, proj_other, ((1,), (1,)))
    attn_grad = attn_grad.astype(BF)
    query_grad, low, own, high = backward(q, attn_grad, attended, probs, k, v, below, above, lon)
    from_below = lat_shift(high, 1)
    from_above = lat_shift(low, -1)

    partial = (dot(attended, grad_mine, ((0,), (0,))) + received.astype(F32)).astype(BF)
    partial = scatter_sum(partial, XZ).astype(BF)
    partial = scatter_sum(partial, "y").astype(BF)
    samples = lax.axis_size(DP)
    gathered = spread(partial, DP).reshape((samples // 2, 2) + partial.shape)
    summed = jnp.sum(gathered.astype(F32), axis=0)
    scaling = 1.0 / math.sqrt(samples * total * lon)
    proj_grad = jnp.concatenate([summed[0], summed[1]], axis=1) * scaling

    own = own + from_below.astype(F32) + from_above.astype(F32)
    shape = query_feats.shape
    return (
        query_grad.reshape(shape),
        own[0].astype(BF).reshape(shape),
        own[1].astype(BF).reshape(shape),
        proj_grad,
    )


def solution(mesh):
    parts = Mesh(mesh.devices.reshape(4, 2, 4, 2, 8), DP + LAT)
    placed = P(DP, LAT, None, None)
    return jax.shard_map(
        local,
        mesh=parts,
        in_specs=(placed, placed, placed, placed, P(LAT, None), P(), P(), P()),
        out_specs=(placed, placed, placed, P(LAT, None)),
        check_vma=False,
    )
```

time: 726 us -> 147 us (0.20)
  waiting for transfers between devices: 524 us -> 17.1 us
  blocking collectives: 71.9 us -> 26.5 us
  starting transfers between devices: 9.99 us -> 54.3 us
  local copies, waits for them, and re-layouts: 46 us -> 5.42 us
  matrix products: 39.6 us -> 7.59 us
  Pallas kernels: 0 us -> 26.1 us
  between operations: 14.2 us -> 0.83 us
  other arithmetic: 18.8 us -> 6.76 us
    reduce_scatter x1 -> x0, waiting for transfers between devices: 273 us -> none  [local(): lax.psum_scatter(jnp.dot(attended.T, grad_flat, preferred_element_type=jn...]
    all_gather x1 -> x0, waiting for transfers between devices: 227 us -> none  [local(): lax.all_gather(out_proj, 'lat', axis=0, tiled=True)]
    psum x1 -> x0, blocking collectives: 71.9 us -> none  [local(): summed = lax.psum(band_rows.astype(jnp.bfloat16), 'dp').astype(jnp.float32)]
    all_to_all x0 -> x4, starting transfers between devices: none -> 37.1 us  [the longest x3 25.3 us: spread(): lax.all_to_all(jnp.broadcast_to(value[None], (size,) + value.shape), axes...]
    all_to_all x0 -> x1, blocking collectives: none -> 26.5 us  [scatter_sum(): received = lax.all_to_all(blocks, axes, 0, 0, tiled=True)]
    pallas_call x0 -> x2, Pallas kernels: none -> 26.1 us  [the longest x1 14 us: forward(): pl.pallas_call(forward_kernel, grid=(pairs,), in_specs=[smem] * 5 + [flat...]
    dot_general x22 -> x4, matrix products: 28 us -> 7.59 us  [dot(): return lax.dot_general(a, b, (dims, ((), ())), preferred_element_type=F32)]
    another operation x7 -> x0, local copies, waits for them, and re-layouts: 16.4 us -> none  [the longest x3 9.46 us: local(): jnp.stack([join_heads(key_part), join_heads(value_part)])]
  transfers between devices with their start and end apart: 6 -> 10, of which waited for: 6 -> 4; matrix products, arithmetic and copies ran while one was open for 6% -> 11% of each run, Pallas kernels for 0% -> 18%
where the time goes in v1:
time: 147 us; the launch traced here: 145 us
  starting transfers between devices  54.3 us (37%)
  blocking collectives  26.5 us (18%)
  Pallas kernels  26.1 us (18%)
  waiting for transfers between devices  17.1 us (12%)
  matrix products  7.59 us (5%)
  other arithmetic  6.76 us (5%)
  local copies, waits for them, and re-layouts  5.42 us (4%)
    all_to_all x1, blocking collectives, scatter_sum(): received = lax.all_to_all(blocks, axes, 0, 0, tiled=True)  26.5 us
    all_to_all x3, starting transfers between devices, spread(): lax.all_to_all(jnp.broadcast_to(value[None], (size,) + value.shape), axes...  25.3 us
    pallas_call x1, Pallas kernels, forward(): pl.pallas_call(forward_kernel, grid=(pairs,), in_specs=[smem] * 5 + [flat...  14 us
    pallas_call x1, Pallas kernels, backward(): pl.pallas_call(backward_kernel, grid=(pairs,), in_specs=[flat, flat, flat...  12.1 us
    all_to_all x1, starting transfers between devices, scatter_sum(): received = lax.all_to_all(blocks, axes, 0, 0, tiled=True)  11.8 us
    ppermute x4, waiting for transfers between devices, lat_shift(): return lax.ppermute(value, LAT, pairs)  11.7 us
    ppermute x4, starting transfers between devices, lat_shift(): return lax.ppermute(value, LAT, pairs)  9.11 us
    ppermute x2, starting transfers between devices, core_swap(): return lax.ppermute(value, 'core', [(0, 1), (1, 0)])  8.07 us
  transfers between devices with their start and end apart: 10, of which 4 were waited for; matrix products, arithmetic and copies ran while one was open for 11% of the time, Pallas kernels for 18%

profile of v1, /device:TPU:1, one launch (start us, length us, event | category | flops | bytes accessed | tf_op | source)
XLA Modules:
  0.0 144.6 jit_solution(4161036127957624291)
XLA Ops:
  0.6 0.0 copy-start
  0.7 0.8 constant_dynamic-slice_fusion
  1.4 0.7 broadcast_in_dim.8
  2.1 7.7 %all-to-all-start = ((bf16[8,16,512]{2,1,0:T(8,128)(2,1)}), bf16[8,16,512]{2,1,0:T(8,128)(2,1)S(1)}, u32[]{:S(2)}, u32[]{:S(2)}) async-start(bf16[8,16,512]{2,1,0:T(8,128)(2,1)} %broadcast_in_dim.8), calls=%async_computation | async-start | bytes 262144 | tf_op jit(solution)/shard_map/all_to_all | solution.py:195
  9.8 2.3 %pad_maximum_fusion = bf16[2,256,1024]{2,1,0:T(8,128)(2,1)} fusion(bf16[1,256,1024]{2,1,0:T(8,128)(2,1)} %bitcast.28, bf16[1,256,1024]{2,1,0:T(8,128)(2,1)} %bitcast.31), kind=kLoop, calls=%fused_computation.5 | loop fusion | flops 524288 | bytes 2097152 | tf_op jit(solution)/shard_map/stack | solution.py:219
  12.0 0.0 copy-start.8
  12.1 0.0 copy-start.9
  12.1 1.4 collective-permute-start.2
  13.5 5.0 %collective-permute-start.1 = (bf16[2,256,1024]{2,1,0:T(8,128)(2,1)}, bf16[2,256,1024]{2,1,0:T(8,128)(2,1)}, u32[]{:S(2)}, u32[]{:S(2)}) collective-permute-start(bf16[2,256,1024]{2,1,0:T(8,128)(2,1)} %pad_maximum_fusion), channel_id=1, source_target_pairs={{0,1},{1,2},{2,3},{3,4},{4,5},{5,6},{6,7},{7,8},{8,9},{9,10},{10,1... | collective-permute-start | bytes 3145736 | tf_op jit(solution)/shard_map/ppermute | solution.py:186
  18.5 0.0 all-to-all-done
  18.5 1.1 broadcast_in_dim.10
  19.6 6.0 %all-to-all-start.1 = ((bf16[8,128,512]{2,1,0:T(8,128)(2,1)}), bf16[8,128,512]{2,1,0:T(8,128)(2,1)}, u32[]{:S(2)}, u32[]{:S(2)}) async-start(bf16[8,128,512]{2,1,0:T(8,128)(2,1)} %broadcast_in_dim.10), calls=%async_computation.1 | async-start | bytes 2097152 | tf_op jit(solution)/shard_map/all_to_all | solution.py:195
  25.6 11.5 %collective-permute-done.2.kn_ref.vn_ref = bf16[2,256,1024]{2,1,0:T(8,128)(2,1)S(1)} collective-permute-done((bf16[2,256,1024]{2,1,0:T(8,128)(2,1)}, bf16[2,256,1024]{2,1,0:T(8,128)(2,1)S(1)}, u32[]{:S(2)}, u32[]{:S(2)}) %collective-permute-start.2) | collective-permute-done | bytes 1048608 | tf_op jit(solution)/shard_map/ppermute | solution.py:186
  37.1 0.2 collective-permute-done.1.kp_ref.vp_ref
  37.4 0.0 copy-done.1
  37.4 0.0 copy-done.2
  37.4 0.0 copy-done.6
  37.4 0.0 copy-done.7
  37.4 0.0 copy-done.8
  37.4 0.0 copy-done.9
  37.4 0.0 copy-start.4
  37.4 1.2 copy-done.4
  38.6 14.0 %attention_forward.1 = (bf16[256,1024]{1,0:T(8,128)(2,1)S(1)}, bf16[8,2,640,256]{3,2,1,0:T(8,128)(2,1)}) custom-call(s32[1]{0:T(128)} %bitcast.4.first_ref, s32[128]{0:T(128)S(1)} %copy-done.6, s32[128]{0:T(128)S(1)} %copy-done.7, s32[128]{0:T(128)S(1)} %copy-done.8, f32[128]{0:T(128)S(1)} %copy-done.9, bf16[256,1024]{1,0:T(8,128)(2,1)S(1)} %bitcast.34, ...), custom_call_target="tpu_custom_call" | custom-call | flops 4000000000 | bytes 12000000 | tf_op jit(solution)/shard_map/attention_forward/pallas_call | solution.py:140
  52.6 1.5 %convolution_convert_fusion = bf16[1024,512]{1,0:T(8,128)(2,1)} fusion(bf16[256,1024]{1,0:T(8,128)(2,1)S(1)} %get-tuple-element.10.o_ref, bf16[256,1024]{1,0:T(8,128)(2,1)S(1)} %bitcast.26, s32[]{:T(128)S(6)} %select_n.8), kind=kOutput, calls=%fused_computation.2 | convolution fusion | flops 268959744 | bytes 1835012 | tf_op jit(solution)/shard_map/dot_general | solution.py:28
  54.1 5.6 %collective-permute-start.5 = (bf16[1024,512]{1,0:T(8,128)(2,1)}, bf16[1024,512]{1,0:T(8,128)(2,1)}, u32[]{:S(2)}, u32[]{:S(2)}) collective-permute-start(bf16[1024,512]{1,0:T(8,128)(2,1)} %convolution_convert_fusion), channel_id=1, source_target_pairs={{0,64},{64,0},{1,65},{65,1},{2,66},{66,2},{3,67},{67,3},{4,68},{68... | collective-permute-start | bytes 3145736 | tf_op jit(solution)/shard_map/ppermute | solution.py:190
  59.6 0.1 all-to-all-done.1
  59.7 2.5 %collective-permute-start = (bf16[1024,512]{1,0:T(8,128)(2,1)}, bf16[1024,512]{1,0:T(8,128)(2,1)}, u32[]{:S(2)}, u32[]{:S(2)}) collective-permute-start(bf16[1024,512]{1,0:T(8,128)(2,1)} %bitcast.3), channel_id=1, source_target_pairs={{0,64},{64,0},{1,65},{65,1},{2,66},{66,2},{3,67},{67,3},{4,68},{68... | collective-permute-start | bytes 3145736 | tf_op jit(solution)/shard_map/ppermute | solution.py:190
  62.2 1.7 %fusion.4 = f32[256,1024]{1,0:T(8,128)S(1)} fusion(bf16[1024,512]{1,0:T(8,128)(2,1)} %bitcast.3, bf16[256,1024]{1,0:T(8,128)(2,1)S(1)} %bitcast.24, s32[]{:T(128)S(6)} %select_n.7), kind=kOutput, calls=%fused_computation.10 | convolution fusion | flops 268435456 | bytes 2359300 | tf_op jit(solution)/shard_map/dot_general | solution.py:28
  63.9 0.0 collective-permute-done.5
  63.9 2.7 %add_convert_fusion = bf16[1024,512]{1,0:T(8,128)(2,1)} fusion(bf16[1024,512]{1,0:T(8,128)(2,1)} %collective-permute-done.5, bf16[256,1024]{1,0:T(8,128)(2,1)S(1)} %get-tuple-element.10.o_ref, bf16[256,1024]{1,0:T(8,128)(2,1)S(1)} %bitcast.27, s32[]{:T(128)S(6)} %select_n.7), kind=kOutput, calls=%fused_computation | convolution fusion | flops 270008320 | bytes 2883588 | tf_op jit(solution)/shard_map/dot_general | solution.py:28
  66.6 11.8 %all-to-all-start.2 = ((bf16[8,128,512]{2,1,0:T(8,128)(2,1)}), bf16[8,128,512]{2,1,0:T(8,128)(2,1)}, u32[]{:S(2)}, u32[]{:S(2)}) async-start(bf16[8,128,512]{2,1,0:T(8,128)(2,1)} %bitcast.36), calls=%async_computation.2 | async-start | bytes 2097152 | tf_op jit(solution)/shard_map/all_to_all | solution.py:203
  78.4 0.0 collective-permute-done
  78.4 1.8 %fusion.g_ref = bf16[256,1024]{1,0:T(8,128)(2,1)S(1)} fusion(f32[256,1024]{1,0:T(8,128)S(1)} %fusion.4, bf16[1024,512]{1,0:T(8,128)(2,1)} %collective-permute-done, bf16[256,1024]{1,0:T(8,128)(2,1)S(1)} %bitcast.25, s32[]{:T(128)S(6)} %select_n.8), kind=kOutput, calls=%fused_computation.4 | convolution fusion | flops 268959744 | bytes 2883588 | tf_op jit(solution)/shard_map/dot_general | solution.py:28
  80.2 0.0 copy-done.5
  80.2 12.1 %attention_backward.1 = (bf16[256,1024]{1,0:T(8,128)(2,1)}, bf16[2,256,1024]{2,1,0:T(8,128)(2,1)S(1)}, f32[2,256,1024]{2,1,0:T(8,128)}, bf16[2,256,1024]{2,1,0:T(8,128)(2,1)}) custom-call(bf16[256,1024]{1,0:T(8,128)(2,1)S(1)} %bitcast.35, bf16[256,1024]{1,0:T(8,128)(2,1)S(1)} %fusion.g_ref, bf16[256,1024]{1,0:T(8,128)(2,1)S(1)} %get-tuple-element.10.o_ref, ...), custom_call_target="tpu_custom_call" | custom-call | flops 8000000000 | bytes 16000000 | tf_op jit(solution)/shard_map/attention_backward/pallas_call | solution.py:166
  92.2 1.3 collective-permute-start.3
  93.6 1.3 collective-permute-start.4
  94.9 0.0 all-to-all-done.2
  94.9 1.4 reduce_sum.33
  96.3 26.5 %all_to_all.25 = bf16[8,16,512]{2,1,0:T(8,128)(2,1)S(1)} all-to-all(bf16[8,16,512]{2,1,0:T(8,128)(2,1)S(1)} %bitcast.38), channel_id=1, replica_groups=mesh['zh'=4,'core'=2,'x'=4,'zl'=2,'y'=8] {'y'}, dimensions={0} | all-to-all | bytes 262144 | tf_op jit(solution)/shard_map/all_to_all | solution.py:203
  122.9 0.7 broadcast_in_dim.22
  123.5 11.7 %all-to-all-start.4 = ((bf16[8,16,512]{2,1,0:T(8,128)(2,1)}), bf16[8,16,512]{2,1,0:T(8,128)(2,1)S(1)}, u32[]{:S(2)}, u32[]{:S(2)}) async-start(bf16[8,16,512]{2,1,0:T(8,128)(2,1)} %broadcast_in_dim.22), calls=%async_computation.4 | async-start | bytes 262144 | tf_op jit(solution)/shard_map/all_to_all | solution.py:195
  135.2 0.0 collective-permute-done.3
  135.2 0.0 collective-permute-done.4
  135.2 2.4 %add_convert_fusion.1 = bf16[2,256,1024]{2,1,0:T(8,128)(2,1)S(1)} fusion(bf16[2,256,1024]{2,1,0:T(8,128)(2,1)} %collective-permute-done.4, f32[2,256,1024]{2,1,0:T(8,128)} %get-tuple-element.13, bf16[2,256,1024]{2,1,0:T(8,128)(2,1)S(1)} %collective-permute-done.3), kind=kLoop, calls=%fused_computation.1 | loop fusion | flops 2621440 | bytes 5242880 | tf_op jit(solution)/shard_map/convert.4
  137.6 1.0 fusion.10
  138.7 5.2 %all-to-all-done.4 = bf16[8,16,512]{2,1,0:T(8,128)(2,1)S(1)} async-done(((bf16[8,16,512]{2,1,0:T(8,128)(2,1)}), bf16[8,16,512]{2,1,0:T(8,128)(2,1)S(1)}, u32[]{:S(2)}, u32[]{:S(2)}) %all-to-all-start.4) | async-done | bytes 131104 | tf_op jit(solution)/shard_map/all_to_all | solution.py:195
  144.0 0.6 maximum_multiply_fusion
  (11 shorter events, 0.1 us)
Async XLA Ops:
  0.6 52.0 %copy-start = (bf16[1,2,128,1024]{3,2,1,0:T(8,128)(2,1)S(1)}, bf16[1,2,128,1024]{3,2,1,0:T(8,128)(2,1)}, u32[]{:S(2)}) copy-start(bf16[1,2,128,1024]{3,2,1,0:T(8,128)(2,1)} %param.12) | copy-start | bytes 1572868
  2.1 16.4 %all-to-all-start = ((bf16[8,16,512]{2,1,0:T(8,128)(2,1)}), bf16[8,16,512]{2,1,0:T(8,128)(2,1)S(1)}, u32[]{:S(2)}, u32[]{:S(2)}) async-start(bf16[8,16,512]{2,1,0:T(8,128)(2,1)} %broadcast_in_dim.8), calls=%async_computation | async-start | bytes 262144 | tf_op jit(solution)/shard_map/all_to_all | solution.py:195
  12.0 25.3 %copy-start.1 = (bf16[1,2,128,1024]{3,2,1,0:T(8,128)(2,1)S(1)}, bf16[1,2,128,1024]{3,2,1,0:T(8,128)(2,1)}, u32[]{:S(2)}) copy-start(bf16[1,2,128,1024]{3,2,1,0:T(8,128)(2,1)} %param.11) | copy-start | bytes 1572868
  12.0 25.3 %copy-start.2 = (bf16[1,2,128,1024]{3,2,1,0:T(8,128)(2,1)S(1)}, bf16[1,2,128,1024]{3,2,1,0:T(8,128)(2,1)}, u32[]{:S(2)}) copy-start(bf16[1,2,128,1024]{3,2,1,0:T(8,128)(2,1)} %param.10) | copy-start | bytes 1572868
  12.0 25.3 %copy-start.6 = (s32[128]{0:T(128)S(1)}, s32[128]{0:T(128)}, u32[]{:S(2)}) copy-start(s32[128]{0:T(128)} %lo_ref.1) | copy-start | bytes 1540
  12.0 25.3 %copy-start.7 = (s32[128]{0:T(128)S(1)}, s32[128]{0:T(128)}, u32[]{:S(2)}) copy-start(s32[128]{0:T(128)} %hi_ref.1) | copy-start | bytes 1540
  12.0 25.3 %copy-start.8 = (s32[128]{0:T(128)S(1)}, s32[128]{0:T(128)}, u32[]{:S(2)}) copy-start(s32[128]{0:T(128)} %half_ref.1) | copy-start | bytes 1540
  12.1 25.3 %copy-start.9 = (f32[128]{0:T(128)S(1)}, f32[128]{0:T(128)}, u32[]{:S(2)}) copy-start(f32[128]{0:T(128)} %constant.41.clone.logw_ref) | copy-start | bytes 1540
  12.1 25.1 %collective-permute-start.2 = (bf16[2,256,1024]{2,1,0:T(8,128)(2,1)}, bf16[2,256,1024]{2,1,0:T(8,128)(2,1)S(1)}, u32[]{:S(2)}, u32[]{:S(2)}) collective-permute-start(bf16[2,256,1024]{2,1,0:T(8,128)(2,1)} %pad_maximum_fusion), channel_id=1, source_target_pairs={{1,0},{2,1},{3,2},{4,3},{5,4},{6,5},{7,6},{8,7},{9,8},{10,9},{11,1... | collective-permute-start | bytes 3145736 | tf_op jit(solution)/shard_map/ppermute | solution.py:186
  13.5 23.9 %collective-permute-start.1 = (bf16[2,256,1024]{2,1,0:T(8,128)(2,1)}, bf16[2,256,1024]{2,1,0:T(8,128)(2,1)}, u32[]{:S(2)}, u32[]{:S(2)}) collective-permute-start(bf16[2,256,1024]{2,1,0:T(8,128)(2,1)} %pad_maximum_fusion), channel_id=1, source_target_pairs={{0,1},{1,2},{2,3},{3,4},{4,5},{5,6},{6,7},{7,8},{8,9},{9,10},{10,1... | collective-permute-start | bytes 3145736 | tf_op jit(solution)/shard_map/ppermute | solution.py:186
  19.6 40.1 %all-to-all-start.1 = ((bf16[8,128,512]{2,1,0:T(8,128)(2,1)}), bf16[8,128,512]{2,1,0:T(8,128)(2,1)}, u32[]{:S(2)}, u32[]{:S(2)}) async-start(bf16[8,128,512]{2,1,0:T(8,128)(2,1)} %broadcast_in_dim.10), calls=%async_computation.1 | async-start | bytes 2097152 | tf_op jit(solution)/shard_map/all_to_all | solution.py:195
  37.1 15.5 %copy-start.3 = (bf16[2,256,1024]{2,1,0:T(8,128)(2,1)}, bf16[2,256,1024]{2,1,0:T(8,128)(2,1)S(1)}, u32[]{:S(2)}) copy-start(bf16[2,256,1024]{2,1,0:T(8,128)(2,1)S(1)} %collective-permute-done.2.kn_ref.vn_ref) | copy-start | bytes 3145732
  37.4 1.2 copy-start.4
  54.1 9.9 %collective-permute-start.5 = (bf16[1024,512]{1,0:T(8,128)(2,1)}, bf16[1024,512]{1,0:T(8,128)(2,1)}, u32[]{:S(2)}, u32[]{:S(2)}) collective-permute-start(bf16[1024,512]{1,0:T(8,128)(2,1)} %convolution_convert_fusion), channel_id=1, source_target_pairs={{0,64},{64,0},{1,65},{65,1},{2,66},{66,2},{3,67},{67,3},{4,68},{68... | collective-permute-start | bytes 3145736 | tf_op jit(solution)/shard_map/ppermute | solution.py:190
  59.7 18.7 %collective-permute-start = (bf16[1024,512]{1,0:T(8,128)(2,1)}, bf16[1024,512]{1,0:T(8,128)(2,1)}, u32[]{:S(2)}, u32[]{:S(2)}) collective-permute-start(bf16[1024,512]{1,0:T(8,128)(2,1)} %bitcast.3), channel_id=1, source_target_pairs={{0,64},{64,0},{1,65},{65,1},{2,66},{66,2},{3,67},{67,3},{4,68},{68... | collective-permute-start | bytes 3145736 | tf_op jit(solution)/shard_map/ppermute | solution.py:190
  66.6 28.3 %all-to-all-start.2 = ((bf16[8,128,512]{2,1,0:T(8,128)(2,1)}), bf16[8,128,512]{2,1,0:T(8,128)(2,1)}, u32[]{:S(2)}, u32[]{:S(2)}) async-start(bf16[8,128,512]{2,1,0:T(8,128)(2,1)} %bitcast.36), calls=%async_computation.2 | async-start | bytes 2097152 | tf_op jit(solution)/shard_map/all_to_all | solution.py:203
  78.4 1.8 %copy-start.5 = (bf16[1,2,128,1024]{3,2,1,0:T(8,128)(2,1)S(1)}, bf16[1,2,128,1024]{3,2,1,0:T(8,128)(2,1)}, u32[]{:S(2)}) copy-start(bf16[1,2,128,1024]{3,2,1,0:T(8,128)(2,1)} %param.9) | copy-start | bytes 1572868
  92.2 42.9 %collective-permute-start.3 = (bf16[2,256,1024]{2,1,0:T(8,128)(2,1)}, bf16[2,256,1024]{2,1,0:T(8,128)(2,1)S(1)}, u32[]{:S(2)}, u32[]{:S(2)}) collective-permute-start(bf16[2,256,1024]{2,1,0:T(8,128)(2,1)} %get-tuple-element.14), channel_id=1, source_target_pairs={{0,1},{1,2},{2,3},{3,4},{4,5},{5,6},{6,7},{7,8},{8,9},{9,10},{10,1... | collective-permute-start | bytes 3145736 | tf_op jit(solution)/shard_map/ppermute | solution.py:186
  93.6 41.6 %collective-permute-start.4 = (bf16[2,256,1024]{2,1,0:T(8,128)(2,1)S(1)}, bf16[2,256,1024]{2,1,0:T(8,128)(2,1)}, u32[]{:S(2)}, u32[]{:S(2)}) collective-permute-start(bf16[2,256,1024]{2,1,0:T(8,128)(2,1)S(1)} %get-tuple-element.15), channel_id=1, source_target_pairs={{1,0},{2,1},{3,2},{4,3},{5,4},{6,5},{7,6},{8,7},{9,8},{10,9},{11,1... | collective-permute-start | bytes 3145736 | tf_op jit(solution)/shard_map/ppermute | solution.py:186
  123.5 20.4 %all-to-all-start.4 = ((bf16[8,16,512]{2,1,0:T(8,128)(2,1)}), bf16[8,16,512]{2,1,0:T(8,128)(2,1)S(1)}, u32[]{:S(2)}, u32[]{:S(2)}) async-start(bf16[8,16,512]{2,1,0:T(8,128)(2,1)} %broadcast_in_dim.22), calls=%async_computation.4 | async-start | bytes 262144 | tf_op jit(solution)/shard_map/all_to_all | solution.py:195

commit v2 on v1

v2 whole, which is shorter than its diff:
```python
import functools
import math

import jax
import jax.numpy as jnp
import numpy as np
from jax import lax
from jax.experimental import pallas as pl
from jax.experimental.pallas import tpu as pltpu
from jax.sharding import Mesh
from jax.sharding import PartitionSpec as P

HEADS = 16
HEAD_DIM = 64
REACH = 2
PAIR = 2 * HEAD_DIM
PPS = 2
HALVES = 2
SCALE = 1.0 / math.sqrt(HEAD_DIM)
SPAN = 2 * REACH + 1
DP = ("zh", "core")
XZ = ("x", "zl")
LAT = ("x", "zl", "y")
BF = jnp.bfloat16
F32 = jnp.float32
VMEM_LIMIT = 60 * 1024 * 1024
LARGE = pl.CostEstimate(flops=2*10**10, bytes_accessed=4*10**7, transcendentals=0)
SMALL = pl.CostEstimate(flops=10**6, bytes_accessed=10**5, transcendentals=0)


def dot(a, b, dims):
    return lax.dot_general(a, b, (dims, ((), ())), preferred_element_type=F32)


def fill_bias(first, lo_ref, hi_ref, half_ref, logw_ref, bias_ref):
    cycles, _, lon = bias_ref.shape
    total = lo_ref.shape[0]
    key_lon = lax.broadcasted_iota(jnp.int32, (lon, lon), 0)
    query_lon = lax.broadcasted_iota(jnp.int32, (lon, lon), 1)
    gap = jnp.abs(key_lon - query_lon)
    dist = jnp.minimum(gap, lon - gap)
    for i in range(cycles):
        cycle = first + i
        lon_ok = dist <= half_ref[cycle]
        for c in range(SPAN):
            key_cycle = cycle - REACH + c
            ok = (key_cycle >= lo_ref[cycle]) & (key_cycle <= hi_ref[cycle])
            weight = logw_ref[jnp.clip(key_cycle, 0, total - 1)]
            value = jnp.where(ok, weight, -jnp.inf)
            bias_ref[i, c * lon : (c + 1) * lon, :] = jnp.where(lon_ok, value, -jnp.inf)


def head_masks(scale):
    lane = lax.broadcasted_iota(jnp.int32, (1, PAIR), 1)
    first = jnp.where(lane < HEAD_DIM, scale, 0.0).astype(F32)
    return first, scale - first


def both_heads(rows, scale):
    first, second = head_masks(scale)
    wide = rows.astype(F32)
    return jnp.concatenate([(wide * first).astype(BF), (wide * second).astype(BF)], axis=0)


def own_columns(both, lon):
    return jnp.concatenate([both[:HEAD_DIM, :lon], both[HEAD_DIM:, lon:]], axis=0).T


def forward_kernel(
    first_ref, lo_ref, hi_ref, half_ref, logw_ref,
    q_ref, kp_ref, ko_ref, kn_ref, vp_ref, vo_ref, vn_ref, *refs,
):
    out_ref, prob_ref, bias_ref = refs[-3:]
    cycles, _, lon = bias_ref.shape

    @pl.when(pl.program_id(0) == 0)
    def _():
        fill_bias(first_ref[0], lo_ref, hi_ref, half_ref, logw_ref, bias_ref)

    units = [(pair, i) for pair in range(PPS) for i in range(cycles)]
    keys, values_t = [], []
    for pair in range(PPS):
        c = slice(pair * PAIR, (pair + 1) * PAIR)
        keys.append(jnp.concatenate([kp_ref[0, :, c], ko_ref[:, c], kn_ref[0, :, c]], axis=0))
        values_t.append(jnp.concatenate([vp_ref[0, :, c], vo_ref[:, c], vn_ref[0, :, c]], axis=0).T)

    def scores_of(unit):
        pair, i = unit
        c = slice(pair * PAIR, (pair + 1) * PAIR)
        queries = both_heads(q_ref[i * lon : (i + 1) * lon, c], SCALE)
        bias = bias_ref.at[i]
        chunks = []
        for n in range(SPAN):
            part = dot(keys[pair][(i + n) * lon : (i + n + 1) * lon], queries, ((1,), (1,)))
            b = bias[n * lon : (n + 1) * lon, :]
            chunks.append(part + jnp.concatenate([b, b], axis=1))
        return chunks

    def finish(unit, chunks):
        pair, i = unit
        c = slice(pair * PAIR, (pair + 1) * PAIR)
        peak = chunks[0]
        for n in chunks[1:]:
            peak = jnp.maximum(peak, n)
        peak = jnp.max(peak, axis=0, keepdims=True)
        chunks = [jnp.exp(n - peak) for n in chunks]
        total = chunks[0]
        for n in chunks[1:]:
            total = total + n
        inverse = 1.0 / jnp.sum(total, axis=0, keepdims=True)
        probs = jnp.concatenate([(n * inverse).astype(BF) for n in chunks], axis=0)
        prob_ref[pair, i] = probs
        window = slice(i * lon, (i + SPAN) * lon)
        attended = dot(values_t[pair][:, window], probs, ((1,), (0,)))
        out_ref[i * lon : (i + 1) * lon, c] = own_columns(attended, lon).astype(BF)

    held = scores_of(units[0])
    for n, unit in enumerate(units):
        later = scores_of(units[n + 1]) if n + 1 < len(units) else None
        finish(unit, held)
        held = later


def backward_kernel(
    q_ref, g_ref, o_ref, prob_ref, kp_ref, ko_ref, kn_ref, vp_ref, vo_ref, vn_ref, *refs,
):
    dq_ref, own_key_ref, own_value_ref, low_ref, high_ref = refs[-5:]
    cycles = prob_ref.shape[1]
    lon = prob_ref.shape[2] // SPAN
    units = [(pair, i) for pair in range(PPS) for i in range(cycles)]
    keys_t, values = [], []
    for pair in range(PPS):
        c = slice(pair * PAIR, (pair + 1) * PAIR)
        keys_t.append(jnp.concatenate([kp_ref[0, :, c], ko_ref[:, c], kn_ref[0, :, c]], axis=0).T)
        values.append(jnp.concatenate([vp_ref[0, :, c], vo_ref[:, c], vn_ref[0, :, c]], axis=0))

    def begin(unit):
        pair, i = unit
        c = slice(pair * PAIR, (pair + 1) * PAIR)
        rows = slice(i * lon, (i + 1) * lon)
        grads = both_heads(g_ref[rows, c], 1.0)
        prob_grad = dot(values[pair][i * lon : (i + SPAN) * lon], grads, ((1,), (1,)))
        product = (g_ref[rows, c].astype(F32) * o_ref[rows, c].astype(F32)).T
        row_dot = jnp.concatenate(
            [
                jnp.sum(product[:HEAD_DIM], axis=0, keepdims=True),
                jnp.sum(product[HEAD_DIM:], axis=0, keepdims=True),
            ],
            axis=1,
        )
        return grads, prob_grad, row_dot

    def finish(unit, held):
        pair, i = unit
        grads, prob_grad, row_dot = held
        c = slice(pair * PAIR, (pair + 1) * PAIR)
        rows = slice(i * lon, (i + 1) * lon)
        window = slice(i * lon, (i + SPAN) * lon)
        probs = prob_ref[pair, i]
        value_part = dot(probs, grads, ((1,), (0,)))
        score_grad = (probs.astype(F32) * (prob_grad - row_dot)).astype(BF)
        queries = both_heads(q_ref[rows, c], SCALE)
        key_part = dot(score_grad, queries, ((1,), (0,)))
        query_part = dot(keys_t[pair][:, window], score_grad, ((1,), (0,)))
        dq_ref[rows, c] = (own_columns(query_part, lon) * SCALE).astype(BF)
        return key_part, value_part

    parts = {}
    held = begin(units[0])
    for n, unit in enumerate(units):
        later = begin(units[n + 1]) if n + 1 < len(units) else None
        parts[unit] = finish(unit, held)
        held = later
        if unit[1] == cycles - 1:
            pair = unit[0]
            c = slice(pair * PAIR, (pair + 1) * PAIR)
            for which in range(2):
                near, far = parts[pair, 0][which], parts[pair, 1][which]
                low_ref[which, :lon, c] = near[:lon].astype(BF)
                low_ref[which, lon:, c] = (near[lon : 2 * lon] + far[:lon]).astype(BF)
                own = near[2 * lon : 4 * lon] + far[lon : 3 * lon]
                (own_key_ref, own_value_ref)[which][:, c] = own.astype(BF)
                high_ref[which, :lon, c] = (near[4 * lon :] + far[3 * lon : 4 * lon]).astype(BF)
                high_ref[which, lon:, c] = far[4 * lon :].astype(BF)


def copies_kernel(half, k_ref, v_ref, out_ref, sems):
    width = out_ref.shape[2]
    copies = []
    for which, source in enumerate((k_ref, v_ref)):
        columns = source.at[:, half * width : (half + 1) * width]
        copies.append(pltpu.make_async_copy(columns, out_ref.at[which], sems.at[which]))
    for copy in copies:
        copy.start()
    for copy in copies:
        copy.wait()


def stack_half(half, k, v):
    rows, width = k.shape
    anywhere = pl.BlockSpec(memory_space=pl.ANY)
    return pl.pallas_call(
        functools.partial(copies_kernel, half),
        in_specs=[anywhere] * 2,
        out_specs=anywhere,
        out_shape=jax.ShapeDtypeStruct((2, rows, width // HALVES), BF),
        scratch_shapes=[pltpu.SemaphoreType.DMA((2,))],
        cost_estimate=SMALL,
        name="stack_half",
    )(k, v)


def half_specs(rows, steps, half):
    width = PPS * PAIR
    flat = pl.BlockSpec((rows, width), lambda p: (0, p + half * steps))
    key = pl.BlockSpec((1, rows, width), lambda p: (0, 0, p))
    value = pl.BlockSpec((1, rows, width), lambda p: (1, 0, p))
    both = pl.BlockSpec((2, rows, width), lambda p: (0, 0, p))
    return flat, key, value, both


def forward(half, band, q, k, v, below, above, lon, previous):
    rows, width = q.shape
    cycles = rows // lon
    pairs = width // PAIR // HALVES
    steps = pairs // PPS
    smem = pl.BlockSpec(memory_space=pltpu.SMEM)
    flat, key, value, _ = half_specs(rows, steps, half)
    operands = [*band, q, below, k, above, below, v, above]
    specs = [smem] * len(band) + [flat, key, flat, key, value, flat, value]
    return pl.pallas_call(
        forward_kernel,
        grid=(steps,),
        in_specs=specs + [pl.BlockSpec(memory_space=pl.ANY)] * len(previous),
        out_specs=[flat, pl.BlockSpec((PPS, cycles, SPAN * lon, 2 * lon), lambda p: (p, 0, 0, 0))],
        out_shape=[
            jax.ShapeDtypeStruct((rows, width), BF),
            jax.ShapeDtypeStruct((pairs, cycles, SPAN * lon, 2 * lon), BF),
        ],
        input_output_aliases={len(operands) + n: n for n in range(len(previous))},
        scratch_shapes=[pltpu.VMEM((cycles, SPAN * lon, lon), F32)],
        compiler_params=pltpu.CompilerParams(vmem_limit_bytes=VMEM_LIMIT),
        cost_estimate=LARGE,
        name="attention_forward",
    )(*operands, *previous)


def backward(half, q, g, o, probs, k, v, below, above, lon, previous):
    rows, width = q.shape
    cycles = rows // lon
    pairs = width // PAIR // HALVES
    steps = pairs // PPS
    flat, key, value, both = half_specs(rows, steps, half)
    prob = pl.BlockSpec((PPS, cycles, SPAN * lon, 2 * lon), lambda p: (p, 0, 0, 0))
    whole = jax.ShapeDtypeStruct((rows, width), BF)
    edge = jax.ShapeDtypeStruct((2, rows, width // HALVES), BF)
    operands = [q, g, o, probs, below, k, above, below, v, above]
    specs = [flat, flat, flat, prob, key, flat, key, value, flat, value]
    return pl.pallas_call(
        backward_kernel,
        grid=(steps,),
        in_specs=specs + [pl.BlockSpec(memory_space=pl.ANY)] * len(previous),
        out_specs=[flat, flat, flat, both, both],
        out_shape=[whole, whole, whole, edge, edge],
        input_output_aliases={len(operands) + n: n for n in range(len(previous))},
        compiler_params=pltpu.CompilerParams(vmem_limit_bytes=VMEM_LIMIT),
        cost_estimate=SMALL,
        name="attention_backward",
    )(*operands, *previous)


def total_kernel(below_ref, above_ref, own_key_ref, own_value_ref, key_ref, value_ref):
    for which, (own, out) in enumerate(((own_key_ref, key_ref), (own_value_ref, value_ref))):
        arrived = below_ref[which].astype(F32) + above_ref[which].astype(F32)
        out[...] = (own[...].astype(F32) + arrived).astype(BF)


def add_arrived(half, own_key, own_value, from_below, from_above):
    rows, width = own_key.shape
    steps = width // HALVES // (PPS * PAIR)
    flat, _, _, both = half_specs(rows, steps, half)
    whole = jax.ShapeDtypeStruct((rows, width), BF)
    return pl.pallas_call(
        total_kernel,
        grid=(steps,),
        in_specs=[both, both, flat, flat],
        out_specs=[flat, flat],
        out_shape=[whole, whole],
        input_output_aliases={2: 0, 3: 1},
        cost_estimate=SMALL,
        name="add_arrived",
    )(from_below, from_above, own_key, own_value)


def lat_shift(value, by):
    size = lax.axis_size(LAT)
    pairs = [(i, i + by) for i in range(size) if 0 <= i + by < size]
    return lax.ppermute(value, LAT, pairs)


def core_swap(value):
    return lax.ppermute(value, "core", [(0, 1), (1, 0)])


def after(value, earlier):
    return lax.optimization_barrier((value, earlier))[0]


def copies_of(value, axes):
    return jnp.broadcast_to(value[None], (lax.axis_size(axes),) + value.shape)


def spread(value, axes):
    return lax.all_to_all(copies_of(value, axes), axes, 0, 0, tiled=True)


def scatter_sum(value, axes):
    size = lax.axis_size(axes)
    blocks = value.reshape((size, value.shape[0] // size) + value.shape[1:])
    received = lax.all_to_all(blocks, axes, 0, 0, tiled=True)
    return jnp.sum(received.astype(F32), axis=0)


def local(query_feats, key_feats, value_feats, out_grad, out_proj, cycle_lo, cycle_hi, lon_half):
    cycles, lon, width = query_feats.shape[1:]
    rows = cycles * lon
    total = cycle_lo.shape[0]
    half_width = width // 2
    q = query_feats.reshape(rows, width)
    k = key_feats.reshape(rows, width)
    v = value_feats.reshape(rows, width)
    grad_flat = out_grad.reshape(rows, width)
    core = lax.axis_index("core")
    mine, others = core * half_width, (1 - core) * half_width

    parts = [stack_half(n, k, v) for n in range(HALVES)]
    proj = after(copies_of(out_proj, "y"), parts[0])
    proj = lax.all_to_all(proj, "y", 0, 0, tiled=True).reshape(-1, width)
    parts[1] = after(parts[1], proj)
    below = [lat_shift(part, 1) for part in parts]
    above = [lat_shift(part, -1) for part in parts]
    proj = copies_of(proj, XZ)
    early_q = after(q, proj)
    proj = lax.all_to_all(proj, XZ, 0, 0, tiled=True).reshape(-1, width)

    latitude = (np.arange(total, dtype=np.float32) + np.float32(0.5)) * np.float32(math.pi / total)
    logw = jnp.asarray(np.log(np.sin(latitude)).astype(np.float32))
    first = (lax.axis_index(LAT) * cycles).astype(jnp.int32).reshape(1)
    band = (first, cycle_lo, cycle_hi, lon_half, logw)
    attended, probs = [], []
    for n in range(HALVES):
        out, prob = forward(n, band, early_q, k, v, below[n], above[n], lon, attended)
        attended = [out]
        probs.append(prob)
    attended = attended[0]

    grad_mine = lax.dynamic_slice_in_dim(grad_flat, mine, half_width, axis=1)
    grad_other = lax.dynamic_slice_in_dim(grad_flat, others, half_width, axis=1)
    sent = dot(attended, grad_other, ((0,), (0,))).astype(BF)
    received = core_swap(sent)
    partial = (dot(attended, grad_mine, ((0,), (0,))) + received.astype(F32)).astype(BF)

    proj, partial = lax.optimization_barrier((proj, partial))
    attn_grad = dot(grad_flat, proj, ((1,), (1,))).astype(BF)
    whole, edges = [], []
    for n in range(HALVES):
        *whole, low, high = backward(
            n, q, attn_grad, attended, probs[n], k, v, below[n], above[n], lon, whole
        )
        edges.append((low, high))
    query_grad, key_grad, value_grad = whole

    partial = scatter_sum(partial, XZ).astype(BF)
    partial = scatter_sum(partial, "y").astype(BF)
    edges[-1] = after(edges[-1], partial)
    samples = lax.axis_size(DP)
    gathered = spread(partial, DP).reshape((samples // 2, 2) + partial.shape)
    summed = jnp.sum(gathered.astype(F32), axis=0)
    scaling = 1.0 / math.sqrt(samples * total * lon)
    proj_grad = jnp.concatenate([summed[0], summed[1]], axis=1) * scaling

    for n, (low, high) in enumerate(edges):
        key_grad, value_grad = add_arrived(
            n, key_grad, value_grad, lat_shift(high, 1), lat_shift(low, -1)
        )
    shape = query_feats.shape
    return (
        query_grad.reshape(shape),
        key_grad.reshape(shape),
        value_grad.reshape(shape),
        proj_grad,
    )


def solution(mesh):
    parts = Mesh(mesh.devices.reshape(4, 2, 4, 2, 8), DP + LAT)
    placed = P(DP, LAT, None, None)
    return jax.shard_map(
        local,
        mesh=parts,
        in_specs=(placed, placed, placed, placed, P(LAT, None), P(), P(), P()),
        out_specs=(placed, placed, placed, P(LAT, None)),
        check_vma=False,
    )
```

time: 147 us -> 180 us (1.22)
  the two profiles are of different devices: /device:TPU:1 before, /device:TPU:120 now
where the time goes in v2:
time: 180 us; the launch traced here: 179 us
  starting transfers between devices  67.1 us (37%)
  Pallas kernels  59.6 us (33%)
  waiting for transfers between devices  19.9 us (11%)
  blocking collectives  16.9 us (9%)
  local copies, waits for them, and re-layouts  7.53 us (4%)
  matrix products  6.15 us (3%)
    ppermute x8, starting transfers between devices, lat_shift(): return lax.ppermute(value, LAT, pairs)  40.4 us
    pallas_call x2, Pallas kernels, stack_half(): pl.pallas_call(functools.partial(copies_kernel, half), in_specs=[anywhere...  34 us
    all_to_all x1, blocking collectives, scatter_sum(): received = lax.all_to_all(blocks, axes, 0, 0, tiled=True)  16.9 us
    ppermute x8, waiting for transfers between devices, lat_shift(): return lax.ppermute(value, LAT, pairs)  13.2 us
    pallas_call x2, Pallas kernels, backward(): pl.pallas_call(backward_kernel, grid=(steps,), in_specs=specs + [pl.Block...  10.9 us
    pallas_call x2, Pallas kernels, forward(): pl.pallas_call(forward_kernel, grid=(steps,), in_specs=specs + [pl.BlockS...  10.5 us
    all_to_all x1, starting transfers between devices, spread(): return lax.all_to_all(copies_of(value, axes), axes, 0, 0, tiled=True)  9.4 us
    dot_general x3, matrix products, dot(): return lax.dot_general(a, b, (dims, ((), ())), preferred_element_type=F32)  6.15 us
  transfers between devices with their start and end apart: 13, of which 4 were waited for; matrix products, arithmetic and copies ran while one was open for 6% of the time, Pallas kernels for 23%

profile of v2, /device:TPU:120, one launch (start us, length us, event | category | flops | bytes accessed | tf_op | source)
XLA Modules:
  0.0 178.9 jit_solution(7109676009512933246)
XLA Ops:
  0.6 0.0 copy-start
  0.6 17.0 %stack_half.2 = bf16[2,256,512]{2,1,0:T(8,128)(2,1)} custom-call(bf16[256,1024]{1,0:T(8,128)(2,1)} %bitcast.27, bf16[256,1024]{1,0:T(8,128)(2,1)} %bitcast.33), custom_call_target="tpu_custom_call" | custom-call | flops 1000000 | bytes 100000 | tf_op jit(solution)/shard_map/stack_half/pallas_call | solution.py:202
  17.7 3.3 %collective-permute-start.3 = (bf16[2,256,512]{2,1,0:T(8,128)(2,1)}, bf16[2,256,512]{2,1,0:T(8,128)(2,1)S(1)}, u32[]{:S(2)}, u32[]{:S(2)}) collective-permute-start(bf16[2,256,512]{2,1,0:T(8,128)(2,1)} %stack_half.2), channel_id=1, source_target_pairs={{1,0},{2,1},{3,2},{4,3},{5,4},{6,5},{7,6},{8,7},{9,8},{10,9},{11,1... | collective-permute-start | bytes 1572872 | tf_op jit(solution)/shard_map/ppermute | solution.py:298
  20.9 5.6 %collective-permute-start.2 = (bf16[2,256,512]{2,1,0:T(8,128)(2,1)}, bf16[2,256,512]{2,1,0:T(8,128)(2,1)S(1)}, u32[]{:S(2)}, u32[]{:S(2)}) collective-permute-start(bf16[2,256,512]{2,1,0:T(8,128)(2,1)} %stack_half.2), channel_id=1, source_target_pairs={{0,1},{1,2},{2,3},{3,4},{4,5},{5,6},{6,7},{7,8},{8,9},{9,10},{10,1... | collective-permute-start | bytes 1572872 | tf_op jit(solution)/shard_map/ppermute | solution.py:298
  26.5 1.5 broadcast_in_dim.8
  28.0 4.5 %all-to-all-start = ((bf16[8,16,1024]{2,1,0:T(8,128)(2,1)}), bf16[8,16,1024]{2,1,0:T(8,128)(2,1)S(1)}, u32[]{:S(2)}, u32[]{:S(2)}) async-start(bf16[8,16,1024]{2,1,0:T(8,128)(2,1)} %broadcast_in_dim.8), calls=%async_computation | async-start | bytes 524288 | tf_op jit(solution)/shard_map/all_to_all | solution.py:338
  32.5 17.0 %stack_half.3 = bf16[2,256,512]{2,1,0:T(8,128)(2,1)} custom-call(bf16[256,1024]{1,0:T(8,128)(2,1)} %bitcast.28, bf16[256,1024]{1,0:T(8,128)(2,1)} %bitcast.34), custom_call_target="tpu_custom_call" | custom-call | flops 1000000 | bytes 100000 | tf_op jit(solution)/shard_map/stack_half/pallas_call | solution.py:202
  49.5 3.4 %collective-permute-start.1 = (bf16[2,256,512]{2,1,0:T(8,128)(2,1)}, bf16[2,256,512]{2,1,0:T(8,128)(2,1)S(1)}, u32[]{:S(2)}, u32[]{:S(2)}) collective-permute-start(bf16[2,256,512]{2,1,0:T(8,128)(2,1)} %stack_half.3), channel_id=1, source_target_pairs={{1,0},{2,1},{3,2},{4,3},{5,4},{6,5},{7,6},{8,7},{9,8},{10,9},{11,1... | collective-permute-start | bytes 1572872 | tf_op jit(solution)/shard_map/ppermute | solution.py:298
  52.9 5.5 %collective-permute-start = (bf16[2,256,512]{2,1,0:T(8,128)(2,1)}, bf16[2,256,512]{2,1,0:T(8,128)(2,1)S(1)}, u32[]{:S(2)}, u32[]{:S(2)}) collective-permute-start(bf16[2,256,512]{2,1,0:T(8,128)(2,1)} %stack_half.3), channel_id=1, source_target_pairs={{0,1},{1,2},{2,3},{3,4},{4,5},{5,6},{6,7},{7,8},{8,9},{9,10},{10,1... | collective-permute-start | bytes 1572872 | tf_op jit(solution)/shard_map/ppermute | solution.py:298
  58.4 0.0 all-to-all-done
  58.4 1.7 broadcast_in_dim.10
  60.1 5.8 %all-to-all-start.1 = ((bf16[8,128,1024]{2,1,0:T(8,128)(2,1)}), bf16[8,128,1024]{2,1,0:T(8,128)(2,1)}, u32[]{:S(2)}, u32[]{:S(2)}) async-start(bf16[8,128,1024]{2,1,0:T(8,128)(2,1)} %broadcast_in_dim.10), calls=%async_computation.1 | async-start | bytes 4194304 | tf_op jit(solution)/shard_map/all_to_all | solution.py:344
  65.9 0.0 collective-permute-done.3.kn_ref.vn_ref
  65.9 0.0 collective-permute-done.2.kp_ref.vp_ref
  65.9 0.8 copy-done.2
  66.7 0.2 copy-done.3
  66.9 5.2 %attention_forward.2 = (bf16[256,1024]{1,0:T(8,128)(2,1)}, bf16[4,2,640,256]{3,2,1,0:T(8,128)(2,1)}) custom-call(s32[1]{0:T(128)} %bitcast.5.first_ref, s32[128]{0:T(128)} %lo_ref.3, s32[128]{0:T(128)} %hi_ref.3, s32[128]{0:T(128)} %half_ref.3, f32[128]{0:T(128)} %constant.41.clone.logw_ref, bf16[256,1024]{1,0:T(8,128)(2,1)} %bitcast.41, ...), custom_call_target="tpu_custom_call" | custom-call | flops 20000000000 | bytes 40000000 | tf_op jit(solution)/shard_map/attention_forward/pallas_call | solution.py:231
  72.1 0.0 collective-permute-done.1.kn_ref.vn_ref
  72.1 0.8 copy-done.4
  72.9 0.2 copy-done.5
  73.1 5.3 %attention_forward.3 = (bf16[256,1024]{1,0:T(8,128)(2,1)}, bf16[4,2,640,256]{3,2,1,0:T(8,128)(2,1)}) custom-call(s32[1]{0:T(128)} %bitcast.5.first_ref, s32[128]{0:T(128)} %lo_ref.3, s32[128]{0:T(128)} %hi_ref.3, s32[128]{0:T(128)} %half_ref.3, f32[128]{0:T(128)} %constant.41.clone.logw_ref, ...), custom_call_target="tpu_custom_call", output_to_operand_aliasing={{0}: (12, {})} | custom-call | flops 20000000000 | bytes 40000000 | tf_op jit(solution)/shard_map/attention_forward/pallas_call | solution.py:231
  78.4 1.6 convolution_convert_fusion
  80.0 1.9 %collective-permute-start.4 = (bf16[1024,512]{1,0:T(8,128)(2,1)S(1)}, bf16[1024,512]{1,0:T(8,128)(2,1)S(1)}, u32[]{:S(2)}, u32[]{:S(2)}) collective-permute-start(bf16[1024,512]{1,0:T(8,128)(2,1)S(1)} %convolution_convert_fusion), channel_id=1, source_target_pairs={{0,64},{64,0},{1,65},{65,1},{2,66},{66,2},{3,67},{67,3},{4,68},{68... | collective-permute-start | bytes 3145736 | tf_op jit(solution)/shard_map/ppermute | solution.py:302
  81.9 2.6 %collective-permute-done.4 = bf16[1024,512]{1,0:T(8,128)(2,1)S(1)} collective-permute-done((bf16[1024,512]{1,0:T(8,128)(2,1)S(1)}, bf16[1024,512]{1,0:T(8,128)(2,1)S(1)}, u32[]{:S(2)}, u32[]{:S(2)}) %collective-permute-start.4) | collective-permute-done | bytes 1048608 | tf_op jit(solution)/shard_map/ppermute | solution.py:302
  84.5 1.5 add_convert_fusion
  86.0 4.1 %all-to-all-done.1 = bf16[8,128,1024]{2,1,0:T(8,128)(2,1)} async-done(((bf16[8,128,1024]{2,1,0:T(8,128)(2,1)}), bf16[8,128,1024]{2,1,0:T(8,128)(2,1)}, u32[]{:S(2)}, u32[]{:S(2)}) %all-to-all-start.1) | async-done | bytes 2097184 | tf_op jit(solution)/shard_map/all_to_all | solution.py:344
  90.1 5.1 %all-to-all-start.2 = ((bf16[8,128,512]{2,1,0:T(8,128)(2,1)}), bf16[8,128,512]{2,1,0:T(8,128)(2,1)S(1)}, u32[]{:S(2)}, u32[]{:S(2)}) async-start(bf16[8,128,512]{2,1,0:T(8,128)(2,1)} %bitcast.9), calls=%async_computation.2 | async-start | bytes 2097152 | tf_op jit(solution)/shard_map/all_to_all | solution.py:320
  95.2 3.1 %fusion.g_ref = bf16[256,1024]{1,0:T(8,128)(2,1)} fusion(bf16[1024,1024]{1,0:T(8,128)(2,1)} %bitcast.4, bf16[256,1024]{1,0:T(8,128)(2,1)S(1)} %bitcast.26), kind=kOutput, calls=%fused_computation.3 | convolution fusion | flops 537133056 | bytes 3145728 | tf_op jit(solution)/shard_map/dot_general | solution.py:32
  98.3 5.4 %attention_backward.2 = (bf16[256,1024]{1,0:T(8,128)(2,1)}, bf16[256,1024]{1,0:T(8,128)(2,1)}, bf16[256,1024]{1,0:T(8,128)(2,1)}, bf16[2,256,512]{2,1,0:T(8,128)(2,1)}, bf16[2,256,512]{2,1,0:T(8,128)(2,1)}) custom-call(bf16[256,1024]{1,0:T(8,128)(2,1)} %bitcast.43, bf16[256,1024]{1,0:T(8,128)(2,1)} %fusion.g_ref, bf16[256,1024]{1,0:T(8,128)(2,1)} %get-tuple-element.31.o_ref, ...), custom_call_target="tpu_custom_call" | custom-call | flops 1000000 | bytes 100000 | tf_op jit(solution)/shard_map/attention_backward/pallas_call | solution.py:259
  103.7 14.9 %collective-permute-start.7 = (bf16[2,256,512]{2,1,0:T(8,128)(2,1)}, bf16[2,256,512]{2,1,0:T(8,128)(2,1)S(1)}, u32[]{:S(2)}, u32[]{:S(2)}) collective-permute-start(bf16[2,256,512]{2,1,0:T(8,128)(2,1)} %get-tuple-element.44), channel_id=1, source_target_pairs={{0,1},{1,2},{2,3},{3,4},{4,5},{5,6},{6,7},{7,8},{8,9},{9,10},{10,1... | collective-permute-start | bytes 1572872 | tf_op jit(solution)/shard_map/ppermute | solution.py:298
  118.6 1.9 %collective-permute-start.8 = (bf16[2,256,512]{2,1,0:T(8,128)(2,1)}, bf16[2,256,512]{2,1,0:T(8,128)(2,1)S(1)}, u32[]{:S(2)}, u32[]{:S(2)}) collective-permute-start(bf16[2,256,512]{2,1,0:T(8,128)(2,1)} %get-tuple-element.45), channel_id=1, source_target_pairs={{1,0},{2,1},{3,2},{4,3},{5,4},{6,5},{7,6},{8,7},{9,8},{10,9},{11,1... | collective-permute-start | bytes 1572872 | tf_op jit(solution)/shard_map/ppermute | solution.py:298
  120.6 0.0 all-to-all-done.2
  120.6 0.1 reduce_sum.33
  120.7 16.9 %all_to_all.25 = bf16[8,16,512]{2,1,0:T(8,128)(2,1)S(1)} all-to-all(bf16[8,16,512]{2,1,0:T(8,128)(2,1)S(1)} %bitcast.47), channel_id=1, replica_groups=mesh['zh'=4,'core'=2,'x'=4,'zl'=2,'y'=8] {'y'}, dimensions={0} | all-to-all | bytes 262144 | tf_op jit(solution)/shard_map/all_to_all | solution.py:320
  137.7 0.7 broadcast_in_dim.22
  138.3 9.4 %all-to-all-start.4 = ((bf16[8,16,512]{2,1,0:T(8,128)(2,1)}), bf16[8,16,512]{2,1,0:T(8,128)(2,1)S(1)}, u32[]{:S(2)}, u32[]{:S(2)}) async-start(bf16[8,16,512]{2,1,0:T(8,128)(2,1)} %broadcast_in_dim.22), calls=%async_computation.4 | async-start | bytes 262144 | tf_op jit(solution)/shard_map/all_to_all | solution.py:314
  147.7 5.5 %attention_backward.3 = (bf16[256,1024]{1,0:T(8,128)(2,1)}, bf16[256,1024]{1,0:T(8,128)(2,1)}, bf16[256,1024]{1,0:T(8,128)(2,1)}, bf16[2,256,512]{2,1,0:T(8,128)(2,1)}, bf16[2,256,512]{2,1,0:T(8,128)(2,1)}) custom-call(bf16[256,1024]{1,0:T(8,128)(2,1)} %bitcast.44, ...), custom_call_target="tpu_custom_call", output_to_operand_aliasing={{0}: (10, {}), {1}: (11, {}), {2}: (12, {})} | custom-call | flops 1000000 | bytes 100000 | tf_op jit(solution)/shard_map/attention_backward/pallas_call | solution.py:259
  153.2 3.6 %collective-permute-start.5 = (bf16[2,256,512]{2,1,0:T(8,128)(2,1)}, bf16[2,256,512]{2,1,0:T(8,128)(2,1)S(1)}, u32[]{:S(2)}, u32[]{:S(2)}) collective-permute-start(bf16[2,256,512]{2,1,0:T(8,128)(2,1)} %get-tuple-element.42), channel_id=1, source_target_pairs={{0,1},{1,2},{2,3},{3,4},{4,5},{5,6},{6,7},{7,8},{8,9},{9,10},{10,1... | collective-permute-start | bytes 1572872 | tf_op jit(solution)/shard_map/ppermute | solution.py:298
  156.8 2.2 %collective-permute-start.6 = (bf16[2,256,512]{2,1,0:T(8,128)(2,1)}, bf16[2,256,512]{2,1,0:T(8,128)(2,1)S(1)}, u32[]{:S(2)}, u32[]{:S(2)}) collective-permute-start(bf16[2,256,512]{2,1,0:T(8,128)(2,1)} %get-tuple-element.43), channel_id=1, source_target_pairs={{1,0},{2,1},{3,2},{4,3},{5,4},{6,5},{7,6},{8,7},{9,8},{10,9},{11,1... | collective-permute-start | bytes 1572872 | tf_op jit(solution)/shard_map/ppermute | solution.py:298
  159.0 0.0 collective-permute-done.7.below_ref
  159.1 0.8 copy-done.6
  159.9 0.2 copy-done.7
  160.0 2.1 %add_arrived.2 = (bf16[256,1024]{1,0:T(8,128)(2,1)}, bf16[256,1024]{1,0:T(8,128)(2,1)}) custom-call(bf16[2,256,512]{2,1,0:T(8,128)(2,1)} %copy-done.6, bf16[2,256,512]{2,1,0:T(8,128)(2,1)} %copy-done.7, bf16[256,1024]{1,0:T(8,128)(2,1)} %get-tuple-element.46.own_key_ref, ...), custom_call_target="tpu_custom_call", output_to_operand_aliasing={{0}: (2, {}), {1}: (3, {})} | custom-call | flops 1000000 | bytes 100000 | tf_op jit(solution)/shard_map/add_arrived/pallas_call | solution.py:283
  162.2 0.6 maximum_multiply_fusion
  162.8 6.8 %collective-permute-done.5.below_ref = bf16[2,256,512]{2,1,0:T(8,128)(2,1)S(1)} collective-permute-done((bf16[2,256,512]{2,1,0:T(8,128)(2,1)}, bf16[2,256,512]{2,1,0:T(8,128)(2,1)S(1)}, u32[]{:S(2)}, u32[]{:S(2)}) %collective-permute-start.5) | collective-permute-done | bytes 524320 | tf_op jit(solution)/shard_map/ppermute | solution.py:298
  169.6 6.3 %collective-permute-done.6.above_ref = bf16[2,256,512]{2,1,0:T(8,128)(2,1)S(1)} collective-permute-done((bf16[2,256,512]{2,1,0:T(8,128)(2,1)}, bf16[2,256,512]{2,1,0:T(8,128)(2,1)S(1)}, u32[]{:S(2)}, u32[]{:S(2)}) %collective-permute-start.6) | collective-permute-done | bytes 524320 | tf_op jit(solution)/shard_map/ppermute | solution.py:298
  176.0 0.8 copy-done.9
  176.8 2.1 %add_arrived.3 = (bf16[256,1024]{1,0:T(8,128)(2,1)}, bf16[256,1024]{1,0:T(8,128)(2,1)}) custom-call(bf16[2,256,512]{2,1,0:T(8,128)(2,1)} %copy-done.8, bf16[2,256,512]{2,1,0:T(8,128)(2,1)} %copy-done.9, bf16[256,1024]{1,0:T(8,128)(2,1)} %get-tuple-element.48.own_key_ref, ...), custom_call_target="tpu_custom_call", output_to_operand_aliasing={{0}: (2, {}), {1}: (3, {})} | custom-call | flops 1000000 | bytes 100000 | tf_op jit(solution)/shard_map/add_arrived/pallas_call | solution.py:283
  (18 shorter events, 0.1 us)
Async XLA Ops:
  0.6 77.7 %copy-start = (bf16[1,2,128,1024]{3,2,1,0:T(8,128)(2,1)S(1)}, bf16[1,2,128,1024]{3,2,1,0:T(8,128)(2,1)}, u32[]{:S(2)}) copy-start(bf16[1,2,128,1024]{3,2,1,0:T(8,128)(2,1)} %param.12) | copy-start | bytes 1572868
  17.7 48.2 %collective-permute-start.3 = (bf16[2,256,512]{2,1,0:T(8,128)(2,1)}, bf16[2,256,512]{2,1,0:T(8,128)(2,1)S(1)}, u32[]{:S(2)}, u32[]{:S(2)}) collective-permute-start(bf16[2,256,512]{2,1,0:T(8,128)(2,1)} %stack_half.2), channel_id=1, source_target_pairs={{1,0},{2,1},{3,2},{4,3},{5,4},{6,5},{7,6},{8,7},{9,8},{10,9},{11,1... | collective-permute-start | bytes 1572872 | tf_op jit(solution)/shard_map/ppermute | solution.py:298
  20.9 45.0 %collective-permute-start.2 = (bf16[2,256,512]{2,1,0:T(8,128)(2,1)}, bf16[2,256,512]{2,1,0:T(8,128)(2,1)S(1)}, u32[]{:S(2)}, u32[]{:S(2)}) collective-permute-start(bf16[2,256,512]{2,1,0:T(8,128)(2,1)} %stack_half.2), channel_id=1, source_target_pairs={{0,1},{1,2},{2,3},{3,4},{4,5},{5,6},{6,7},{7,8},{8,9},{9,10},{10,1... | collective-permute-start | bytes 1572872 | tf_op jit(solution)/shard_map/ppermute | solution.py:298
  28.0 30.4 %all-to-all-start = ((bf16[8,16,1024]{2,1,0:T(8,128)(2,1)}), bf16[8,16,1024]{2,1,0:T(8,128)(2,1)S(1)}, u32[]{:S(2)}, u32[]{:S(2)}) async-start(bf16[8,16,1024]{2,1,0:T(8,128)(2,1)} %broadcast_in_dim.8), calls=%async_computation | async-start | bytes 524288 | tf_op jit(solution)/shard_map/all_to_all | solution.py:338
  49.5 22.6 %collective-permute-start.1 = (bf16[2,256,512]{2,1,0:T(8,128)(2,1)}, bf16[2,256,512]{2,1,0:T(8,128)(2,1)S(1)}, u32[]{:S(2)}, u32[]{:S(2)}) collective-permute-start(bf16[2,256,512]{2,1,0:T(8,128)(2,1)} %stack_half.3), channel_id=1, source_target_pairs={{1,0},{2,1},{3,2},{4,3},{5,4},{6,5},{7,6},{8,7},{9,8},{10,9},{11,1... | collective-permute-start | bytes 1572872 | tf_op jit(solution)/shard_map/ppermute | solution.py:298
  52.9 19.2 %collective-permute-start = (bf16[2,256,512]{2,1,0:T(8,128)(2,1)}, bf16[2,256,512]{2,1,0:T(8,128)(2,1)S(1)}, u32[]{:S(2)}, u32[]{:S(2)}) collective-permute-start(bf16[2,256,512]{2,1,0:T(8,128)(2,1)} %stack_half.3), channel_id=1, source_target_pairs={{0,1},{1,2},{2,3},{3,4},{4,5},{5,6},{6,7},{7,8},{8,9},{9,10},{10,1... | collective-permute-start | bytes 1572872 | tf_op jit(solution)/shard_map/ppermute | solution.py:298
  60.1 30.0 %all-to-all-start.1 = ((bf16[8,128,1024]{2,1,0:T(8,128)(2,1)}), bf16[8,128,1024]{2,1,0:T(8,128)(2,1)}, u32[]{:S(2)}, u32[]{:S(2)}) async-start(bf16[8,128,1024]{2,1,0:T(8,128)(2,1)} %broadcast_in_dim.10), calls=%async_computation.1 | async-start | bytes 4194304 | tf_op jit(solution)/shard_map/all_to_all | solution.py:344
  65.9 0.8 copy-start.2
  65.9 1.0 copy-start.3
  72.1 0.8 copy-start.4
  72.1 1.0 copy-start.5
  78.4 6.1 %copy-start.1 = (bf16[256,1024]{1,0:T(8,128)(2,1)S(1)}, bf16[256,1024]{1,0:T(8,128)(2,1)}, u32[]{:S(2)}) copy-start(bf16[256,1024]{1,0:T(8,128)(2,1)} %get-tuple-element.31.o_ref) | copy-start | bytes 1572868
  80.0 4.6 %collective-permute-start.4 = (bf16[1024,512]{1,0:T(8,128)(2,1)S(1)}, bf16[1024,512]{1,0:T(8,128)(2,1)S(1)}, u32[]{:S(2)}, u32[]{:S(2)}) collective-permute-start(bf16[1024,512]{1,0:T(8,128)(2,1)S(1)} %convolution_convert_fusion), channel_id=1, source_target_pairs={{0,64},{64,0},{1,65},{65,1},{2,66},{66,2},{3,67},{67,3},{4,68},{68... | collective-permute-start | bytes 3145736 | tf_op jit(solution)/shard_map/ppermute | solution.py:302
  90.1 30.5 %all-to-all-start.2 = ((bf16[8,128,512]{2,1,0:T(8,128)(2,1)}), bf16[8,128,512]{2,1,0:T(8,128)(2,1)S(1)}, u32[]{:S(2)}, u32[]{:S(2)}) async-start(bf16[8,128,512]{2,1,0:T(8,128)(2,1)} %bitcast.9), calls=%async_computation.2 | async-start | bytes 2097152 | tf_op jit(solution)/shard_map/all_to_all | solution.py:320
  103.7 55.3 %collective-permute-start.7 = (bf16[2,256,512]{2,1,0:T(8,128)(2,1)}, bf16[2,256,512]{2,1,0:T(8,128)(2,1)S(1)}, u32[]{:S(2)}, u32[]{:S(2)}) collective-permute-start(bf16[2,256,512]{2,1,0:T(8,128)(2,1)} %get-tuple-element.44), channel_id=1, source_target_pairs={{0,1},{1,2},{2,3},{3,4},{4,5},{5,6},{6,7},{7,8},{8,9},{9,10},{10,1... | collective-permute-start | bytes 1572872 | tf_op jit(solution)/shard_map/ppermute | solution.py:298
  118.6 40.4 %collective-permute-start.8 = (bf16[2,256,512]{2,1,0:T(8,128)(2,1)}, bf16[2,256,512]{2,1,0:T(8,128)(2,1)S(1)}, u32[]{:S(2)}, u32[]{:S(2)}) collective-permute-start(bf16[2,256,512]{2,1,0:T(8,128)(2,1)} %get-tuple-element.45), channel_id=1, source_target_pairs={{1,0},{2,1},{3,2},{4,3},{5,4},{6,5},{7,6},{8,7},{9,8},{10,9},{11,1... | collective-permute-start | bytes 1572872 | tf_op jit(solution)/shard_map/ppermute | solution.py:298
  138.3 23.8 %all-to-all-start.4 = ((bf16[8,16,512]{2,1,0:T(8,128)(2,1)}), bf16[8,16,512]{2,1,0:T(8,128)(2,1)S(1)}, u32[]{:S(2)}, u32[]{:S(2)}) async-start(bf16[8,16,512]{2,1,0:T(8,128)(2,1)} %broadcast_in_dim.22), calls=%async_computation.4 | async-start | bytes 262144 | tf_op jit(solution)/shard_map/all_to_all | solution.py:314
  153.2 16.4 %collective-permute-start.5 = (bf16[2,256,512]{2,1,0:T(8,128)(2,1)}, bf16[2,256,512]{2,1,0:T(8,128)(2,1)S(1)}, u32[]{:S(2)}, u32[]{:S(2)}) collective-permute-start(bf16[2,256,512]{2,1,0:T(8,128)(2,1)} %get-tuple-element.42), channel_id=1, source_target_pairs={{0,1},{1,2},{2,3},{3,4},{4,5},{5,6},{6,7},{7,8},{8,9},{9,10},{10,1... | collective-permute-start | bytes 1572872 | tf_op jit(solution)/shard_map/ppermute | solution.py:298
  156.8 19.2 %collective-permute-start.6 = (bf16[2,256,512]{2,1,0:T(8,128)(2,1)}, bf16[2,256,512]{2,1,0:T(8,128)(2,1)S(1)}, u32[]{:S(2)}, u32[]{:S(2)}) collective-permute-start(bf16[2,256,512]{2,1,0:T(8,128)(2,1)} %get-tuple-element.43), channel_id=1, source_target_pairs={{1,0},{2,1},{3,2},{4,3},{5,4},{6,5},{7,6},{8,7},{9,8},{10,9},{11,1... | collective-permute-start | bytes 1572872 | tf_op jit(solution)/shard_map/ppermute | solution.py:298
  159.1 0.8 copy-start.6
  159.1 0.9 copy-start.7
  169.6 6.4 %copy-start.8 = (bf16[2,256,512]{2,1,0:T(8,128)(2,1)}, bf16[2,256,512]{2,1,0:T(8,128)(2,1)S(1)}, u32[]{:S(2)}) copy-start(bf16[2,256,512]{2,1,0:T(8,128)(2,1)S(1)} %collective-permute-done.5.below_ref) | copy-start | bytes 1572868
  176.0 0.8 copy-start.9

commit v3 on v2

--- a/solution.py
+++ b/solution.py
@@ -1,4 +1,3 @@
-import functools
 import math
 
 import jax
@@ -19,7 +18,7 @@
 SCALE = 1.0 / math.sqrt(HEAD_DIM)
 SPAN = 2 * REACH + 1
 DP = ("zh", "core")
-XZ = ("x", "zl")
+ZY = ("zl", "y")
 LAT = ("x", "zl", "y")
 BF = jnp.bfloat16
 F32 = jnp.float32
@@ -182,32 +181,6 @@
                 (own_key_ref, own_value_ref)[which][:, c] = own.astype(BF)
                 high_ref[which, :lon, c] = (near[4 * lon :] + far[3 * lon : 4 * lon]).astype(BF)
                 high_ref[which, lon:, c] = far[4 * lon :].astype(BF)
-
-
-def copies_kernel(half, k_ref, v_ref, out_ref, sems):
-    width = out_ref.shape[2]
-    copies = []
-    for which, source in enumerate((k_ref, v_ref)):
-        columns = source.at[:, half * width : (half + 1) * width]
-        copies.append(pltpu.make_async_copy(columns, out_ref.at[which], sems.at[which]))
-    for copy in copies:
-        copy.start()
-    for copy in copies:
-        copy.wait()
-
-
-def stack_half(half, k, v):
-    rows, width = k.shape
-    anywhere = pl.BlockSpec(memory_space=pl.ANY)
-    return pl.pallas_call(
-        functools.partial(copies_kernel, half),
-        in_specs=[anywhere] * 2,
-        out_specs=anywhere,
-        out_shape=jax.ShapeDtypeStruct((2, rows, width // HALVES), BF),
-        scratch_shapes=[pltpu.SemaphoreType.DMA((2,))],
-        cost_estimate=SMALL,
-        name="stack_half",
-    )(k, v)
 
 
 def half_specs(rows, steps, half):
@@ -302,10 +275,6 @@
     return lax.ppermute(value, "core", [(0, 1), (1, 0)])
 
 
-def after(value, earlier):
-    return lax.optimization_barrier((value, earlier))[0]
-
-
 def copies_of(value, axes):
     return jnp.broadcast_to(value[None], (lax.axis_size(axes),) + value.shape)
 
@@ -333,15 +302,16 @@
     core = lax.axis_index("core")
     mine, others = core * half_width, (1 - core) * half_width
 
-    parts = [stack_half(n, k, v) for n in range(HALVES)]
-    proj = after(copies_of(out_proj, "y"), parts[0])
-    proj = lax.all_to_all(proj, "y", 0, 0, tiled=True).reshape(-1, width)
-    parts[1] = after(parts[1], proj)
+    parts = [
+        jnp.stack([k[:, n : n + width // HALVES], v[:, n : n + width // HALVES]])
+        for n in range(0, width, width // HALVES)
+    ]
     below = [lat_shift(part, 1) for part in parts]
     above = [lat_shift(part, -1) for part in parts]
-    proj = copies_of(proj, XZ)
-    early_q = after(q, proj)
-    proj = lax.all_to_all(proj, XZ, 0, 0, tiled=True).reshape(-1, width)
+    proj = spread(out_proj, ZY).reshape(-1, width)
+    proj = copies_of(proj, "x")
+    proj, early_q = lax.optimization_barrier((proj, q))
+    proj = lax.all_to_all(proj, "x", 0, 0, tiled=True).reshape(-1, width)
 
     latitude = (np.arange(total, dtype=np.float32) + np.float32(0.5)) * np.float32(math.pi / total)
     logw = jnp.asarray(np.log(np.sin(latitude)).astype(np.float32))
@@ -370,9 +340,10 @@
         edges.append((low, high))
     query_grad, key_grad, value_grad = whole
 
-    partial = scatter_sum(partial, XZ).astype(BF)
-    partial = scatter_sum(partial, "y").astype(BF)
-    edges[-1] = after(edges[-1], partial)
+    partial = scatter_sum(partial, "x").astype(BF)
+    partial, edges[-1] = lax.optimization_barrier((partial, edges[-1]))
+    partial = scatter_sum(partial, ZY).astype(BF)
+    partial, edges[-1] = lax.optimization_barrier((partial, edges[-1]))
     samples = lax.axis_size(DP)
     gathered = spread(partial, DP).reshape((samples // 2, 2) + partial.shape)
     summed = jnp.sum(gathered.astype(F32), axis=0)

time: 180 us -> 143 us (0.79)
  the two profiles are of different devices: /device:TPU:120 before, /device:TPU:1 now
where the time goes in v3:
time: 143 us; the launch traced here: 141 us
  starting transfers between devices  61.4 us (43%)
  waiting for transfers between devices  34.8 us (24%)
  Pallas kernels  25.6 us (18%)
  local copies, waits for them, and re-layouts  9.02 us (6%)
  matrix products  6.18 us (4%)
  other arithmetic  3.29 us (2%)
    all_to_all x2, starting transfers between devices, spread(): return lax.all_to_all(copies_of(value, axes), axes, 0, 0, tiled=True)  23.7 us
    ppermute x8, starting transfers between devices, lat_shift(): return lax.ppermute(value, LAT, pairs)  18.5 us
    ppermute x8, waiting for transfers between devices, lat_shift(): return lax.ppermute(value, LAT, pairs)  13.6 us
    all_to_all x1, waiting for transfers between devices, local(): proj = lax.all_to_all(proj, 'x', 0, 0, tiled=True).reshape(-1, width)  13.3 us
    pallas_call x2, Pallas kernels, backward(): pl.pallas_call(backward_kernel, grid=(steps,), in_specs=specs + [pl.Block...  10.9 us
    pallas_call x2, Pallas kernels, forward(): pl.pallas_call(forward_kernel, grid=(steps,), in_specs=specs + [pl.BlockS...  10.5 us
    all_to_all x1, starting transfers between devices, local(): proj = lax.all_to_all(proj, 'x', 0, 0, tiled=True).reshape(-1, width)  8.84 us
    all_to_all x2, starting transfers between devices, scatter_sum(): received = lax.all_to_all(blocks, axes, 0, 0, tiled=True)  7.05 us
  transfers between devices with their start and end apart: 14, of which 9 were waited for; matrix products, arithmetic and copies ran while one was open for 9% of the time, Pallas kernels for 17%

profile of v3, /device:TPU:1, one launch (start us, length us, event | category | flops | bytes accessed | tf_op | source)
XLA Modules:
  0.0 141.2 jit_solution(8331668185809048978)
XLA Ops:
  0.6 0.0 copy-start
  0.6 1.7 %broadcast_in_dim.8 = bf16[16,16,1024]{2,1,0:T(8,128)(2,1)} broadcast(bf16[16,1024]{1,0:T(8,128)(2,1)} %param.13), dimensions={1,2} | broadcast | bytes 557056 | tf_op jit(solution)/shard_map/broadcast_in_dim | solution.py:279
  2.3 9.6 %all-to-all-start = ((bf16[16,16,1024]{2,1,0:T(8,128)(2,1)}), bf16[16,16,1024]{2,1,0:T(8,128)(2,1)S(1)}, u32[]{:S(2)}, u32[]{:S(2)}) async-start(bf16[16,16,1024]{2,1,0:T(8,128)(2,1)} %broadcast_in_dim.8), calls=%async_computation | async-start | bytes 1048576 | tf_op jit(solution)/shard_map/all_to_all | solution.py:283
  11.9 1.3 slice_bitcast_fusion
  13.1 0.8 pad_maximum_fusion.1
  14.0 1.3 collective-permute-start.3
  15.3 4.0 %collective-permute-start.2 = (bf16[2,256,512]{2,1,0:T(8,128)(2,1)}, bf16[2,256,512]{2,1,0:T(8,128)(2,1)S(1)}, u32[]{:S(2)}, u32[]{:S(2)}) collective-permute-start(bf16[2,256,512]{2,1,0:T(8,128)(2,1)} %pad_maximum_fusion.1), channel_id=1, source_target_pairs={{0,1},{1,2},{2,3},{3,4},{4,5},{5,6},{6,7},{7,8},{8,9},{9,10},{10,1... | collective-permute-start | bytes 1572872 | tf_op jit(solution)/shard_map/ppermute | solution.py:271
  19.3 0.8 pad_maximum_fusion
  20.1 1.3 collective-permute-start.1
  21.4 4.0 %collective-permute-start = (bf16[2,256,512]{2,1,0:T(8,128)(2,1)}, bf16[2,256,512]{2,1,0:T(8,128)(2,1)S(1)}, u32[]{:S(2)}, u32[]{:S(2)}) collective-permute-start(bf16[2,256,512]{2,1,0:T(8,128)(2,1)} %pad_maximum_fusion), channel_id=1, source_target_pairs={{0,1},{1,2},{2,3},{3,4},{4,5},{5,6},{6,7},{7,8},{8,9},{9,10},{10,1... | collective-permute-start | bytes 1572872 | tf_op jit(solution)/shard_map/ppermute | solution.py:271
  25.5 0.2 all-to-all-done
  25.6 1.7 %broadcast_in_dim.10 = bf16[4,256,1024]{2,1,0:T(8,128)(2,1)} broadcast(bf16[256,1024]{1,0:T(8,128)(2,1)S(1)} %bitcast.51), dimensions={1,2} | broadcast | bytes 2621440 | tf_op jit(solution)/shard_map/broadcast_in_dim | solution.py:279
  27.3 8.8 %all-to-all-start.1 = ((bf16[4,256,1024]{2,1,0:T(8,128)(2,1)}), bf16[4,256,1024]{2,1,0:T(8,128)(2,1)}, u32[]{:S(2)}, u32[]{:S(2)}) async-start(bf16[4,256,1024]{2,1,0:T(8,128)(2,1)} %broadcast_in_dim.10), calls=%async_computation.1 | async-start | bytes 4194304 | tf_op jit(solution)/shard_map/all_to_all | solution.py:314
  36.2 0.8 copy-done.2
  37.0 0.2 copy-done.3
  37.1 5.3 %attention_forward.2 = (bf16[256,1024]{1,0:T(8,128)(2,1)}, bf16[4,2,640,256]{3,2,1,0:T(8,128)(2,1)}) custom-call(s32[1]{0:T(128)} %bitcast.3.first_ref, s32[128]{0:T(128)} %lo_ref.3, s32[128]{0:T(128)} %hi_ref.3, s32[128]{0:T(128)} %half_ref.3, f32[128]{0:T(128)} %constant.41.clone.logw_ref, bf16[256,1024]{1,0:T(8,128)(2,1)} %bitcast.47, ...), custom_call_target="tpu_custom_call" | custom-call | flops 20000000000 | bytes 40000000 | tf_op jit(solution)/shard_map/attention_forward/pallas_call | solution.py:204
  42.4 5.0 %collective-permute-done.1.kn_ref.vn_ref = bf16[2,256,512]{2,1,0:T(8,128)(2,1)S(1)} collective-permute-done((bf16[2,256,512]{2,1,0:T(8,128)(2,1)}, bf16[2,256,512]{2,1,0:T(8,128)(2,1)S(1)}, u32[]{:S(2)}, u32[]{:S(2)}) %collective-permute-start.1) | collective-permute-done | bytes 524320 | tf_op jit(solution)/shard_map/ppermute | solution.py:271
  47.5 0.8 copy-done.4
  48.2 0.2 copy-done.5
  48.4 5.3 %attention_forward.3 = (bf16[256,1024]{1,0:T(8,128)(2,1)}, bf16[4,2,640,256]{3,2,1,0:T(8,128)(2,1)}) custom-call(s32[1]{0:T(128)} %bitcast.3.first_ref, s32[128]{0:T(128)} %lo_ref.3, s32[128]{0:T(128)} %hi_ref.3, s32[128]{0:T(128)} %half_ref.3, f32[128]{0:T(128)} %constant.41.clone.logw_ref, ...), custom_call_target="tpu_custom_call", output_to_operand_aliasing={{0}: (12, {})} | custom-call | flops 20000000000 | bytes 40000000 | tf_op jit(solution)/shard_map/attention_forward/pallas_call | solution.py:204
  53.7 1.6 %convolution_convert_fusion = bf16[1024,512]{1,0:T(8,128)(2,1)S(1)} fusion(bf16[256,1024]{1,0:T(8,128)(2,1)} %get-tuple-element.35.o_ref, bf16[256,1024]{1,0:T(8,128)(2,1)S(1)} %bitcast.33, s32[]{:T(128)S(6)} %select_n.7), kind=kOutput, calls=%fused_computation.1 | convolution fusion | flops 268959744 | bytes 1835012 | tf_op jit(solution)/shard_map/dot_general | solution.py:31
  55.3 3.3 %collective-permute-start.4 = (bf16[1024,512]{1,0:T(8,128)(2,1)S(1)}, bf16[1024,512]{1,0:T(8,128)(2,1)S(1)}, u32[]{:S(2)}, u32[]{:S(2)}) collective-permute-start(bf16[1024,512]{1,0:T(8,128)(2,1)S(1)} %convolution_convert_fusion), channel_id=1, source_target_pairs={{0,64},{64,0},{1,65},{65,1},{2,66},{66,2},{3,67},{67,3},{4,68},{68... | collective-permute-start | bytes 3145736 | tf_op jit(solution)/shard_map/ppermute | solution.py:275
  58.6 2.3 %collective-permute-done.4 = bf16[1024,512]{1,0:T(8,128)(2,1)S(1)} collective-permute-done((bf16[1024,512]{1,0:T(8,128)(2,1)S(1)}, bf16[1024,512]{1,0:T(8,128)(2,1)S(1)}, u32[]{:S(2)}, u32[]{:S(2)}) %collective-permute-start.4) | collective-permute-done | bytes 1048608 | tf_op jit(solution)/shard_map/ppermute | solution.py:275
  60.9 1.5 %add_convert_fusion = bf16[1024,512]{1,0:T(8,128)(2,1)} fusion(bf16[1024,512]{1,0:T(8,128)(2,1)S(1)} %collective-permute-done.4, bf16[256,1024]{1,0:T(8,128)(2,1)S(1)} %copy-done.1, bf16[256,1024]{1,0:T(8,128)(2,1)S(1)} %bitcast.32, s32[]{:T(128)S(6)} %select_n.6), kind=kOutput, calls=%fused_computation | convolution fusion | flops 270008320 | bytes 2883588 | tf_op jit(solution)/shard_map/dot_general | solution.py:31
  62.3 13.3 %all-to-all-done.1 = bf16[4,256,1024]{2,1,0:T(8,128)(2,1)} async-done(((bf16[4,256,1024]{2,1,0:T(8,128)(2,1)}), bf16[4,256,1024]{2,1,0:T(8,128)(2,1)}, u32[]{:S(2)}, u32[]{:S(2)}) %all-to-all-start.1) | async-done | bytes 2097184 | tf_op jit(solution)/shard_map/all_to_all | solution.py:314
  75.7 3.5 %all-to-all-start.2 = ((bf16[4,256,512]{2,1,0:T(8,128)(2,1)}), bf16[4,256,512]{2,1,0:T(8,128)(2,1)S(1)}, u32[]{:S(2)}, u32[]{:S(2)}) async-start(bf16[4,256,512]{2,1,0:T(8,128)(2,1)} %bitcast.13), calls=%async_computation.2 | async-start | bytes 2097152 | tf_op jit(solution)/shard_map/all_to_all | solution.py:289
  79.2 3.1 %fusion.g_ref = bf16[256,1024]{1,0:T(8,128)(2,1)} fusion(bf16[1024,1024]{1,0:T(8,128)(2,1)} %bitcast.2, bf16[256,1024]{1,0:T(8,128)(2,1)S(1)} %bitcast.34), kind=kOutput, calls=%fused_computation.3 | convolution fusion | flops 537133056 | bytes 3145728 | tf_op jit(solution)/shard_map/dot_general | solution.py:31
  82.3 5.4 %attention_backward.2 = (bf16[256,1024]{1,0:T(8,128)(2,1)}, bf16[256,1024]{1,0:T(8,128)(2,1)}, bf16[256,1024]{1,0:T(8,128)(2,1)}, bf16[2,256,512]{2,1,0:T(8,128)(2,1)}, bf16[2,256,512]{2,1,0:T(8,128)(2,1)}) custom-call(bf16[256,1024]{1,0:T(8,128)(2,1)} %bitcast.49, bf16[256,1024]{1,0:T(8,128)(2,1)} %fusion.g_ref, bf16[256,1024]{1,0:T(8,128)(2,1)} %get-tuple-element.35.o_ref, ...), custom_call_target="tpu_custom_call" | custom-call | flops 1000000 | bytes 100000 | tf_op jit(solution)/shard_map/attention_backward/pallas_call | solution.py:232
  87.8 5.5 %attention_backward.3 = (bf16[256,1024]{1,0:T(8,128)(2,1)}, bf16[256,1024]{1,0:T(8,128)(2,1)}, bf16[256,1024]{1,0:T(8,128)(2,1)}, bf16[2,256,512]{2,1,0:T(8,128)(2,1)}, bf16[2,256,512]{2,1,0:T(8,128)(2,1)}) custom-call(bf16[256,1024]{1,0:T(8,128)(2,1)} %bitcast.50, ...), custom_call_target="tpu_custom_call", output_to_operand_aliasing={{0}: (10, {}), {1}: (11, {}), {2}: (12, {})} | custom-call | flops 1000000 | bytes 100000 | tf_op jit(solution)/shard_map/attention_backward/pallas_call | solution.py:232
  93.2 0.6 all-to-all-done.2
  93.9 0.9 reduce_sum.33
  94.8 3.5 %all-to-all-start.3 = ((bf16[16,16,512]{2,1,0:T(8,128)(2,1)}), bf16[16,16,512]{2,1,0:T(8,128)(2,1)S(1)}, u32[]{:S(2)}, u32[]{:S(2)}) async-start(bf16[16,16,512]{2,1,0:T(8,128)(2,1)} %bitcast.14), calls=%async_computation.3 | async-start | bytes 524288 | tf_op jit(solution)/shard_map/all_to_all | solution.py:289
  98.3 3.2 %collective-permute-start.7 = (bf16[2,256,512]{2,1,0:T(8,128)(2,1)}, bf16[2,256,512]{2,1,0:T(8,128)(2,1)S(1)}, u32[]{:S(2)}, u32[]{:S(2)}) collective-permute-start(bf16[2,256,512]{2,1,0:T(8,128)(2,1)} %get-tuple-element.51), channel_id=1, source_target_pairs={{0,1},{1,2},{2,3},{3,4},{4,5},{5,6},{6,7},{7,8},{8,9},{9,10},{10,1... | collective-permute-start | bytes 1572872 | tf_op jit(solution)/shard_map/ppermute | solution.py:271
  101.5 1.3 collective-permute-start.8
  102.8 3.3 %all-to-all-done.3 = bf16[16,16,512]{2,1,0:T(8,128)(2,1)S(1)} async-done(((bf16[16,16,512]{2,1,0:T(8,128)(2,1)}), bf16[16,16,512]{2,1,0:T(8,128)(2,1)S(1)}, u32[]{:S(2)}, u32[]{:S(2)}) %all-to-all-start.3) | async-done | bytes 262176 | tf_op jit(solution)/shard_map/all_to_all | solution.py:289
  106.2 0.7 broadcast_in_dim.22
  106.8 14.2 %all-to-all-start.4 = ((bf16[8,16,512]{2,1,0:T(8,128)(2,1)}), bf16[8,16,512]{2,1,0:T(8,128)(2,1)S(1)}, u32[]{:S(2)}, u32[]{:S(2)}) async-start(bf16[8,16,512]{2,1,0:T(8,128)(2,1)} %broadcast_in_dim.22), calls=%async_computation.4 | async-start | bytes 262144 | tf_op jit(solution)/shard_map/all_to_all | solution.py:283
  121.0 2.2 %collective-permute-start.5 = (bf16[2,256,512]{2,1,0:T(8,128)(2,1)}, bf16[2,256,512]{2,1,0:T(8,128)(2,1)S(1)}, u32[]{:S(2)}, u32[]{:S(2)}) collective-permute-start(bf16[2,256,512]{2,1,0:T(8,128)(2,1)} %get-tuple-element.49), channel_id=1, source_target_pairs={{0,1},{1,2},{2,3},{3,4},{4,5},{5,6},{6,7},{7,8},{8,9},{9,10},{10,1... | collective-permute-start | bytes 1572872 | tf_op jit(solution)/shard_map/ppermute | solution.py:271
  123.2 1.3 collective-permute-start.6
  124.5 0.8 copy-done.8
  125.3 0.2 copy-done.9
  125.5 2.1 %add_arrived.2 = (bf16[256,1024]{1,0:T(8,128)(2,1)}, bf16[256,1024]{1,0:T(8,128)(2,1)}) custom-call(bf16[2,256,512]{2,1,0:T(8,128)(2,1)} %copy-done.8, bf16[2,256,512]{2,1,0:T(8,128)(2,1)} %copy-done.9, bf16[256,1024]{1,0:T(8,128)(2,1)} %get-tuple-element.53.own_key_ref, ...), custom_call_target="tpu_custom_call", output_to_operand_aliasing={{0}: (2, {}), {1}: (3, {})} | custom-call | flops 1000000 | bytes 100000 | tf_op jit(solution)/shard_map/add_arrived/pallas_call | solution.py:256
  127.6 1.5 %all-to-all-done.4 = bf16[8,16,512]{2,1,0:T(8,128)(2,1)S(1)} async-done(((bf16[8,16,512]{2,1,0:T(8,128)(2,1)}), bf16[8,16,512]{2,1,0:T(8,128)(2,1)S(1)}, u32[]{:S(2)}, u32[]{:S(2)}) %all-to-all-start.4) | async-done | bytes 131104 | tf_op jit(solution)/shard_map/all_to_all | solution.py:283
  129.1 0.6 maximum_multiply_fusion
  129.7 5.1 %collective-permute-done.5.below_ref = bf16[2,256,512]{2,1,0:T(8,128)(2,1)S(1)} collective-permute-done((bf16[2,256,512]{2,1,0:T(8,128)(2,1)}, bf16[2,256,512]{2,1,0:T(8,128)(2,1)S(1)}, u32[]{:S(2)}, u32[]{:S(2)}) %collective-permute-start.5) | collective-permute-done | bytes 524320 | tf_op jit(solution)/shard_map/ppermute | solution.py:271
  134.8 3.5 %collective-permute-done.6.above_ref = bf16[2,256,512]{2,1,0:T(8,128)(2,1)S(1)} collective-permute-done((bf16[2,256,512]{2,1,0:T(8,128)(2,1)S(1)}, bf16[2,256,512]{2,1,0:T(8,128)(2,1)S(1)}, u32[]{:S(2)}, u32[]{:S(2)}) %collective-permute-start.6) | collective-permute-done | bytes 524320 | tf_op jit(solution)/shard_map/ppermute | solution.py:271
  138.3 0.8 copy-done.7
  139.1 2.1 %add_arrived.3 = (bf16[256,1024]{1,0:T(8,128)(2,1)}, bf16[256,1024]{1,0:T(8,128)(2,1)}) custom-call(bf16[2,256,512]{2,1,0:T(8,128)(2,1)} %copy-done.6, bf16[2,256,512]{2,1,0:T(8,128)(2,1)} %copy-done.7, bf16[256,1024]{1,0:T(8,128)(2,1)} %get-tuple-element.55.own_key_ref, ...), custom_call_target="tpu_custom_call", output_to_operand_aliasing={{0}: (2, {}), {1}: (3, {})} | custom-call | flops 1000000 | bytes 100000 | tf_op jit(solution)/shard_map/add_arrived/pallas_call | solution.py:256
  (22 shorter events, 0.1 us)
Async XLA Ops:
  0.6 53.1 %copy-start = (bf16[1,2,128,1024]{3,2,1,0:T(8,128)(2,1)S(1)}, bf16[1,2,128,1024]{3,2,1,0:T(8,128)(2,1)}, u32[]{:S(2)}) copy-start(bf16[1,2,128,1024]{3,2,1,0:T(8,128)(2,1)} %param.12) | copy-start | bytes 1572868
  2.3 23.3 %all-to-all-start = ((bf16[16,16,1024]{2,1,0:T(8,128)(2,1)}), bf16[16,16,1024]{2,1,0:T(8,128)(2,1)S(1)}, u32[]{:S(2)}, u32[]{:S(2)}) async-start(bf16[16,16,1024]{2,1,0:T(8,128)(2,1)} %broadcast_in_dim.8), calls=%async_computation | async-start | bytes 1048576 | tf_op jit(solution)/shard_map/all_to_all | solution.py:283
  14.0 22.2 %collective-permute-start.3 = (bf16[2,256,512]{2,1,0:T(8,128)(2,1)}, bf16[2,256,512]{2,1,0:T(8,128)(2,1)S(1)}, u32[]{:S(2)}, u32[]{:S(2)}) collective-permute-start(bf16[2,256,512]{2,1,0:T(8,128)(2,1)} %pad_maximum_fusion.1), channel_id=1, source_target_pairs={{1,0},{2,1},{3,2},{4,3},{5,4},{6,5},{7,6},{8,7},{9,8},{10,9},{11,1... | collective-permute-start | bytes 1572872 | tf_op jit(solution)/shard_map/ppermute | solution.py:271
  15.3 20.9 %collective-permute-start.2 = (bf16[2,256,512]{2,1,0:T(8,128)(2,1)}, bf16[2,256,512]{2,1,0:T(8,128)(2,1)S(1)}, u32[]{:S(2)}, u32[]{:S(2)}) collective-permute-start(bf16[2,256,512]{2,1,0:T(8,128)(2,1)} %pad_maximum_fusion.1), channel_id=1, source_target_pairs={{0,1},{1,2},{2,3},{3,4},{4,5},{5,6},{6,7},{7,8},{8,9},{9,10},{10,1... | collective-permute-start | bytes 1572872 | tf_op jit(solution)/shard_map/ppermute | solution.py:271
  20.1 27.3 %collective-permute-start.1 = (bf16[2,256,512]{2,1,0:T(8,128)(2,1)}, bf16[2,256,512]{2,1,0:T(8,128)(2,1)S(1)}, u32[]{:S(2)}, u32[]{:S(2)}) collective-permute-start(bf16[2,256,512]{2,1,0:T(8,128)(2,1)} %pad_maximum_fusion), channel_id=1, source_target_pairs={{1,0},{2,1},{3,2},{4,3},{5,4},{6,5},{7,6},{8,7},{9,8},{10,9},{11,1... | collective-permute-start | bytes 1572872 | tf_op jit(solution)/shard_map/ppermute | solution.py:271
  21.4 26.0 %collective-permute-start = (bf16[2,256,512]{2,1,0:T(8,128)(2,1)}, bf16[2,256,512]{2,1,0:T(8,128)(2,1)S(1)}, u32[]{:S(2)}, u32[]{:S(2)}) collective-permute-start(bf16[2,256,512]{2,1,0:T(8,128)(2,1)} %pad_maximum_fusion), channel_id=1, source_target_pairs={{0,1},{1,2},{2,3},{3,4},{4,5},{5,6},{6,7},{7,8},{8,9},{9,10},{10,1... | collective-permute-start | bytes 1572872 | tf_op jit(solution)/shard_map/ppermute | solution.py:271
  27.3 48.4 %all-to-all-start.1 = ((bf16[4,256,1024]{2,1,0:T(8,128)(2,1)}), bf16[4,256,1024]{2,1,0:T(8,128)(2,1)}, u32[]{:S(2)}, u32[]{:S(2)}) async-start(bf16[4,256,1024]{2,1,0:T(8,128)(2,1)} %broadcast_in_dim.10), calls=%async_computation.1 | async-start | bytes 4194304 | tf_op jit(solution)/shard_map/all_to_all | solution.py:314
  36.1 0.8 copy-start.2
  36.2 1.0 copy-start.3
  47.4 0.8 copy-start.4
  47.5 1.0 copy-start.5
  53.7 7.1 %copy-start.1 = (bf16[256,1024]{1,0:T(8,128)(2,1)S(1)}, bf16[256,1024]{1,0:T(8,128)(2,1)}, u32[]{:S(2)}) copy-start(bf16[256,1024]{1,0:T(8,128)(2,1)} %get-tuple-element.35.o_ref) | copy-start | bytes 1572868
  55.3 5.5 %collective-permute-start.4 = (bf16[1024,512]{1,0:T(8,128)(2,1)S(1)}, bf16[1024,512]{1,0:T(8,128)(2,1)S(1)}, u32[]{:S(2)}, u32[]{:S(2)}) collective-permute-start(bf16[1024,512]{1,0:T(8,128)(2,1)S(1)} %convolution_convert_fusion), channel_id=1, source_target_pairs={{0,64},{64,0},{1,65},{65,1},{2,66},{66,2},{3,67},{67,3},{4,68},{68... | collective-permute-start | bytes 3145736 | tf_op jit(solution)/shard_map/ppermute | solution.py:275
  75.7 18.2 %all-to-all-start.2 = ((bf16[4,256,512]{2,1,0:T(8,128)(2,1)}), bf16[4,256,512]{2,1,0:T(8,128)(2,1)S(1)}, u32[]{:S(2)}, u32[]{:S(2)}) async-start(bf16[4,256,512]{2,1,0:T(8,128)(2,1)} %bitcast.13), calls=%async_computation.2 | async-start | bytes 2097152 | tf_op jit(solution)/shard_map/all_to_all | solution.py:289
  93.2 29.9 %copy-start.10 = (bf16[2,256,512]{2,1,0:T(8,128)(2,1)S(1)}, bf16[2,256,512]{2,1,0:T(8,128)(2,1)}, u32[]{:S(2)}) copy-start(bf16[2,256,512]{2,1,0:T(8,128)(2,1)} %get-tuple-element.50) | copy-start | bytes 1572868
  94.8 11.4 %all-to-all-start.3 = ((bf16[16,16,512]{2,1,0:T(8,128)(2,1)}), bf16[16,16,512]{2,1,0:T(8,128)(2,1)S(1)}, u32[]{:S(2)}, u32[]{:S(2)}) async-start(bf16[16,16,512]{2,1,0:T(8,128)(2,1)} %bitcast.14), calls=%async_computation.3 | async-start | bytes 524288 | tf_op jit(solution)/shard_map/all_to_all | solution.py:289
  98.3 26.2 %collective-permute-start.7 = (bf16[2,256,512]{2,1,0:T(8,128)(2,1)}, bf16[2,256,512]{2,1,0:T(8,128)(2,1)S(1)}, u32[]{:S(2)}, u32[]{:S(2)}) collective-permute-start(bf16[2,256,512]{2,1,0:T(8,128)(2,1)} %get-tuple-element.51), channel_id=1, source_target_pairs={{0,1},{1,2},{2,3},{3,4},{4,5},{5,6},{6,7},{7,8},{8,9},{9,10},{10,1... | collective-permute-start | bytes 1572872 | tf_op jit(solution)/shard_map/ppermute | solution.py:271
  101.5 23.0 %collective-permute-start.8 = (bf16[2,256,512]{2,1,0:T(8,128)(2,1)}, bf16[2,256,512]{2,1,0:T(8,128)(2,1)S(1)}, u32[]{:S(2)}, u32[]{:S(2)}) collective-permute-start(bf16[2,256,512]{2,1,0:T(8,128)(2,1)} %get-tuple-element.52), channel_id=1, source_target_pairs={{1,0},{2,1},{3,2},{4,3},{5,4},{6,5},{7,6},{8,7},{9,8},{10,9},{11,1... | collective-permute-start | bytes 1572872 | tf_op jit(solution)/shard_map/ppermute | solution.py:271
  106.8 22.2 %all-to-all-start.4 = ((bf16[8,16,512]{2,1,0:T(8,128)(2,1)}), bf16[8,16,512]{2,1,0:T(8,128)(2,1)S(1)}, u32[]{:S(2)}, u32[]{:S(2)}) async-start(bf16[8,16,512]{2,1,0:T(8,128)(2,1)} %broadcast_in_dim.22), calls=%async_computation.4 | async-start | bytes 262144 | tf_op jit(solution)/shard_map/all_to_all | solution.py:283
  121.0 13.8 %collective-permute-start.5 = (bf16[2,256,512]{2,1,0:T(8,128)(2,1)}, bf16[2,256,512]{2,1,0:T(8,128)(2,1)S(1)}, u32[]{:S(2)}, u32[]{:S(2)}) collective-permute-start(bf16[2,256,512]{2,1,0:T(8,128)(2,1)} %get-tuple-element.49), channel_id=1, source_target_pairs={{0,1},{1,2},{2,3},{3,4},{4,5},{5,6},{6,7},{7,8},{8,9},{9,10},{10,1... | collective-permute-start | bytes 1572872 | tf_op jit(solution)/shard_map/ppermute | solution.py:271
  123.2 15.1 %collective-permute-start.6 = (bf16[2,256,512]{2,1,0:T(8,128)(2,1)S(1)}, bf16[2,256,512]{2,1,0:T(8,128)(2,1)S(1)}, u32[]{:S(2)}, u32[]{:S(2)}) collective-permute-start(bf16[2,256,512]{2,1,0:T(8,128)(2,1)S(1)} %copy-done.10), channel_id=1, source_target_pairs={{1,0},{2,1},{3,2},{4,3},{5,4},{6,5},{7,6},{8,7},{9,8},{10,9},{11,1... | collective-permute-start | bytes 1572872 | tf_op jit(solution)/shard_map/ppermute | solution.py:271
  124.5 0.8 copy-start.8
  124.5 1.0 copy-start.9
  134.8 3.5 %copy-start.6 = (bf16[2,256,512]{2,1,0:T(8,128)(2,1)}, bf16[2,256,512]{2,1,0:T(8,128)(2,1)S(1)}, u32[]{:S(2)}) copy-start(bf16[2,256,512]{2,1,0:T(8,128)(2,1)S(1)} %collective-permute-done.5.below_ref) | copy-start | bytes 1572868
  138.3 0.8 copy-start.7

commit v4 on v3

--- a/solution.py
+++ b/solution.py
@@ -22,7 +22,7 @@
 LAT = ("x", "zl", "y")
 BF = jnp.bfloat16
 F32 = jnp.float32
-VMEM_LIMIT = 60 * 1024 * 1024
+VMEM_LIMIT = 60*1024*1024
 LARGE = pl.CostEstimate(flops=2*10**10, bytes_accessed=4*10**7, transcendentals=0)
 SMALL = pl.CostEstimate(flops=10**6, bytes_accessed=10**5, transcendentals=0)
 
@@ -308,10 +308,11 @@
     ]
     below = [lat_shift(part, 1) for part in parts]
     above = [lat_shift(part, -1) for part in parts]
-    proj = spread(out_proj, ZY).reshape(-1, width)
+    proj = lax.dynamic_slice_in_dim(out_proj, mine, half_width, axis=1)
+    proj = spread(proj, ZY).reshape(-1, half_width)
     proj = copies_of(proj, "x")
     proj, early_q = lax.optimization_barrier((proj, q))
-    proj = lax.all_to_all(proj, "x", 0, 0, tiled=True).reshape(-1, width)
+    proj = lax.all_to_all(proj, "x", 0, 0, tiled=True).reshape(-1, half_width)
 
     latitude = (np.arange(total, dtype=np.float32) + np.float32(0.5)) * np.float32(math.pi / total)
     logw = jnp.asarray(np.log(np.sin(latitude)).astype(np.float32))
@@ -327,11 +328,12 @@
     grad_mine = lax.dynamic_slice_in_dim(grad_flat, mine, half_width, axis=1)
     grad_other = lax.dynamic_slice_in_dim(grad_flat, others, half_width, axis=1)
     sent = dot(attended, grad_other, ((0,), (0,))).astype(BF)
+    proj, sent = lax.optimization_barrier((proj, sent))
     received = core_swap(sent)
+    proj_other = core_swap(proj)
     partial = (dot(attended, grad_mine, ((0,), (0,))) + received.astype(F32)).astype(BF)
-
-    proj, partial = lax.optimization_barrier((proj, partial))
-    attn_grad = dot(grad_flat, proj, ((1,), (1,))).astype(BF)
+    attn_grad = dot(grad_mine, proj, ((1,), (1,))) + dot(grad_other, proj_other, ((1,), (1,)))
+    attn_grad = attn_grad.astype(BF)
     whole, edges = [], []
     for n in range(HALVES):
         *whole, low, high = backward(
@@ -341,19 +343,18 @@
     query_grad, key_grad, value_grad = whole
 
     partial = scatter_sum(partial, "x").astype(BF)
-    partial, edges[-1] = lax.optimization_barrier((partial, edges[-1]))
+    arrived = [(lat_shift(edges[0][1], 1), lat_shift(edges[0][0], -1))]
+    partial, arrived[0], edges[1] = lax.optimization_barrier((partial, arrived[0], edges[1]))
     partial = scatter_sum(partial, ZY).astype(BF)
-    partial, edges[-1] = lax.optimization_barrier((partial, edges[-1]))
+    arrived.append((lat_shift(edges[1][1], 1), lat_shift(edges[1][0], -1)))
     samples = lax.axis_size(DP)
     gathered = spread(partial, DP).reshape((samples // 2, 2) + partial.shape)
     summed = jnp.sum(gathered.astype(F32), axis=0)
     scaling = 1.0 / math.sqrt(samples * total * lon)
     proj_grad = jnp.concatenate([summed[0], summed[1]], axis=1) * scaling
 
-    for n, (low, high) in enumerate(edges):
-        key_grad, value_grad = add_arrived(
-            n, key_grad, value_grad, lat_shift(high, 1), lat_shift(low, -1)
-        )
+    for n, (from_below, from_above) in enumerate(arrived):
+        key_grad, value_grad = add_arrived(n, key_grad, value_grad, from_below, from_above)
     shape = query_feats.shape
     return (
         query_grad.reshape(shape),

time: 143 us -> 132 us (0.923)
  waiting for transfers between devices: 34.8 us -> 21.4 us
  starting transfers between devices: 61.4 us -> 64.9 us
  local copies, waits for them, and re-layouts: 9.02 us -> 6.61 us
    ppermute x8, waiting for transfers between devices: 13.6 us -> 5.56 us  [lat_shift(): return lax.ppermute(value, LAT, pairs)]
    all_to_all x1, waiting for transfers between devices: 13.3 us -> 6.29 us  [local(): proj = lax.all_to_all(proj, 'x', 0, 0, tiled=True).reshape(-1, half_width)]
    all_to_all x2, starting transfers between devices: 7.05 us -> 12.1 us  [scatter_sum(): received = lax.all_to_all(blocks, axes, 0, 0, tiled=True)]
    all_to_all x2, waiting for transfers between devices: 1.63 us -> 6.28 us  [spread(): return lax.all_to_all(copies_of(value, axes), axes, 0, 0, tiled=True)]
    all_to_all x1, starting transfers between devices: 8.84 us -> 4.32 us  [local(): proj = lax.all_to_all(proj, 'x', 0, 0, tiled=True).reshape(-1, half_width)]
    ppermute x1 -> x2, waiting for transfers between devices: 2.26 us -> 0.07 us  [core_swap(): return lax.ppermute(value, 'core', [(0, 1), (1, 0)])]
    all_to_all x2, starting transfers between devices: 23.7 us -> 25.2 us  [spread(): return lax.all_to_all(copies_of(value, axes), axes, 0, 0, tiled=True)]
    broadcast_in_dim x3, local copies, waits for them, and re-layouts: 4 us -> 2.54 us  [copies_of(): return jnp.broadcast_to(value[None], (lax.axis_size(axes),) + value.shape)]
  transfers between devices with their start and end apart: 14 -> 15, of which waited for: 9 -> 7; matrix products, arithmetic and copies ran while one was open for 9% -> 10% of each run, Pallas kernels for 17% -> 20%
where the time goes in v4:
time: 132 us; the launch traced here: 131 us
  starting transfers between devices  64.9 us (49%)
  Pallas kernels  25.7 us (19%)
  waiting for transfers between devices  21.4 us (16%)
  matrix products  6.93 us (5%)
  local copies, waits for them, and re-layouts  6.61 us (5%)
  other arithmetic  4.55 us (3%)
    all_to_all x2, starting transfers between devices, spread(): return lax.all_to_all(copies_of(value, axes), axes, 0, 0, tiled=True)  25.2 us
    ppermute x8, starting transfers between devices, lat_shift(): return lax.ppermute(value, LAT, pairs)  18.9 us
    all_to_all x2, starting transfers between devices, scatter_sum(): received = lax.all_to_all(blocks, axes, 0, 0, tiled=True)  12.1 us
    pallas_call x2, Pallas kernels, backward(): pl.pallas_call(backward_kernel, grid=(steps,), in_specs=specs + [pl.Block...  10.9 us
    pallas_call x2, Pallas kernels, forward(): pl.pallas_call(forward_kernel, grid=(steps,), in_specs=specs + [pl.BlockS...  10.5 us
    dot_general x4, matrix products, dot(): return lax.dot_general(a, b, (dims, ((), ())), preferred_element_type=F32)  6.93 us
    all_to_all x1, waiting for transfers between devices, local(): proj = lax.all_to_all(proj, 'x', 0, 0, tiled=True).reshape(-1, half_width)  6.29 us
    all_to_all x2, waiting for transfers between devices, spread(): return lax.all_to_all(copies_of(value, axes), axes, 0, 0, tiled=True)  6.28 us
  transfers between devices with their start and end apart: 15, of which 7 were waited for; matrix products, arithmetic and copies ran while one was open for 10% of the time, Pallas kernels for 20%

profile of v4, /device:TPU:1, one launch (start us, length us, event | category | flops | bytes accessed | tf_op | source)
XLA Modules:
  0.0 130.9 jit_solution(14596612133128512140)
XLA Ops:
  0.6 0.0 copy-start
  0.7 1.3 %slice_bitcast_fusion = (bf16[1,256,512]{2,1,0:T(8,128)(2,1)S(1)}, bf16[1,256,512]{2,1,0:T(8,128)(2,1)S(1)}, bf16[1,256,512]{2,1,0:T(8,128)(2,1)S(1)}, bf16[1,256,512]{2,1,0:T(8,128)(2,1)S(1)}) fusion(bf16[256,1024]{1,0:T(8,128)(2,1)} %bitcast.34, bf16[256,1024]{1,0:T(8,128)(2,1)} %bitcast.39), kind=kLoop, calls=%fused_computation.6 | loop fusion | bytes 2097152 | tf_op jit(solution)/shard_map/stack | solution.py:306
  2.0 0.8 pad_maximum_fusion.1
  2.8 4.0 %collective-permute-start.2 = (bf16[2,256,512]{2,1,0:T(8,128)(2,1)}, bf16[2,256,512]{2,1,0:T(8,128)(2,1)S(1)}, u32[]{:S(2)}, u32[]{:S(2)}) collective-permute-start(bf16[2,256,512]{2,1,0:T(8,128)(2,1)} %pad_maximum_fusion.1), channel_id=1, source_target_pairs={{0,1},{1,2},{2,3},{3,4},{4,5},{5,6},{6,7},{7,8},{8,9},{9,10},{10,1... | collective-permute-start | bytes 1572872 | tf_op jit(solution)/shard_map/ppermute | solution.py:271
  6.9 1.3 collective-permute-start.3
  8.2 0.7 broadcast_in_dim.8
  8.9 10.7 %all-to-all-start = ((bf16[16,16,512]{2,1,0:T(8,128)(2,1)}), bf16[16,16,512]{2,1,0:T(8,128)(2,1)S(1)}, u32[]{:S(2)}, u32[]{:S(2)}) async-start(bf16[16,16,512]{2,1,0:T(8,128)(2,1)} %broadcast_in_dim.8), calls=%async_computation | async-start | bytes 524288 | tf_op jit(solution)/shard_map/all_to_all | solution.py:283
  19.7 0.8 pad_maximum_fusion
  20.5 3.3 %collective-permute-start = (bf16[2,256,512]{2,1,0:T(8,128)(2,1)}, bf16[2,256,512]{2,1,0:T(8,128)(2,1)S(1)}, u32[]{:S(2)}, u32[]{:S(2)}) collective-permute-start(bf16[2,256,512]{2,1,0:T(8,128)(2,1)} %pad_maximum_fusion), channel_id=1, source_target_pairs={{0,1},{1,2},{2,3},{3,4},{4,5},{5,6},{6,7},{7,8},{8,9},{9,10},{10,1... | collective-permute-start | bytes 1572872 | tf_op jit(solution)/shard_map/ppermute | solution.py:271
  23.8 1.3 collective-permute-start.1
  25.1 3.5 %all-to-all-done = bf16[16,16,512]{2,1,0:T(8,128)(2,1)S(1)} async-done(((bf16[16,16,512]{2,1,0:T(8,128)(2,1)}), bf16[16,16,512]{2,1,0:T(8,128)(2,1)S(1)}, u32[]{:S(2)}, u32[]{:S(2)}) %all-to-all-start) | async-done | bytes 262176 | tf_op jit(solution)/shard_map/all_to_all | solution.py:283
  28.6 1.1 broadcast_in_dim.10
  29.7 4.3 %all-to-all-start.1 = ((bf16[4,256,512]{2,1,0:T(8,128)(2,1)}), bf16[4,256,512]{2,1,0:T(8,128)(2,1)S(1)}, u32[]{:S(2)}, u32[]{:S(2)}) async-start(bf16[4,256,512]{2,1,0:T(8,128)(2,1)} %broadcast_in_dim.10), calls=%async_computation.1 | async-start | bytes 2097152 | tf_op jit(solution)/shard_map/all_to_all | solution.py:315
  34.0 0.0 collective-permute-done.2.kp_ref.vp_ref
  34.0 0.0 collective-permute-done.3.kn_ref.vn_ref
  34.1 0.8 copy-done.2
  34.9 0.2 copy-done.3
  35.1 5.3 %attention_forward.2 = (bf16[256,1024]{1,0:T(8,128)(2,1)}, bf16[4,2,640,256]{3,2,1,0:T(8,128)(2,1)}) custom-call(s32[1]{0:T(128)} %bitcast.4.first_ref, s32[128]{0:T(128)} %lo_ref.3, s32[128]{0:T(128)} %hi_ref.3, s32[128]{0:T(128)} %half_ref.3, f32[128]{0:T(128)} %constant.41.clone.logw_ref, bf16[256,1024]{1,0:T(8,128)(2,1)} %bitcast.48, ...), custom_call_target="tpu_custom_call" | custom-call | flops 20000000000 | bytes 40000000 | tf_op jit(solution)/shard_map/attention_forward/pallas_call | solution.py:204
  40.4 0.8 copy-done.4
  41.1 5.3 %attention_forward.3 = (bf16[256,1024]{1,0:T(8,128)(2,1)}, bf16[4,2,640,256]{3,2,1,0:T(8,128)(2,1)}) custom-call(s32[1]{0:T(128)} %bitcast.4.first_ref, s32[128]{0:T(128)} %lo_ref.3, s32[128]{0:T(128)} %hi_ref.3, s32[128]{0:T(128)} %half_ref.3, f32[128]{0:T(128)} %constant.41.clone.logw_ref, ...), custom_call_target="tpu_custom_call", output_to_operand_aliasing={{0}: (12, {})} | custom-call | flops 20000000000 | bytes 40000000 | tf_op jit(solution)/shard_map/attention_forward/pallas_call | solution.py:204
  46.4 2.5 %convolution_convert_fusion = bf16[1024,512]{1,0:T(8,128)(2,1)} fusion(bf16[256,1024]{1,0:T(8,128)(2,1)} %get-tuple-element.34.o_ref, bf16[256,1024]{1,0:T(8,128)(2,1)S(1)} %bitcast.31, s32[]{:T(128)S(6)} %select_n.8), kind=kOutput, calls=%fused_computation.1 | convolution fusion | flops 268959744 | bytes 1835012 | tf_op jit(solution)/shard_map/dot_general | solution.py:31
  49.0 6.3 %all-to-all-done.1 = bf16[4,256,512]{2,1,0:T(8,128)(2,1)S(1)} async-done(((bf16[4,256,512]{2,1,0:T(8,128)(2,1)}), bf16[4,256,512]{2,1,0:T(8,128)(2,1)S(1)}, u32[]{:S(2)}, u32[]{:S(2)}) %all-to-all-start.1) | async-done | bytes 1048608 | tf_op jit(solution)/shard_map/all_to_all | solution.py:315
  55.2 2.4 %collective-permute-start.5 = (bf16[1024,512]{1,0:T(8,128)(2,1)}, bf16[1024,512]{1,0:T(8,128)(2,1)S(1)}, u32[]{:S(2)}, u32[]{:S(2)}) collective-permute-start(bf16[1024,512]{1,0:T(8,128)(2,1)} %convolution_convert_fusion), channel_id=1, source_target_pairs={{0,64},{64,0},{1,65},{65,1},{2,66},{66,2},{3,67},{67,3},{4,68},{68... | collective-permute-start | bytes 3145736 | tf_op jit(solution)/shard_map/ppermute | solution.py:275
  57.6 1.9 %collective-permute-start.4 = (bf16[1024,512]{1,0:T(8,128)(2,1)S(1)}, bf16[1024,512]{1,0:T(8,128)(2,1)}, u32[]{:S(2)}, u32[]{:S(2)}) collective-permute-start(bf16[1024,512]{1,0:T(8,128)(2,1)S(1)} %bitcast.46), channel_id=1, source_target_pairs={{0,64},{64,0},{1,65},{65,1},{2,66},{66,2},{3,67},{67,3},{4,68},{68... | collective-permute-start | bytes 3145736 | tf_op jit(solution)/shard_map/ppermute | solution.py:275
  59.6 0.5 fusion.4
  60.1 0.1 collective-permute-done.5
  60.1 1.4 %add_convert_fusion = bf16[1024,512]{1,0:T(8,128)(2,1)} fusion(bf16[1024,512]{1,0:T(8,128)(2,1)S(1)} %collective-permute-done.5, bf16[256,1024]{1,0:T(8,128)(2,1)S(1)} %copy-done.1, bf16[256,1024]{1,0:T(8,128)(2,1)S(1)} %bitcast.33, s32[]{:T(128)S(6)} %select_n.7), kind=kOutput, calls=%fused_computation | convolution fusion | flops 270008320 | bytes 2883588 | tf_op jit(solution)/shard_map/dot_general | solution.py:31
  61.6 4.3 %all-to-all-start.2 = ((bf16[4,256,512]{2,1,0:T(8,128)(2,1)}), bf16[4,256,512]{2,1,0:T(8,128)(2,1)}, u32[]{:S(2)}, u32[]{:S(2)}) async-start(bf16[4,256,512]{2,1,0:T(8,128)(2,1)} %bitcast.12), calls=%async_computation.2 | async-start | bytes 2097152 | tf_op jit(solution)/shard_map/all_to_all | solution.py:289
  65.8 2.5 %fusion.g_ref = bf16[256,1024]{1,0:T(8,128)(2,1)} fusion(f32[256,1024]{1,0:T(8,128)S(1)} %fusion.4, bf16[1024,512]{1,0:T(8,128)(2,1)} %collective-permute-done.4, bf16[256,1024]{1,0:T(8,128)(2,1)S(1)} %bitcast.32, s32[]{:T(128)S(6)} %select_n.8), kind=kOutput, calls=%fused_computation.3 | convolution fusion | flops 268959744 | bytes 2883588 | tf_op jit(solution)/shard_map/dot_general | solution.py:31
  68.3 5.4 %attention_backward.2 = (bf16[256,1024]{1,0:T(8,128)(2,1)}, bf16[256,1024]{1,0:T(8,128)(2,1)}, bf16[256,1024]{1,0:T(8,128)(2,1)}, bf16[2,256,512]{2,1,0:T(8,128)(2,1)}, bf16[2,256,512]{2,1,0:T(8,128)(2,1)}) custom-call(bf16[256,1024]{1,0:T(8,128)(2,1)} %bitcast.50, bf16[256,1024]{1,0:T(8,128)(2,1)} %fusion.g_ref, bf16[256,1024]{1,0:T(8,128)(2,1)} %get-tuple-element.34.o_ref, ...), custom_call_target="tpu_custom_call" | custom-call | flops 1000000 | bytes 100000 | tf_op jit(solution)/shard_map/attention_backward/pallas_call | solution.py:232
  73.8 3.1 %collective-permute-start.6 = (bf16[2,256,512]{2,1,0:T(8,128)(2,1)}, bf16[2,256,512]{2,1,0:T(8,128)(2,1)S(1)}, u32[]{:S(2)}, u32[]{:S(2)}) collective-permute-start(bf16[2,256,512]{2,1,0:T(8,128)(2,1)} %get-tuple-element.43), channel_id=1, source_target_pairs={{0,1},{1,2},{2,3},{3,4},{4,5},{5,6},{6,7},{7,8},{8,9},{9,10},{10,1... | collective-permute-start | bytes 1572872 | tf_op jit(solution)/shard_map/ppermute | solution.py:271
  76.9 1.3 collective-permute-start.7
  78.2 5.5 %attention_backward.3 = (bf16[256,1024]{1,0:T(8,128)(2,1)}, bf16[256,1024]{1,0:T(8,128)(2,1)}, bf16[256,1024]{1,0:T(8,128)(2,1)}, bf16[2,256,512]{2,1,0:T(8,128)(2,1)}, bf16[2,256,512]{2,1,0:T(8,128)(2,1)}) custom-call(bf16[256,1024]{1,0:T(8,128)(2,1)} %bitcast.51, ...), custom_call_target="tpu_custom_call", output_to_operand_aliasing={{0}: (10, {}), {1}: (11, {}), {2}: (12, {})} | custom-call | flops 1000000 | bytes 100000 | tf_op jit(solution)/shard_map/attention_backward/pallas_call | solution.py:232
  83.7 2.2 %reduce_sum.33 = bf16[256,512]{1,0:T(8,128)(2,1)} reduce(bf16[4,256,512]{2,1,0:T(8,128)(2,1)} %all-to-all-done.2, bf16[]{:T(256)} %constant.38.clone.1), dimensions={0}, to_apply=%region_0.0 | reduce | flops 393216 | bytes 1310722 | tf_op jit(solution)/shard_map/reduce_sum | solution.py:290
  85.8 1.8 %collective-permute-done.6.below_ref = bf16[2,256,512]{2,1,0:T(8,128)(2,1)S(1)} collective-permute-done((bf16[2,256,512]{2,1,0:T(8,128)(2,1)}, bf16[2,256,512]{2,1,0:T(8,128)(2,1)S(1)}, u32[]{:S(2)}, u32[]{:S(2)}) %collective-permute-start.6) | collective-permute-done | bytes 524320 | tf_op jit(solution)/shard_map/ppermute | solution.py:271
  87.7 3.7 %collective-permute-done.7.above_ref = bf16[2,256,512]{2,1,0:T(8,128)(2,1)S(1)} collective-permute-done((bf16[2,256,512]{2,1,0:T(8,128)(2,1)}, bf16[2,256,512]{2,1,0:T(8,128)(2,1)S(1)}, u32[]{:S(2)}, u32[]{:S(2)}) %collective-permute-start.7) | collective-permute-done | bytes 524320 | tf_op jit(solution)/shard_map/ppermute | solution.py:271
  91.4 7.9 %all-to-all-start.3 = ((bf16[16,16,512]{2,1,0:T(8,128)(2,1)}), bf16[16,16,512]{2,1,0:T(8,128)(2,1)S(1)}, u32[]{:S(2)}, u32[]{:S(2)}) async-start(bf16[16,16,512]{2,1,0:T(8,128)(2,1)} %bitcast.15), calls=%async_computation.3 | async-start | bytes 524288 | tf_op jit(solution)/shard_map/all_to_all | solution.py:289
  99.3 3.3 %collective-permute-start.8 = (bf16[2,256,512]{2,1,0:T(8,128)(2,1)}, bf16[2,256,512]{2,1,0:T(8,128)(2,1)S(1)}, u32[]{:S(2)}, u32[]{:S(2)}) collective-permute-start(bf16[2,256,512]{2,1,0:T(8,128)(2,1)} %get-tuple-element.47), channel_id=1, source_target_pairs={{0,1},{1,2},{2,3},{3,4},{4,5},{5,6},{6,7},{7,8},{8,9},{9,10},{10,1... | collective-permute-start | bytes 1572872 | tf_op jit(solution)/shard_map/ppermute | solution.py:271
  102.6 1.3 collective-permute-start.9
  103.9 3.2 %all-to-all-done.3 = bf16[16,16,512]{2,1,0:T(8,128)(2,1)S(1)} async-done(((bf16[16,16,512]{2,1,0:T(8,128)(2,1)}), bf16[16,16,512]{2,1,0:T(8,128)(2,1)S(1)}, u32[]{:S(2)}, u32[]{:S(2)}) %all-to-all-start.3) | async-done | bytes 262176 | tf_op jit(solution)/shard_map/all_to_all | solution.py:289
  107.1 0.7 broadcast_in_dim.22
  107.7 14.5 %all-to-all-start.4 = ((bf16[8,16,512]{2,1,0:T(8,128)(2,1)}), bf16[8,16,512]{2,1,0:T(8,128)(2,1)S(1)}, u32[]{:S(2)}, u32[]{:S(2)}) async-start(bf16[8,16,512]{2,1,0:T(8,128)(2,1)} %broadcast_in_dim.22), calls=%async_computation.4 | async-start | bytes 262144 | tf_op jit(solution)/shard_map/all_to_all | solution.py:283
  122.2 2.1 %add_arrived.2 = (bf16[256,1024]{1,0:T(8,128)(2,1)}, bf16[256,1024]{1,0:T(8,128)(2,1)}) custom-call(bf16[2,256,512]{2,1,0:T(8,128)(2,1)} %copy-done.5, bf16[2,256,512]{2,1,0:T(8,128)(2,1)} %copy-done.6, bf16[256,1024]{1,0:T(8,128)(2,1)} %get-tuple-element.51.own_key_ref, ...), custom_call_target="tpu_custom_call", output_to_operand_aliasing={{0}: (2, {}), {1}: (3, {})} | custom-call | flops 1000000 | bytes 100000 | tf_op jit(solution)/shard_map/add_arrived/pallas_call | solution.py:256
  124.4 0.8 copy-done.7
  125.2 0.2 copy-done.8
  125.3 2.1 %add_arrived.3 = (bf16[256,1024]{1,0:T(8,128)(2,1)}, bf16[256,1024]{1,0:T(8,128)(2,1)}) custom-call(bf16[2,256,512]{2,1,0:T(8,128)(2,1)} %copy-done.7, bf16[2,256,512]{2,1,0:T(8,128)(2,1)} %copy-done.8, bf16[256,1024]{1,0:T(8,128)(2,1)} %get-tuple-element.53.own_key_ref, ...), custom_call_target="tpu_custom_call", output_to_operand_aliasing={{0}: (2, {}), {1}: (3, {})} | custom-call | flops 1000000 | bytes 100000 | tf_op jit(solution)/shard_map/add_arrived/pallas_call | solution.py:256
  127.4 2.8 %all-to-all-done.4 = bf16[8,16,512]{2,1,0:T(8,128)(2,1)S(1)} async-done(((bf16[8,16,512]{2,1,0:T(8,128)(2,1)}), bf16[8,16,512]{2,1,0:T(8,128)(2,1)S(1)}, u32[]{:S(2)}, u32[]{:S(2)}) %all-to-all-start.4) | async-done | bytes 131104 | tf_op jit(solution)/shard_map/all_to_all | solution.py:283
  130.3 0.6 maximum_multiply_fusion
  (24 shorter events, 0.1 us)
Async XLA Ops:
  0.6 45.8 %copy-start = (bf16[1,2,128,1024]{3,2,1,0:T(8,128)(2,1)S(1)}, bf16[1,2,128,1024]{3,2,1,0:T(8,128)(2,1)}, u32[]{:S(2)}) copy-start(bf16[1,2,128,1024]{3,2,1,0:T(8,128)(2,1)} %param.12) | copy-start | bytes 1572868
  0.6 7.5 %copy-start.9 = (bf16[16,1024]{1,0:T(8,128)(2,1)S(1)}, bf16[16,1024]{1,0:T(8,128)(2,1)}, u32[]{:S(2)}) copy-start(bf16[16,1024]{1,0:T(8,128)(2,1)} %param.13) | copy-start | bytes 98308
  2.8 31.2 %collective-permute-start.2 = (bf16[2,256,512]{2,1,0:T(8,128)(2,1)}, bf16[2,256,512]{2,1,0:T(8,128)(2,1)S(1)}, u32[]{:S(2)}, u32[]{:S(2)}) collective-permute-start(bf16[2,256,512]{2,1,0:T(8,128)(2,1)} %pad_maximum_fusion.1), channel_id=1, source_target_pairs={{0,1},{1,2},{2,3},{3,4},{4,5},{5,6},{6,7},{7,8},{8,9},{9,10},{10,1... | collective-permute-start | bytes 1572872 | tf_op jit(solution)/shard_map/ppermute | solution.py:271
  6.9 27.2 %collective-permute-start.3 = (bf16[2,256,512]{2,1,0:T(8,128)(2,1)}, bf16[2,256,512]{2,1,0:T(8,128)(2,1)S(1)}, u32[]{:S(2)}, u32[]{:S(2)}) collective-permute-start(bf16[2,256,512]{2,1,0:T(8,128)(2,1)} %pad_maximum_fusion.1), channel_id=1, source_target_pairs={{1,0},{2,1},{3,2},{4,3},{5,4},{6,5},{7,6},{8,7},{9,8},{10,9},{11,1... | collective-permute-start | bytes 1572872 | tf_op jit(solution)/shard_map/ppermute | solution.py:271
  8.9 19.6 %all-to-all-start = ((bf16[16,16,512]{2,1,0:T(8,128)(2,1)}), bf16[16,16,512]{2,1,0:T(8,128)(2,1)S(1)}, u32[]{:S(2)}, u32[]{:S(2)}) async-start(bf16[16,16,512]{2,1,0:T(8,128)(2,1)} %broadcast_in_dim.8), calls=%async_computation | async-start | bytes 524288 | tf_op jit(solution)/shard_map/all_to_all | solution.py:283
  20.5 19.8 %collective-permute-start = (bf16[2,256,512]{2,1,0:T(8,128)(2,1)}, bf16[2,256,512]{2,1,0:T(8,128)(2,1)S(1)}, u32[]{:S(2)}, u32[]{:S(2)}) collective-permute-start(bf16[2,256,512]{2,1,0:T(8,128)(2,1)} %pad_maximum_fusion), channel_id=1, source_target_pairs={{0,1},{1,2},{2,3},{3,4},{4,5},{5,6},{6,7},{7,8},{8,9},{9,10},{10,1... | collective-permute-start | bytes 1572872 | tf_op jit(solution)/shard_map/ppermute | solution.py:271
  23.8 16.6 %collective-permute-start.1 = (bf16[2,256,512]{2,1,0:T(8,128)(2,1)}, bf16[2,256,512]{2,1,0:T(8,128)(2,1)}, u32[]{:S(2)}, u32[]{:S(2)}) collective-permute-start(bf16[2,256,512]{2,1,0:T(8,128)(2,1)} %pad_maximum_fusion), channel_id=1, source_target_pairs={{1,0},{2,1},{3,2},{4,3},{5,4},{6,5},{7,6},{8,7},{9,8},{10,9},{11,1... | collective-permute-start | bytes 1572872 | tf_op jit(solution)/shard_map/ppermute | solution.py:271
  29.7 25.5 %all-to-all-start.1 = ((bf16[4,256,512]{2,1,0:T(8,128)(2,1)}), bf16[4,256,512]{2,1,0:T(8,128)(2,1)S(1)}, u32[]{:S(2)}, u32[]{:S(2)}) async-start(bf16[4,256,512]{2,1,0:T(8,128)(2,1)} %broadcast_in_dim.10), calls=%async_computation.1 | async-start | bytes 2097152 | tf_op jit(solution)/shard_map/all_to_all | solution.py:315
  34.0 0.8 copy-start.2
  34.0 1.0 copy-start.3
  40.3 0.8 copy-start.4
  46.4 13.7 %copy-start.1 = (bf16[256,1024]{1,0:T(8,128)(2,1)S(1)}, bf16[256,1024]{1,0:T(8,128)(2,1)}, u32[]{:S(2)}) copy-start(bf16[256,1024]{1,0:T(8,128)(2,1)} %get-tuple-element.34.o_ref) | copy-start | bytes 1572868
  55.2 4.9 %collective-permute-start.5 = (bf16[1024,512]{1,0:T(8,128)(2,1)}, bf16[1024,512]{1,0:T(8,128)(2,1)S(1)}, u32[]{:S(2)}, u32[]{:S(2)}) collective-permute-start(bf16[1024,512]{1,0:T(8,128)(2,1)} %convolution_convert_fusion), channel_id=1, source_target_pairs={{0,64},{64,0},{1,65},{65,1},{2,66},{66,2},{3,67},{67,3},{4,68},{68... | collective-permute-start | bytes 3145736 | tf_op jit(solution)/shard_map/ppermute | solution.py:275
  57.6 8.2 %collective-permute-start.4 = (bf16[1024,512]{1,0:T(8,128)(2,1)S(1)}, bf16[1024,512]{1,0:T(8,128)(2,1)}, u32[]{:S(2)}, u32[]{:S(2)}) collective-permute-start(bf16[1024,512]{1,0:T(8,128)(2,1)S(1)} %bitcast.46), channel_id=1, source_target_pairs={{0,64},{64,0},{1,65},{65,1},{2,66},{66,2},{3,67},{67,3},{4,68},{68... | collective-permute-start | bytes 3145736 | tf_op jit(solution)/shard_map/ppermute | solution.py:275
  61.6 22.1 %all-to-all-start.2 = ((bf16[4,256,512]{2,1,0:T(8,128)(2,1)}), bf16[4,256,512]{2,1,0:T(8,128)(2,1)}, u32[]{:S(2)}, u32[]{:S(2)}) async-start(bf16[4,256,512]{2,1,0:T(8,128)(2,1)} %bitcast.12), calls=%async_computation.2 | async-start | bytes 2097152 | tf_op jit(solution)/shard_map/all_to_all | solution.py:289
  73.8 13.9 %collective-permute-start.6 = (bf16[2,256,512]{2,1,0:T(8,128)(2,1)}, bf16[2,256,512]{2,1,0:T(8,128)(2,1)S(1)}, u32[]{:S(2)}, u32[]{:S(2)}) collective-permute-start(bf16[2,256,512]{2,1,0:T(8,128)(2,1)} %get-tuple-element.43), channel_id=1, source_target_pairs={{0,1},{1,2},{2,3},{3,4},{4,5},{5,6},{6,7},{7,8},{8,9},{9,10},{10,1... | collective-permute-start | bytes 1572872 | tf_op jit(solution)/shard_map/ppermute | solution.py:271
  76.9 14.5 %collective-permute-start.7 = (bf16[2,256,512]{2,1,0:T(8,128)(2,1)}, bf16[2,256,512]{2,1,0:T(8,128)(2,1)S(1)}, u32[]{:S(2)}, u32[]{:S(2)}) collective-permute-start(bf16[2,256,512]{2,1,0:T(8,128)(2,1)} %get-tuple-element.44), channel_id=1, source_target_pairs={{1,0},{2,1},{3,2},{4,3},{5,4},{6,5},{7,6},{8,7},{9,8},{10,9},{11,1... | collective-permute-start | bytes 1572872 | tf_op jit(solution)/shard_map/ppermute | solution.py:271
  87.7 34.6 %copy-start.5 = (bf16[2,256,512]{2,1,0:T(8,128)(2,1)}, bf16[2,256,512]{2,1,0:T(8,128)(2,1)S(1)}, u32[]{:S(2)}) copy-start(bf16[2,256,512]{2,1,0:T(8,128)(2,1)S(1)} %collective-permute-done.6.below_ref) | copy-start | bytes 1572868
  91.4 30.8 %copy-start.6 = (bf16[2,256,512]{2,1,0:T(8,128)(2,1)}, bf16[2,256,512]{2,1,0:T(8,128)(2,1)S(1)}, u32[]{:S(2)}) copy-start(bf16[2,256,512]{2,1,0:T(8,128)(2,1)S(1)} %collective-permute-done.7.above_ref) | copy-start | bytes 1572868
  91.4 15.6 %all-to-all-start.3 = ((bf16[16,16,512]{2,1,0:T(8,128)(2,1)}), bf16[16,16,512]{2,1,0:T(8,128)(2,1)S(1)}, u32[]{:S(2)}, u32[]{:S(2)}) async-start(bf16[16,16,512]{2,1,0:T(8,128)(2,1)} %bitcast.15), calls=%async_computation.3 | async-start | bytes 524288 | tf_op jit(solution)/shard_map/all_to_all | solution.py:289
  99.3 25.1 %collective-permute-start.8 = (bf16[2,256,512]{2,1,0:T(8,128)(2,1)}, bf16[2,256,512]{2,1,0:T(8,128)(2,1)S(1)}, u32[]{:S(2)}, u32[]{:S(2)}) collective-permute-start(bf16[2,256,512]{2,1,0:T(8,128)(2,1)} %get-tuple-element.47), channel_id=1, source_target_pairs={{0,1},{1,2},{2,3},{3,4},{4,5},{5,6},{6,7},{7,8},{8,9},{9,10},{10,1... | collective-permute-start | bytes 1572872 | tf_op jit(solution)/shard_map/ppermute | solution.py:271
  102.6 21.8 %collective-permute-start.9 = (bf16[2,256,512]{2,1,0:T(8,128)(2,1)}, bf16[2,256,512]{2,1,0:T(8,128)(2,1)S(1)}, u32[]{:S(2)}, u32[]{:S(2)}) collective-permute-start(bf16[2,256,512]{2,1,0:T(8,128)(2,1)} %get-tuple-element.48), channel_id=1, source_target_pairs={{1,0},{2,1},{3,2},{4,3},{5,4},{6,5},{7,6},{8,7},{9,8},{10,9},{11,1... | collective-permute-start | bytes 1572872 | tf_op jit(solution)/shard_map/ppermute | solution.py:271
  107.7 22.5 %all-to-all-start.4 = ((bf16[8,16,512]{2,1,0:T(8,128)(2,1)}), bf16[8,16,512]{2,1,0:T(8,128)(2,1)S(1)}, u32[]{:S(2)}, u32[]{:S(2)}) async-start(bf16[8,16,512]{2,1,0:T(8,128)(2,1)} %broadcast_in_dim.22), calls=%async_computation.4 | async-start | bytes 262144 | tf_op jit(solution)/shard_map/all_to_all | solution.py:283
  124.4 0.8 copy-start.7
  124.4 1.0 copy-start.8

commit v5 on v4

--- a/solution.py
+++ b/solution.py
@@ -23,7 +23,7 @@
 BF = jnp.bfloat16
 F32 = jnp.float32
 VMEM_LIMIT = 60*1024*1024
-LARGE = pl.CostEstimate(flops=2*10**10, bytes_accessed=4*10**7, transcendentals=0)
+SUM_LIMIT = 8 * 1024 * 1024
 SMALL = pl.CostEstimate(flops=10**6, bytes_accessed=10**5, transcendentals=0)
 
 
@@ -121,9 +121,29 @@
 
 
 def backward_kernel(
-    q_ref, g_ref, o_ref, prob_ref, kp_ref, ko_ref, kn_ref, vp_ref, vo_ref, vn_ref, *refs,
+    q_ref, g_ref, o_ref, ko_ref, vo_ref,
+    prob0_ref, kp0_ref, kn0_ref, vp0_ref, vn0_ref,
+    prob1_ref, kp1_ref, kn1_ref, vp1_ref, vn1_ref,
+    dq_ref, own_key_ref, own_value_ref, low_ref, high_ref,
 ):
-    dq_ref, own_key_ref, own_value_ref, low_ref, high_ref = refs[-5:]
+    step, steps = pl.program_id(0), pl.num_programs(0)
+    shared = (q_ref, g_ref, o_ref, ko_ref, vo_ref)
+    outs = (dq_ref, own_key_ref, own_value_ref, low_ref, high_ref)
+
+    @pl.when(step < steps // HALVES)
+    def _():
+        backward_pairs(*shared, prob0_ref, kp0_ref, kn0_ref, vp0_ref, vn0_ref, *outs)
+
+    @pl.when(step >= steps // HALVES)
+    def _():
+        backward_pairs(*shared, prob1_ref, kp1_ref, kn1_ref, vp1_ref, vn1_ref, *outs)
+
+
+def backward_pairs(
+    q_ref, g_ref, o_ref, ko_ref, vo_ref,
+    prob_ref, kp_ref, kn_ref, vp_ref, vn_ref,
+    dq_ref, own_key_ref, own_value_ref, low_ref, high_ref,
+):
     cycles = prob_ref.shape[1]
     lon = prob_ref.shape[2] // SPAN
     units = [(pair, i) for pair in range(PPS) for i in range(cycles)]
@@ -188,8 +208,7 @@
     flat = pl.BlockSpec((rows, width), lambda p: (0, p + half * steps))
     key = pl.BlockSpec((1, rows, width), lambda p: (0, 0, p))
     value = pl.BlockSpec((1, rows, width), lambda p: (1, 0, p))
-    both = pl.BlockSpec((2, rows, width), lambda p: (0, 0, p))
-    return flat, key, value, both
+    return flat, key, value
 
 
 def forward(half, band, q, k, v, below, above, lon, previous):
@@ -198,7 +217,7 @@
     pairs = width // PAIR // HALVES
     steps = pairs // PPS
     smem = pl.BlockSpec(memory_space=pltpu.SMEM)
-    flat, key, value, _ = half_specs(rows, steps, half)
+    flat, key, value = half_specs(rows, steps, half)
     operands = [*band, q, below, k, above, below, v, above]
     specs = [smem] * len(band) + [flat, key, flat, key, value, flat, value]
     return pl.pallas_call(
@@ -213,33 +232,43 @@
         input_output_aliases={len(operands) + n: n for n in range(len(previous))},
         scratch_shapes=[pltpu.VMEM((cycles, SPAN * lon, lon), F32)],
         compiler_params=pltpu.CompilerParams(vmem_limit_bytes=VMEM_LIMIT),
-        cost_estimate=LARGE,
+        cost_estimate=SMALL,
         name="attention_forward",
     )(*operands, *previous)
 
 
-def backward(half, q, g, o, probs, k, v, below, above, lon, previous):
+def backward(q, g, o, probs, k, v, below, above, lon):
     rows, width = q.shape
     cycles = rows // lon
-    pairs = width // PAIR // HALVES
-    steps = pairs // PPS
-    flat, key, value, both = half_specs(rows, steps, half)
-    prob = pl.BlockSpec((PPS, cycles, SPAN * lon, 2 * lon), lambda p: (p, 0, 0, 0))
+    block = PPS * PAIR
+    steps = width // block
+    flat = pl.BlockSpec((rows, block), lambda p: (0, p))
+    both = pl.BlockSpec((2, rows, block), lambda p: (0, 0, p))
+    operands, specs = [q, g, o, k, v], [flat] * 5
+    for n in range(HALVES):
+
+        def place(p, n=n):
+            return jnp.clip(p - n * (steps // HALVES), 0, steps // HALVES - 1)
+
+        key = pl.BlockSpec((1, rows, block), lambda p, place=place: (0, 0, place(p)))
+        value = pl.BlockSpec((1, rows, block), lambda p, place=place: (1, 0, place(p)))
+        prob = pl.BlockSpec(
+            (PPS, cycles, SPAN * lon, 2 * lon), lambda p, place=place: (place(p), 0, 0, 0)
+        )
+        operands += [probs[n], below[n], above[n], below[n], above[n]]
+        specs += [prob, key, key, value, value]
     whole = jax.ShapeDtypeStruct((rows, width), BF)
-    edge = jax.ShapeDtypeStruct((2, rows, width // HALVES), BF)
-    operands = [q, g, o, probs, below, k, above, below, v, above]
-    specs = [flat, flat, flat, prob, key, flat, key, value, flat, value]
+    edge = jax.ShapeDtypeStruct((2, rows, width), BF)
     return pl.pallas_call(
         backward_kernel,
         grid=(steps,),
-        in_specs=specs + [pl.BlockSpec(memory_space=pl.ANY)] * len(previous),
+        in_specs=specs,
         out_specs=[flat, flat, flat, both, both],
         out_shape=[whole, whole, whole, edge, edge],
-        input_output_aliases={len(operands) + n: n for n in range(len(previous))},
         compiler_params=pltpu.CompilerParams(vmem_limit_bytes=VMEM_LIMIT),
         cost_estimate=SMALL,
         name="attention_backward",
-    )(*operands, *previous)
+    )(*operands)
 
 
 def total_kernel(below_ref, above_ref, own_key_ref, own_value_ref, key_ref, value_ref):
@@ -248,21 +277,42 @@
         out[...] = (own[...].astype(F32) + arrived).astype(BF)
 
 
-def add_arrived(half, own_key, own_value, from_below, from_above):
+def add_arrived(own_key, own_value, from_below, from_above):
     rows, width = own_key.shape
-    steps = width // HALVES // (PPS * PAIR)
-    flat, _, _, both = half_specs(rows, steps, half)
+    block = width // 2
+    flat = pl.BlockSpec((rows, block), lambda p: (0, p))
+    both = pl.BlockSpec((2, rows, block), lambda p: (0, 0, p))
     whole = jax.ShapeDtypeStruct((rows, width), BF)
     return pl.pallas_call(
         total_kernel,
-        grid=(steps,),
+        grid=(width // block,),
         in_specs=[both, both, flat, flat],
         out_specs=[flat, flat],
         out_shape=[whole, whole],
-        input_output_aliases={2: 0, 3: 1},
+        compiler_params=pltpu.CompilerParams(vmem_limit_bytes=SUM_LIMIT),
         cost_estimate=SMALL,
         name="add_arrived",
     )(from_below, from_above, own_key, own_value)
+
+
+def stack_kernel(k_ref, v_ref, out_ref):
+    out_ref[0] = k_ref[...]
+    out_ref[1] = v_ref[...]
+
+
+def stack_half(half, k, v):
+    rows, width = k.shape
+    flat = pl.BlockSpec((rows, width // HALVES), lambda p: (0, half))
+    return pl.pallas_call(
+        stack_kernel,
+        grid=(1,),
+        in_specs=[flat, flat],
+        out_specs=pl.BlockSpec((2, rows, width // HALVES), lambda p: (0, 0, 0)),
+        out_shape=jax.ShapeDtypeStruct((2, rows, width // HALVES), BF),
+        compiler_params=pltpu.CompilerParams(vmem_limit_bytes=VMEM_LIMIT),
+        cost_estimate=SMALL,
+        name="stack_half",
+    )(k, v)
 
 
 def lat_shift(value, by):
@@ -302,28 +352,24 @@
     core = lax.axis_index("core")
     mine, others = core * half_width, (1 - core) * half_width
 
-    parts = [
-        jnp.stack([k[:, n : n + width // HALVES], v[:, n : n + width // HALVES]])
-        for n in range(0, width, width // HALVES)
-    ]
+    parts = [stack_half(n, k, v) for n in range(HALVES)]
     below = [lat_shift(part, 1) for part in parts]
     above = [lat_shift(part, -1) for part in parts]
     proj = lax.dynamic_slice_in_dim(out_proj, mine, half_width, axis=1)
     proj = spread(proj, ZY).reshape(-1, half_width)
-    proj = copies_of(proj, "x")
-    proj, early_q = lax.optimization_barrier((proj, q))
-    proj = lax.all_to_all(proj, "x", 0, 0, tiled=True).reshape(-1, half_width)
-
     latitude = (np.arange(total, dtype=np.float32) + np.float32(0.5)) * np.float32(math.pi / total)
     logw = jnp.asarray(np.log(np.sin(latitude)).astype(np.float32))
     first = (lax.axis_index(LAT) * cycles).astype(jnp.int32).reshape(1)
     band = (first, cycle_lo, cycle_hi, lon_half, logw)
-    attended, probs = [], []
-    for n in range(HALVES):
-        out, prob = forward(n, band, early_q, k, v, below[n], above[n], lon, attended)
-        attended = [out]
-        probs.append(prob)
-    attended = attended[0]
+    attended, probs_first = forward(0, band, q, k, v, below[0], above[0], lon, [])
+    proj, attended = lax.optimization_barrier((proj, attended))
+    proj = copies_of(proj, "x")
+    proj, later_q = lax.optimization_barrier((proj, q))
+    proj = lax.all_to_all(proj, "x", 0, 0, tiled=True).reshape(-1, half_width)
+    attended, probs_second = forward(
+        1, band, later_q, k, v, below[1], above[1], lon, [attended]
+    )
+    probs = (probs_first, probs_second)
 
     grad_mine = lax.dynamic_slice_in_dim(grad_flat, mine, half_width, axis=1)
     grad_other = lax.dynamic_slice_in_dim(grad_flat, others, half_width, axis=1)
@@ -334,27 +380,20 @@
     partial = (dot(attended, grad_mine, ((0,), (0,))) + received.astype(F32)).astype(BF)
     attn_grad = dot(grad_mine, proj, ((1,), (1,))) + dot(grad_other, proj_other, ((1,), (1,)))
     attn_grad = attn_grad.astype(BF)
-    whole, edges = [], []
-    for n in range(HALVES):
-        *whole, low, high = backward(
-            n, q, attn_grad, attended, probs[n], k, v, below[n], above[n], lon, whole
-        )
-        edges.append((low, high))
-    query_grad, key_grad, value_grad = whole
-
+    query_grad, own_key, own_value, low, high = backward(
+        q, attn_grad, attended, probs, k, v, below, above, lon
+    )
     partial = scatter_sum(partial, "x").astype(BF)
-    arrived = [(lat_shift(edges[0][1], 1), lat_shift(edges[0][0], -1))]
-    partial, arrived[0], edges[1] = lax.optimization_barrier((partial, arrived[0], edges[1]))
+    partial, low, high = lax.optimization_barrier((partial, low, high))
     partial = scatter_sum(partial, ZY).astype(BF)
-    arrived.append((lat_shift(edges[1][1], 1), lat_shift(edges[1][0], -1)))
+    from_below, from_above = lat_shift(high, 1), lat_shift(low, -1)
     samples = lax.axis_size(DP)
     gathered = spread(partial, DP).reshape((samples // 2, 2) + partial.shape)
     summed = jnp.sum(gathered.astype(F32), axis=0)
     scaling = 1.0 / math.sqrt(samples * total * lon)
     proj_grad = jnp.concatenate([summed[0], summed[1]], axis=1) * scaling
 
-    for n, (from_below, from_above) in enumerate(arrived):
-        key_grad, value_grad = add_arrived(n, key_grad, value_grad, from_below, from_above)
+    key_grad, value_grad = add_arrived(own_key, own_value, from_below, from_above)
     shape = query_feats.shape
     return (
         query_grad.reshape(shape),

time: 132 us -> 135 us (1.023)
  blocking collectives: 0 us -> 34.5 us
  starting transfers between devices: 64.9 us -> 45.4 us
  waiting for transfers between devices: 21.4 us -> 13.3 us
  other arithmetic: 4.55 us -> 1.61 us
    all_to_all x0 -> x1, blocking collectives: none -> 34.5 us  [spread(): return lax.all_to_all(copies_of(value, axes), axes, 0, 0, tiled=True)]
    all_to_all x2 -> x1, starting transfers between devices: 25.2 us -> 9.52 us  [spread(): return lax.all_to_all(copies_of(value, axes), axes, 0, 0, tiled=True)]
    all_to_all x2 -> x1, waiting for transfers between devices: 6.28 us -> 0.01 us  [spread(): return lax.all_to_all(copies_of(value, axes), axes, 0, 0, tiled=True)]
    ppermute x8 -> x6, waiting for transfers between devices: 5.56 us -> 0.02 us  [lat_shift(): return lax.ppermute(value, LAT, pairs)]
    all_to_all x2, starting transfers between devices: 12.1 us -> 7.05 us  [scatter_sum(): received = lax.all_to_all(blocks, axes, 0, 0, tiled=True)]
    ppermute x8 -> x6, starting transfers between devices: 18.9 us -> 15.8 us  [lat_shift(): return lax.ppermute(value, LAT, pairs)]
    all_to_all x1, starting transfers between devices: 4.32 us -> 6.73 us  [local(): proj = lax.all_to_all(proj, 'x', 0, 0, tiled=True).reshape(-1, half_width)]
    all_to_all x2, waiting for transfers between devices: 3.16 us -> 5.21 us  [scatter_sum(): received = lax.all_to_all(blocks, axes, 0, 0, tiled=True)]
  transfers between devices with their start and end apart: 15 -> 12, of which waited for: 7 -> 4; matrix products, arithmetic and copies ran while one was open for 10% -> 8% of each run, Pallas kernels for 20% -> 17%
where the time goes in v5:
time: 135 us
  starting transfers between devices  45.4 us (34%)
  blocking collectives  34.5 us (26%)
  Pallas kernels  25.5 us (19%)
  waiting for transfers between devices  13.3 us (10%)
  matrix products  7.06 us (5%)
  local copies, waits for them, and re-layouts  6.24 us (5%)
  other arithmetic  1.61 us (1%)
    all_to_all x1, blocking collectives, spread(): return lax.all_to_all(copies_of(value, axes), axes, 0, 0, tiled=True)  34.5 us
    ppermute x6, starting transfers between devices, lat_shift(): return lax.ppermute(value, LAT, pairs)  15.8 us
    pallas_call x2, Pallas kernels, forward(): pl.pallas_call(forward_kernel, grid=(steps,), in_specs=specs + [pl.BlockS...  10.5 us
    pallas_call x1, Pallas kernels, backward(): pl.pallas_call(backward_kernel, grid=(steps,), in_specs=specs, out_specs=...  9.9 us
    all_to_all x1, starting transfers between devices, spread(): return lax.all_to_all(copies_of(value, axes), axes, 0, 0, tiled=True)  9.52 us
    all_to_all x1, waiting for transfers between devices, local(): proj = lax.all_to_all(proj, 'x', 0, 0, tiled=True).reshape(-1, half_width)  7.56 us
    dot_general x4, matrix products, dot(): return lax.dot_general(a, b, (dims, ((), ())), preferred_element_type=F32)  7.06 us
    all_to_all x2, starting transfers between devices, scatter_sum(): received = lax.all_to_all(blocks, axes, 0, 0, tiled=True)  7.05 us
  transfers between devices with their start and end apart: 12, of which 4 were waited for; matrix products, arithmetic and copies ran while one was open for 8% of the time, Pallas kernels for 17%

profile of v5, /device:TPU:1, one launch (start us, length us, event | category | flops | bytes accessed | tf_op | source)
XLA Modules:
  0.0 134.5 jit_solution(12021891248355484003)
XLA Ops:
  0.6 0.0 copy-start
  0.6 1.9 %stack_half.2 = bf16[2,256,512]{2,1,0:T(8,128)(2,1)} custom-call(bf16[256,1024]{1,0:T(8,128)(2,1)} %bitcast.26, bf16[256,1024]{1,0:T(8,128)(2,1)} %bitcast.31), custom_call_target="tpu_custom_call" | custom-call | flops 1000000 | bytes 100000 | tf_op jit(solution)/shard_map/stack_half/pallas_call | solution.py:306
  2.6 1.3 collective-permute-start.1
  3.8 4.7 %collective-permute-start = (bf16[2,256,512]{2,1,0:T(8,128)(2,1)}, bf16[2,256,512]{2,1,0:T(8,128)(2,1)S(1)}, u32[]{:S(2)}, u32[]{:S(2)}) collective-permute-start(bf16[2,256,512]{2,1,0:T(8,128)(2,1)} %stack_half.2), channel_id=1, source_target_pairs={{0,1},{1,2},{2,3},{3,4},{4,5},{5,6},{6,7},{7,8},{8,9},{9,10},{10,1... | collective-permute-start | bytes 1572872 | tf_op jit(solution)/shard_map/ppermute | solution.py:321
  8.6 0.7 constant_dynamic-slice_fusion
  9.3 0.7 broadcast_in_dim.6
  10.0 9.5 %all-to-all-start = ((bf16[16,16,512]{2,1,0:T(8,128)(2,1)}), bf16[16,16,512]{2,1,0:T(8,128)(2,1)S(1)}, u32[]{:S(2)}, u32[]{:S(2)}) async-start(bf16[16,16,512]{2,1,0:T(8,128)(2,1)} %broadcast_in_dim.6), calls=%async_computation | async-start | bytes 524288 | tf_op jit(solution)/shard_map/all_to_all | solution.py:333
  19.5 1.9 %stack_half.3 = bf16[2,256,512]{2,1,0:T(8,128)(2,1)} custom-call(bf16[256,1024]{1,0:T(8,128)(2,1)} %bitcast.27, bf16[256,1024]{1,0:T(8,128)(2,1)} %bitcast.32), custom_call_target="tpu_custom_call" | custom-call | flops 1000000 | bytes 100000 | tf_op jit(solution)/shard_map/stack_half/pallas_call | solution.py:306
  21.4 1.3 collective-permute-start.3
  22.7 4.0 %collective-permute-start.2 = (bf16[2,256,512]{2,1,0:T(8,128)(2,1)}, bf16[2,256,512]{2,1,0:T(8,128)(2,1)S(1)}, u32[]{:S(2)}, u32[]{:S(2)}) collective-permute-start(bf16[2,256,512]{2,1,0:T(8,128)(2,1)} %stack_half.3), channel_id=1, source_target_pairs={{0,1},{1,2},{2,3},{3,4},{4,5},{5,6},{6,7},{7,8},{8,9},{9,10},{10,1... | collective-permute-start | bytes 1572872 | tf_op jit(solution)/shard_map/ppermute | solution.py:321
  26.7 0.0 collective-permute-done.1.kn_ref.vn_ref.kn0_ref.vn0_ref
  26.7 0.0 collective-permute-done.kp_ref.vp_ref.kp0_ref.vp0_ref
  26.8 0.8 copy-done.3
  27.5 0.2 copy-done.4
  27.8 5.3 %attention_forward.2 = (bf16[256,1024]{1,0:T(8,128)(2,1)}, bf16[4,2,640,256]{3,2,1,0:T(8,128)(2,1)}) custom-call(s32[1]{0:T(128)} %bitcast.3.first_ref, s32[128]{0:T(128)} %lo_ref.3, s32[128]{0:T(128)} %hi_ref.3, s32[128]{0:T(128)} %half_ref.3, f32[128]{0:T(128)} %constant.41.clone.logw_ref, bf16[256,1024]{1,0:T(8,128)(2,1)} %bitcast.36, ...), custom_call_target="tpu_custom_call" | custom-call | flops 1000000 | bytes 100000 | tf_op jit(solution)/shard_map/attention_forward/pallas_call | solution.py:223
  33.1 0.0 all-to-all-done
  33.1 1.1 broadcast_in_dim.7
  34.2 6.7 %all-to-all-start.1 = ((bf16[4,256,512]{2,1,0:T(8,128)(2,1)}), bf16[4,256,512]{2,1,0:T(8,128)(2,1)}, u32[]{:S(2)}, u32[]{:S(2)}) async-start(bf16[4,256,512]{2,1,0:T(8,128)(2,1)} %broadcast_in_dim.7), calls=%async_computation.1 | async-start | bytes 2097152 | tf_op jit(solution)/shard_map/all_to_all | solution.py:368
  40.9 0.0 collective-permute-done.3.kn_ref.vn_ref.kn1_ref.vn1_ref
  40.9 0.0 collective-permute-done.2.kp_ref.vp_ref.kp1_ref.vp1_ref
  40.9 0.8 copy-done.5
  41.7 0.8 copy-done.6
  42.5 5.3 %attention_forward.3 = (bf16[256,1024]{1,0:T(8,128)(2,1)}, bf16[4,2,640,256]{3,2,1,0:T(8,128)(2,1)}) custom-call(s32[1]{0:T(128)} %bitcast.3.first_ref, s32[128]{0:T(128)} %lo_ref.3, s32[128]{0:T(128)} %hi_ref.3, s32[128]{0:T(128)} %half_ref.3, f32[128]{0:T(128)} %constant.41.clone.logw_ref, ...), custom_call_target="tpu_custom_call", output_to_operand_aliasing={{0}: (12, {})} | custom-call | flops 1000000 | bytes 100000 | tf_op jit(solution)/shard_map/attention_forward/pallas_call | solution.py:223
  47.7 0.0 copy-done
  47.7 0.0 copy-start.7
  47.8 2.6 %convolution_convert_fusion = bf16[1024,512]{1,0:T(8,128)(2,1)} fusion(bf16[256,1024]{1,0:T(8,128)(2,1)} %get-tuple-element.29.o_ref, bf16[256,1024]{1,0:T(8,128)(2,1)S(1)} %bitcast.23, s32[]{:T(128)S(6)} %select_n.8), kind=kOutput, calls=%fused_computation.1 | convolution fusion | flops 268959744 | bytes 1835012 | tf_op jit(solution)/shard_map/dot_general | solution.py:31
  50.4 7.6 %all-to-all-done.1 = bf16[4,256,512]{2,1,0:T(8,128)(2,1)} async-done(((bf16[4,256,512]{2,1,0:T(8,128)(2,1)}), bf16[4,256,512]{2,1,0:T(8,128)(2,1)}, u32[]{:S(2)}, u32[]{:S(2)}) %all-to-all-start.1) | async-done | bytes 1048608 | tf_op jit(solution)/shard_map/all_to_all | solution.py:368
  57.9 4.4 %collective-permute-start.5 = (bf16[1024,512]{1,0:T(8,128)(2,1)}, bf16[1024,512]{1,0:T(8,128)(2,1)S(1)}, u32[]{:S(2)}, u32[]{:S(2)}) collective-permute-start(bf16[1024,512]{1,0:T(8,128)(2,1)} %convolution_convert_fusion), channel_id=1, source_target_pairs={{0,64},{64,0},{1,65},{65,1},{2,66},{66,2},{3,67},{67,3},{4,68},{68... | collective-permute-start | bytes 3145736 | tf_op jit(solution)/shard_map/ppermute | solution.py:325
  62.3 1.9 %collective-permute-start.4 = (bf16[1024,512]{1,0:T(8,128)(2,1)}, bf16[1024,512]{1,0:T(8,128)(2,1)S(1)}, u32[]{:S(2)}, u32[]{:S(2)}) collective-permute-start(bf16[1024,512]{1,0:T(8,128)(2,1)} %bitcast.6), channel_id=1, source_target_pairs={{0,64},{64,0},{1,65},{65,1},{2,66},{66,2},{3,67},{67,3},{4,68},{68... | collective-permute-start | bytes 3145736 | tf_op jit(solution)/shard_map/ppermute | solution.py:325
  64.3 0.5 collective-permute-done.5
  64.8 1.5 %add_convert_fusion = bf16[1024,512]{1,0:T(8,128)(2,1)} fusion(bf16[1024,512]{1,0:T(8,128)(2,1)S(1)} %collective-permute-done.5, bf16[256,1024]{1,0:T(8,128)(2,1)S(1)} %copy-done.7, bf16[256,1024]{1,0:T(8,128)(2,1)S(1)} %bitcast.25, s32[]{:T(128)S(6)} %select_n.7), kind=kOutput, calls=%fused_computation | convolution fusion | flops 270008320 | bytes 2883588 | tf_op jit(solution)/shard_map/dot_general | solution.py:31
  66.3 3.5 %all-to-all-start.2 = ((bf16[4,256,512]{2,1,0:T(8,128)(2,1)}), bf16[4,256,512]{2,1,0:T(8,128)(2,1)S(1)}, u32[]{:S(2)}, u32[]{:S(2)}) async-start(bf16[4,256,512]{2,1,0:T(8,128)(2,1)} %bitcast.8), calls=%async_computation.2 | async-start | bytes 2097152 | tf_op jit(solution)/shard_map/all_to_all | solution.py:339
  69.8 1.7 %fusion.4 = f32[256,1024]{1,0:T(8,128)S(1)} fusion(bf16[1024,512]{1,0:T(8,128)(2,1)} %bitcast.6, bf16[256,1024]{1,0:T(8,128)(2,1)S(1)} %bitcast.22, s32[]{:T(128)S(6)} %select_n.7), kind=kOutput, calls=%fused_computation.8 | convolution fusion | flops 268435456 | bytes 2359300 | tf_op jit(solution)/shard_map/dot_general | solution.py:31
  71.5 0.0 collective-permute-done.4
  71.5 1.3 fusion.g_ref
  72.8 9.9 %attention_backward.1 = (bf16[256,1024]{1,0:T(8,128)(2,1)}, bf16[256,1024]{1,0:T(8,128)(2,1)}, bf16[256,1024]{1,0:T(8,128)(2,1)}, bf16[2,256,1024]{2,1,0:T(8,128)(2,1)}, bf16[2,256,1024]{2,1,0:T(8,128)(2,1)}) custom-call(bf16[256,1024]{1,0:T(8,128)(2,1)} %bitcast.38, bf16[256,1024]{1,0:T(8,128)(2,1)} %fusion.g_ref, ...), custom_call_target="tpu_custom_call" | custom-call | flops 1000000 | bytes 100000 | tf_op jit(solution)/shard_map/attention_backward/pallas_call | solution.py:262
  82.7 1.9 %all-to-all-done.2 = bf16[4,256,512]{2,1,0:T(8,128)(2,1)S(1)} async-done(((bf16[4,256,512]{2,1,0:T(8,128)(2,1)}), bf16[4,256,512]{2,1,0:T(8,128)(2,1)S(1)}, u32[]{:S(2)}, u32[]{:S(2)}) %all-to-all-start.2) | async-done | bytes 1048608 | tf_op jit(solution)/shard_map/all_to_all | solution.py:339
  84.6 0.9 reduce_sum.33
  85.5 3.5 %all-to-all-start.3 = ((bf16[16,16,512]{2,1,0:T(8,128)(2,1)}), bf16[16,16,512]{2,1,0:T(8,128)(2,1)S(1)}, u32[]{:S(2)}, u32[]{:S(2)}) async-start(bf16[16,16,512]{2,1,0:T(8,128)(2,1)} %bitcast.11), calls=%async_computation.3 | async-start | bytes 524288 | tf_op jit(solution)/shard_map/all_to_all | solution.py:339
  89.1 3.2 %collective-permute-start.6 = (bf16[2,256,1024]{2,1,0:T(8,128)(2,1)}, bf16[2,256,1024]{2,1,0:T(8,128)(2,1)S(1)}, u32[]{:S(2)}, u32[]{:S(2)}) collective-permute-start(bf16[2,256,1024]{2,1,0:T(8,128)(2,1)} %get-tuple-element.37), channel_id=1, source_target_pairs={{0,1},{1,2},{2,3},{3,4},{4,5},{5,6},{6,7},{7,8},{8,9},{9,10},{10,1... | collective-permute-start | bytes 3145736 | tf_op jit(solution)/shard_map/ppermute | solution.py:321
  92.3 1.3 collective-permute-start.7
  93.6 3.3 %all-to-all-done.3 = bf16[16,16,512]{2,1,0:T(8,128)(2,1)S(1)} async-done(((bf16[16,16,512]{2,1,0:T(8,128)(2,1)}), bf16[16,16,512]{2,1,0:T(8,128)(2,1)S(1)}, u32[]{:S(2)}, u32[]{:S(2)}) %all-to-all-start.3) | async-done | bytes 262176 | tf_op jit(solution)/shard_map/all_to_all | solution.py:339
  96.9 34.5 %all_to_all.25 = bf16[8,16,512]{2,1,0:T(8,128)(2,1)S(1)} all-to-all(bf16[8,16,512]{2,1,0:T(8,128)(2,1)S(1)} %broadcast_in_dim.8), channel_id=1, replica_groups=mesh['zh'=4,'core'=2,'x'=4,'zl'=2,'y'=8] {'zh','core'}, dimensions={0} | all-to-all | bytes 262144 | tf_op jit(solution)/shard_map/all_to_all | solution.py:333
  131.5 0.6 maximum_multiply_fusion
  132.1 0.0 collective-permute-done.6.below_ref
  132.1 0.0 collective-permute-done.7.above_ref
  132.1 1.0 copy-done.2
  133.2 1.4 %add_arrived.1 = (bf16[256,1024]{1,0:T(8,128)(2,1)}, bf16[256,1024]{1,0:T(8,128)(2,1)}) custom-call(bf16[2,256,1024]{2,1,0:T(8,128)(2,1)S(1)} %collective-permute-done.6.below_ref, bf16[2,256,1024]{2,1,0:T(8,128)(2,1)S(1)} %collective-permute-done.7.above_ref, bf16[256,1024]{1,0:T(8,128)(2,1)S(1)} %copy-done.1, bf16[256,1024]{1,0:T(8,128)(2,1)S(1)} %copy-done.2), custom_call_target="tpu_custom_call" | custom-call | flops 1000000 | bytes 100000 | tf_op jit(solution)/shard_map/add_arrived/pallas_call | solution.py:286
  (12 shorter events, 0.1 us)
Async XLA Ops:
  0.6 47.1 %copy-start = (bf16[1,2,128,1024]{3,2,1,0:T(8,128)(2,1)S(1)}, bf16[1,2,128,1024]{3,2,1,0:T(8,128)(2,1)}, u32[]{:S(2)}) copy-start(bf16[1,2,128,1024]{3,2,1,0:T(8,128)(2,1)} %param.12) | copy-start | bytes 1572868
  2.6 24.2 %collective-permute-start.1 = (bf16[2,256,512]{2,1,0:T(8,128)(2,1)}, bf16[2,256,512]{2,1,0:T(8,128)(2,1)S(1)}, u32[]{:S(2)}, u32[]{:S(2)}) collective-permute-start(bf16[2,256,512]{2,1,0:T(8,128)(2,1)} %stack_half.2), channel_id=1, source_target_pairs={{1,0},{2,1},{3,2},{4,3},{5,4},{6,5},{7,6},{8,7},{9,8},{10,9},{11,1... | collective-permute-start | bytes 1572872 | tf_op jit(solution)/shard_map/ppermute | solution.py:321
  3.8 22.9 %collective-permute-start = (bf16[2,256,512]{2,1,0:T(8,128)(2,1)}, bf16[2,256,512]{2,1,0:T(8,128)(2,1)S(1)}, u32[]{:S(2)}, u32[]{:S(2)}) collective-permute-start(bf16[2,256,512]{2,1,0:T(8,128)(2,1)} %stack_half.2), channel_id=1, source_target_pairs={{0,1},{1,2},{2,3},{3,4},{4,5},{5,6},{6,7},{7,8},{8,9},{9,10},{10,1... | collective-permute-start | bytes 1572872 | tf_op jit(solution)/shard_map/ppermute | solution.py:321
  10.0 23.0 %all-to-all-start = ((bf16[16,16,512]{2,1,0:T(8,128)(2,1)}), bf16[16,16,512]{2,1,0:T(8,128)(2,1)S(1)}, u32[]{:S(2)}, u32[]{:S(2)}) async-start(bf16[16,16,512]{2,1,0:T(8,128)(2,1)} %broadcast_in_dim.6), calls=%async_computation | async-start | bytes 524288 | tf_op jit(solution)/shard_map/all_to_all | solution.py:333
  21.4 19.5 %collective-permute-start.3 = (bf16[2,256,512]{2,1,0:T(8,128)(2,1)}, bf16[2,256,512]{2,1,0:T(8,128)(2,1)S(1)}, u32[]{:S(2)}, u32[]{:S(2)}) collective-permute-start(bf16[2,256,512]{2,1,0:T(8,128)(2,1)} %stack_half.3), channel_id=1, source_target_pairs={{1,0},{2,1},{3,2},{4,3},{5,4},{6,5},{7,6},{8,7},{9,8},{10,9},{11,1... | collective-permute-start | bytes 1572872 | tf_op jit(solution)/shard_map/ppermute | solution.py:321
  22.7 18.2 %collective-permute-start.2 = (bf16[2,256,512]{2,1,0:T(8,128)(2,1)}, bf16[2,256,512]{2,1,0:T(8,128)(2,1)S(1)}, u32[]{:S(2)}, u32[]{:S(2)}) collective-permute-start(bf16[2,256,512]{2,1,0:T(8,128)(2,1)} %stack_half.3), channel_id=1, source_target_pairs={{0,1},{1,2},{2,3},{3,4},{4,5},{5,6},{6,7},{7,8},{8,9},{9,10},{10,1... | collective-permute-start | bytes 1572872 | tf_op jit(solution)/shard_map/ppermute | solution.py:321
  26.7 0.8 copy-start.3
  26.7 1.0 copy-start.4
  34.2 23.8 %all-to-all-start.1 = ((bf16[4,256,512]{2,1,0:T(8,128)(2,1)}), bf16[4,256,512]{2,1,0:T(8,128)(2,1)}, u32[]{:S(2)}, u32[]{:S(2)}) async-start(bf16[4,256,512]{2,1,0:T(8,128)(2,1)} %broadcast_in_dim.7), calls=%async_computation.1 | async-start | bytes 2097152 | tf_op jit(solution)/shard_map/all_to_all | solution.py:368
  40.9 0.8 copy-start.5
  41.7 0.8 copy-start.6
  47.7 17.1 %copy-start.7 = (bf16[256,1024]{1,0:T(8,128)(2,1)S(1)}, bf16[256,1024]{1,0:T(8,128)(2,1)}, u32[]{:S(2)}) copy-start(bf16[256,1024]{1,0:T(8,128)(2,1)} %get-tuple-element.29.o_ref) | copy-start | bytes 1572868
  57.9 6.9 %collective-permute-start.5 = (bf16[1024,512]{1,0:T(8,128)(2,1)}, bf16[1024,512]{1,0:T(8,128)(2,1)S(1)}, u32[]{:S(2)}, u32[]{:S(2)}) collective-permute-start(bf16[1024,512]{1,0:T(8,128)(2,1)} %convolution_convert_fusion), channel_id=1, source_target_pairs={{0,64},{64,0},{1,65},{65,1},{2,66},{66,2},{3,67},{67,3},{4,68},{68... | collective-permute-start | bytes 3145736 | tf_op jit(solution)/shard_map/ppermute | solution.py:325
  62.3 9.2 %collective-permute-start.4 = (bf16[1024,512]{1,0:T(8,128)(2,1)}, bf16[1024,512]{1,0:T(8,128)(2,1)S(1)}, u32[]{:S(2)}, u32[]{:S(2)}) collective-permute-start(bf16[1024,512]{1,0:T(8,128)(2,1)} %bitcast.6), channel_id=1, source_target_pairs={{0,64},{64,0},{1,65},{65,1},{2,66},{66,2},{3,67},{67,3},{4,68},{68... | collective-permute-start | bytes 3145736 | tf_op jit(solution)/shard_map/ppermute | solution.py:325
  66.3 18.3 %all-to-all-start.2 = ((bf16[4,256,512]{2,1,0:T(8,128)(2,1)}), bf16[4,256,512]{2,1,0:T(8,128)(2,1)S(1)}, u32[]{:S(2)}, u32[]{:S(2)}) async-start(bf16[4,256,512]{2,1,0:T(8,128)(2,1)} %bitcast.8), calls=%async_computation.2 | async-start | bytes 2097152 | tf_op jit(solution)/shard_map/all_to_all | solution.py:339
  82.7 49.4 %copy-start.1 = (bf16[256,1024]{1,0:T(8,128)(2,1)S(1)}, bf16[256,1024]{1,0:T(8,128)(2,1)}, u32[]{:S(2)}) copy-start(bf16[256,1024]{1,0:T(8,128)(2,1)} %get-tuple-element.39.own_key_ref) | copy-start | bytes 1572868
  85.5 11.4 %all-to-all-start.3 = ((bf16[16,16,512]{2,1,0:T(8,128)(2,1)}), bf16[16,16,512]{2,1,0:T(8,128)(2,1)S(1)}, u32[]{:S(2)}, u32[]{:S(2)}) async-start(bf16[16,16,512]{2,1,0:T(8,128)(2,1)} %bitcast.11), calls=%async_computation.3 | async-start | bytes 524288 | tf_op jit(solution)/shard_map/all_to_all | solution.py:339
  89.1 43.0 %collective-permute-start.6 = (bf16[2,256,1024]{2,1,0:T(8,128)(2,1)}, bf16[2,256,1024]{2,1,0:T(8,128)(2,1)S(1)}, u32[]{:S(2)}, u32[]{:S(2)}) collective-permute-start(bf16[2,256,1024]{2,1,0:T(8,128)(2,1)} %get-tuple-element.37), channel_id=1, source_target_pairs={{0,1},{1,2},{2,3},{3,4},{4,5},{5,6},{6,7},{7,8},{8,9},{9,10},{10,1... | collective-permute-start | bytes 3145736 | tf_op jit(solution)/shard_map/ppermute | solution.py:321
  92.3 39.8 %collective-permute-start.7 = (bf16[2,256,1024]{2,1,0:T(8,128)(2,1)}, bf16[2,256,1024]{2,1,0:T(8,128)(2,1)S(1)}, u32[]{:S(2)}, u32[]{:S(2)}) collective-permute-start(bf16[2,256,1024]{2,1,0:T(8,128)(2,1)} %get-tuple-element.38), channel_id=1, source_target_pairs={{1,0},{2,1},{3,2},{4,3},{5,4},{6,5},{7,6},{8,7},{9,8},{10,9},{11,1... | collective-permute-start | bytes 3145736 | tf_op jit(solution)/shard_map/ppermute | solution.py:321
  132.1 1.0 copy-start.2

commit v6 on v5

--- a/solution.py
+++ b/solution.py
@@ -24,6 +24,7 @@
 F32 = jnp.float32
 VMEM_LIMIT = 60*1024*1024
 SUM_LIMIT = 8 * 1024 * 1024
+LARGE = pl.CostEstimate(flops=2*10**10, bytes_accessed=4*10**7, transcendentals=0)
 SMALL = pl.CostEstimate(flops=10**6, bytes_accessed=10**5, transcendentals=0)
 
 
@@ -232,7 +233,7 @@
         input_output_aliases={len(operands) + n: n for n in range(len(previous))},
         scratch_shapes=[pltpu.VMEM((cycles, SPAN * lon, lon), F32)],
         compiler_params=pltpu.CompilerParams(vmem_limit_bytes=VMEM_LIMIT),
-        cost_estimate=SMALL,
+        cost_estimate=LARGE,
         name="attention_forward",
     )(*operands, *previous)
 
@@ -357,19 +358,20 @@
     above = [lat_shift(part, -1) for part in parts]
     proj = lax.dynamic_slice_in_dim(out_proj, mine, half_width, axis=1)
     proj = spread(proj, ZY).reshape(-1, half_width)
+    proj = copies_of(proj, "x")
+    proj, early_q = lax.optimization_barrier((proj, q))
+    proj = lax.all_to_all(proj, "x", 0, 0, tiled=True).reshape(-1, half_width)
+
     latitude = (np.arange(total, dtype=np.float32) + np.float32(0.5)) * np.float32(math.pi / total)
     logw = jnp.asarray(np.log(np.sin(latitude)).astype(np.float32))
     first = (lax.axis_index(LAT) * cycles).astype(jnp.int32).reshape(1)
     band = (first, cycle_lo, cycle_hi, lon_half, logw)
-    attended, probs_first = forward(0, band, q, k, v, below[0], above[0], lon, [])
-    proj, attended = lax.optimization_barrier((proj, attended))
-    proj = copies_of(proj, "x")
-    proj, later_q = lax.optimization_barrier((proj, q))
-    proj = lax.all_to_all(proj, "x", 0, 0, tiled=True).reshape(-1, half_width)
-    attended, probs_second = forward(
-        1, band, later_q, k, v, below[1], above[1], lon, [attended]
-    )
-    probs = (probs_first, probs_second)
+    attended, probs = [], []
+    for n in range(HALVES):
+        out, prob = forward(n, band, early_q, k, v, below[n], above[n], lon, attended)
+        attended = [out]
+        probs.append(prob)
+    attended = attended[0]
 
     grad_mine = lax.dynamic_slice_in_dim(grad_flat, mine, half_width, axis=1)
     grad_other = lax.dynamic_slice_in_dim(grad_flat, others, half_width, axis=1)
@@ -384,7 +386,6 @@
         q, attn_grad, attended, probs, k, v, below, above, lon
     )
     partial = scatter_sum(partial, "x").astype(BF)
-    partial, low, high = lax.optimization_barrier((partial, low, high))
     partial = scatter_sum(partial, ZY).astype(BF)
     from_below, from_above = lat_shift(high, 1), lat_shift(low, -1)
     samples = lax.axis_size(DP)

time: 135 us -> 142 us (1.052)
  the two profiles are of different devices: /device:TPU:1 before, /device:TPU:42 now
where the time goes in v6:
time: 142 us; the launch traced here: 141 us
  starting transfers between devices  50.7 us (36%)
  blocking collectives  39.1 us (28%)
  Pallas kernels  25.6 us (18%)
  waiting for transfers between devices  9.78 us (7%)
  local copies, waits for them, and re-layouts  6 us (4%)
  matrix products  5.81 us (4%)
  other arithmetic  3.11 us (2%)
    all_to_all x1, blocking collectives, scatter_sum(): received = lax.all_to_all(blocks, axes, 0, 0, tiled=True)  39.1 us
    all_to_all x2, starting transfers between devices, spread(): return lax.all_to_all(copies_of(value, axes), axes, 0, 0, tiled=True)  19 us
    ppermute x6, starting transfers between devices, lat_shift(): return lax.ppermute(value, LAT, pairs)  17.8 us
    pallas_call x2, Pallas kernels, forward(): pl.pallas_call(forward_kernel, grid=(steps,), in_specs=specs + [pl.BlockS...  10.5 us
    pallas_call x1, Pallas kernels, backward(): pl.pallas_call(backward_kernel, grid=(steps,), in_specs=specs, out_specs=...  9.94 us
    all_to_all x2, waiting for transfers between devices, spread(): return lax.all_to_all(copies_of(value, axes), axes, 0, 0, tiled=True)  9.33 us
    dot_general x4, matrix products, dot(): return lax.dot_general(a, b, (dims, ((), ())), preferred_element_type=F32)  5.81 us
    all_to_all x1, starting transfers between devices, local(): proj = lax.all_to_all(proj, 'x', 0, 0, tiled=True).reshape(-1, half_width)  4.82 us
  transfers between devices with their start and end apart: 12, of which 3 were waited for; matrix products, arithmetic and copies ran while one was open for 8% of the time, Pallas kernels for 17%

profile of v6, /device:TPU:42, one launch (start us, length us, event | category | flops | bytes accessed | tf_op | source)
XLA Modules:
  0.0 141.0 jit_solution(8952465725118647491)
XLA Ops:
  0.6 0.0 copy-start
  0.6 1.9 %stack_half.3 = bf16[2,256,512]{2,1,0:T(8,128)(2,1)} custom-call(bf16[256,1024]{1,0:T(8,128)(2,1)} %bitcast.26, bf16[256,1024]{1,0:T(8,128)(2,1)} %bitcast.31), custom_call_target="tpu_custom_call" | custom-call | flops 1000000 | bytes 100000 | tf_op jit(solution)/shard_map/stack_half/pallas_call | solution.py:307
  2.6 3.2 %collective-permute-start.3 = (bf16[2,256,512]{2,1,0:T(8,128)(2,1)}, bf16[2,256,512]{2,1,0:T(8,128)(2,1)S(1)}, u32[]{:S(2)}, u32[]{:S(2)}) collective-permute-start(bf16[2,256,512]{2,1,0:T(8,128)(2,1)} %stack_half.3), channel_id=1, source_target_pairs={{1,0},{2,1},{3,2},{4,3},{5,4},{6,5},{7,6},{8,7},{9,8},{10,9},{11,1... | collective-permute-start | bytes 1572872 | tf_op jit(solution)/shard_map/ppermute | solution.py:322
  5.8 2.6 %collective-permute-start.2 = (bf16[2,256,512]{2,1,0:T(8,128)(2,1)}, bf16[2,256,512]{2,1,0:T(8,128)(2,1)S(1)}, u32[]{:S(2)}, u32[]{:S(2)}) collective-permute-start(bf16[2,256,512]{2,1,0:T(8,128)(2,1)} %stack_half.3), channel_id=1, source_target_pairs={{0,1},{1,2},{2,3},{3,4},{4,5},{5,6},{6,7},{7,8},{8,9},{9,10},{10,1... | collective-permute-start | bytes 1572872 | tf_op jit(solution)/shard_map/ppermute | solution.py:322
  8.4 0.7 constant_dynamic-slice_fusion
  9.1 0.7 broadcast_in_dim.8
  9.9 9.6 %all-to-all-start = ((bf16[16,16,512]{2,1,0:T(8,128)(2,1)}), bf16[16,16,512]{2,1,0:T(8,128)(2,1)S(1)}, u32[]{:S(2)}, u32[]{:S(2)}) async-start(bf16[16,16,512]{2,1,0:T(8,128)(2,1)} %broadcast_in_dim.8), calls=%async_computation | async-start | bytes 524288 | tf_op jit(solution)/shard_map/all_to_all | solution.py:334
  19.4 1.9 %stack_half.2 = bf16[2,256,512]{2,1,0:T(8,128)(2,1)} custom-call(bf16[256,1024]{1,0:T(8,128)(2,1)} %bitcast.27, bf16[256,1024]{1,0:T(8,128)(2,1)} %bitcast.32), custom_call_target="tpu_custom_call" | custom-call | flops 1000000 | bytes 100000 | tf_op jit(solution)/shard_map/stack_half/pallas_call | solution.py:307
  21.3 3.4 %collective-permute-start.1 = (bf16[2,256,512]{2,1,0:T(8,128)(2,1)}, bf16[2,256,512]{2,1,0:T(8,128)(2,1)S(1)}, u32[]{:S(2)}, u32[]{:S(2)}) collective-permute-start(bf16[2,256,512]{2,1,0:T(8,128)(2,1)} %stack_half.2), channel_id=1, source_target_pairs={{1,0},{2,1},{3,2},{4,3},{5,4},{6,5},{7,6},{8,7},{9,8},{10,9},{11,1... | collective-permute-start | bytes 1572872 | tf_op jit(solution)/shard_map/ppermute | solution.py:322
  24.7 2.5 %collective-permute-start = (bf16[2,256,512]{2,1,0:T(8,128)(2,1)}, bf16[2,256,512]{2,1,0:T(8,128)(2,1)}, u32[]{:S(2)}, u32[]{:S(2)}) collective-permute-start(bf16[2,256,512]{2,1,0:T(8,128)(2,1)} %stack_half.2), channel_id=1, source_target_pairs={{0,1},{1,2},{2,3},{3,4},{4,5},{5,6},{6,7},{7,8},{8,9},{9,10},{10,1... | collective-permute-start | bytes 1572872 | tf_op jit(solution)/shard_map/ppermute | solution.py:322
  27.2 1.8 %all-to-all-done = bf16[16,16,512]{2,1,0:T(8,128)(2,1)S(1)} async-done(((bf16[16,16,512]{2,1,0:T(8,128)(2,1)}), bf16[16,16,512]{2,1,0:T(8,128)(2,1)S(1)}, u32[]{:S(2)}, u32[]{:S(2)}) %all-to-all-start) | async-done | bytes 262176 | tf_op jit(solution)/shard_map/all_to_all | solution.py:334
  29.0 1.1 broadcast_in_dim.10
  30.1 4.8 %all-to-all-start.1 = ((bf16[4,256,512]{2,1,0:T(8,128)(2,1)}), bf16[4,256,512]{2,1,0:T(8,128)(2,1)S(1)}, u32[]{:S(2)}, u32[]{:S(2)}) async-start(bf16[4,256,512]{2,1,0:T(8,128)(2,1)} %broadcast_in_dim.10), calls=%async_computation.1 | async-start | bytes 2097152 | tf_op jit(solution)/shard_map/all_to_all | solution.py:363
  34.9 0.0 collective-permute-done.3.kn_ref.vn_ref.kn0_ref.vn0_ref
  34.9 0.0 collective-permute-done.2.kp_ref.vp_ref.kp0_ref.vp0_ref
  34.9 0.8 copy-done.4
  35.7 0.2 copy-done.5
  35.9 5.2 %attention_forward.2 = (bf16[256,1024]{1,0:T(8,128)(2,1)}, bf16[4,2,640,256]{3,2,1,0:T(8,128)(2,1)}) custom-call(s32[1]{0:T(128)} %bitcast.4.first_ref, s32[128]{0:T(128)} %lo_ref.3, s32[128]{0:T(128)} %hi_ref.3, s32[128]{0:T(128)} %half_ref.3, f32[128]{0:T(128)} %constant.41.clone.logw_ref, bf16[256,1024]{1,0:T(8,128)(2,1)} %bitcast.40, ...), custom_call_target="tpu_custom_call" | custom-call | flops 20000000000 | bytes 40000000 | tf_op jit(solution)/shard_map/attention_forward/pallas_call | solution.py:224
  41.1 0.0 collective-permute-done.1.kn_ref.vn_ref.kn1_ref.vn1_ref
  41.1 0.0 copy-start.6
  41.1 0.0 collective-permute-done.kp_ref.vp_ref.kp1_ref.vp1_ref
  41.1 0.8 copy-done.6
  41.9 5.3 %attention_forward.3 = (bf16[256,1024]{1,0:T(8,128)(2,1)}, bf16[4,2,640,256]{3,2,1,0:T(8,128)(2,1)}) custom-call(s32[1]{0:T(128)} %bitcast.4.first_ref, s32[128]{0:T(128)} %lo_ref.3, s32[128]{0:T(128)} %hi_ref.3, s32[128]{0:T(128)} %half_ref.3, f32[128]{0:T(128)} %constant.41.clone.logw_ref, ...), custom_call_target="tpu_custom_call", output_to_operand_aliasing={{0}: (12, {})} | custom-call | flops 20000000000 | bytes 40000000 | tf_op jit(solution)/shard_map/attention_forward/pallas_call | solution.py:224
  47.2 2.6 %convolution_convert_fusion = bf16[1024,512]{1,0:T(8,128)(2,1)} fusion(bf16[256,1024]{1,0:T(8,128)(2,1)} %get-tuple-element.22.o_ref, bf16[256,1024]{1,0:T(8,128)(2,1)S(1)} %bitcast.23, s32[]{:T(128)S(6)} %select_n.8), kind=kOutput, calls=%fused_computation.1 | convolution fusion | flops 268959744 | bytes 1835012 | tf_op jit(solution)/shard_map/dot_general | solution.py:32
  49.7 0.0 all-to-all-done.1
  49.7 1.9 %collective-permute-start.7 = (bf16[1024,512]{1,0:T(8,128)(2,1)}, bf16[1024,512]{1,0:T(8,128)(2,1)S(1)}, u32[]{:S(2)}, u32[]{:S(2)}) collective-permute-start(bf16[1024,512]{1,0:T(8,128)(2,1)} %convolution_convert_fusion), channel_id=1, source_target_pairs={{0,64},{64,0},{1,65},{65,1},{2,66},{66,2},{3,67},{67,3},{4,68},{68... | collective-permute-start | bytes 3145736 | tf_op jit(solution)/shard_map/ppermute | solution.py:326
  51.7 2.4 %collective-permute-start.4 = (bf16[1024,512]{1,0:T(8,128)(2,1)S(1)}, bf16[1024,512]{1,0:T(8,128)(2,1)S(1)}, u32[]{:S(2)}, u32[]{:S(2)}) collective-permute-start(bf16[1024,512]{1,0:T(8,128)(2,1)S(1)} %bitcast.36), channel_id=1, source_target_pairs={{0,64},{64,0},{1,65},{65,1},{2,66},{66,2},{3,67},{67,3},{4,68},{68... | collective-permute-start | bytes 3145736 | tf_op jit(solution)/shard_map/ppermute | solution.py:326
  54.1 0.4 collective-permute-done.7
  54.5 1.5 %add_convert_fusion = bf16[1024,512]{1,0:T(8,128)(2,1)} fusion(bf16[1024,512]{1,0:T(8,128)(2,1)S(1)} %collective-permute-done.7, bf16[256,1024]{1,0:T(8,128)(2,1)S(1)} %copy-done.3, bf16[256,1024]{1,0:T(8,128)(2,1)S(1)} %bitcast.25, s32[]{:T(128)S(6)} %select_n.7), kind=kOutput, calls=%fused_computation | convolution fusion | flops 270008320 | bytes 2883588 | tf_op jit(solution)/shard_map/dot_general | solution.py:32
  56.0 4.8 %all-to-all-start.2 = ((bf16[4,256,512]{2,1,0:T(8,128)(2,1)}), bf16[4,256,512]{2,1,0:T(8,128)(2,1)}, u32[]{:S(2)}, u32[]{:S(2)}) async-start(bf16[4,256,512]{2,1,0:T(8,128)(2,1)} %bitcast.10), calls=%async_computation.2 | async-start | bytes 2097152 | tf_op jit(solution)/shard_map/all_to_all | solution.py:340
  60.8 0.5 fusion.4
  61.3 0.0 collective-permute-done.4
  61.3 1.3 fusion.g_ref
  62.6 9.9 %attention_backward.1 = (bf16[256,1024]{1,0:T(8,128)(2,1)}, bf16[256,1024]{1,0:T(8,128)(2,1)}, bf16[256,1024]{1,0:T(8,128)(2,1)}, bf16[2,256,1024]{2,1,0:T(8,128)(2,1)}, bf16[2,256,1024]{2,1,0:T(8,128)(2,1)}) custom-call(bf16[256,1024]{1,0:T(8,128)(2,1)} %bitcast.42, bf16[256,1024]{1,0:T(8,128)(2,1)} %fusion.g_ref, ...), custom_call_target="tpu_custom_call" | custom-call | flops 1000000 | bytes 100000 | tf_op jit(solution)/shard_map/attention_backward/pallas_call | solution.py:263
  72.5 4.2 %collective-permute-start.5 = (bf16[2,256,1024]{2,1,0:T(8,128)(2,1)}, bf16[2,256,1024]{2,1,0:T(8,128)(2,1)S(1)}, u32[]{:S(2)}, u32[]{:S(2)}) collective-permute-start(bf16[2,256,1024]{2,1,0:T(8,128)(2,1)} %get-tuple-element.27), channel_id=1, source_target_pairs={{0,1},{1,2},{2,3},{3,4},{4,5},{5,6},{6,7},{7,8},{8,9},{9,10},{10,1... | collective-permute-start | bytes 3145736 | tf_op jit(solution)/shard_map/ppermute | solution.py:322
  76.8 1.9 %collective-permute-start.6 = (bf16[2,256,1024]{2,1,0:T(8,128)(2,1)}, bf16[2,256,1024]{2,1,0:T(8,128)(2,1)S(1)}, u32[]{:S(2)}, u32[]{:S(2)}) collective-permute-start(bf16[2,256,1024]{2,1,0:T(8,128)(2,1)} %get-tuple-element.28), channel_id=1, source_target_pairs={{1,0},{2,1},{3,2},{4,3},{5,4},{6,5},{7,6},{8,7},{9,8},{10,9},{11,1... | collective-permute-start | bytes 3145736 | tf_op jit(solution)/shard_map/ppermute | solution.py:322
  78.7 0.0 all-to-all-done.2
  78.7 1.5 %reduce_sum.33 = bf16[256,512]{1,0:T(8,128)(2,1)S(1)} reduce(bf16[4,256,512]{2,1,0:T(8,128)(2,1)} %all-to-all-done.2, bf16[]{:T(256)} %constant.38.clone.1), dimensions={0}, to_apply=%region_0.0 | reduce | flops 393216 | bytes 1310722 | tf_op jit(solution)/shard_map/reduce_sum | solution.py:341
  80.2 39.1 %all_to_all.25 = bf16[16,16,512]{2,1,0:T(8,128)(2,1)} all-to-all(bf16[16,16,512]{2,1,0:T(8,128)(2,1)S(1)} %bitcast.39), channel_id=1, replica_groups=mesh['zh'=4,'core'=2,'x'=4,'zl'=2,'y'=8] {'zl','y'}, dimensions={0} | all-to-all | bytes 524288 | tf_op jit(solution)/shard_map/all_to_all | solution.py:340
  119.3 1.0 reduce_sum.34
  120.3 0.7 broadcast_in_dim.22
  120.9 9.4 %all-to-all-start.4 = ((bf16[8,16,512]{2,1,0:T(8,128)(2,1)}), bf16[8,16,512]{2,1,0:T(8,128)(2,1)S(1)}, u32[]{:S(2)}, u32[]{:S(2)}) async-start(bf16[8,16,512]{2,1,0:T(8,128)(2,1)} %broadcast_in_dim.22), calls=%async_computation.4 | async-start | bytes 262144 | tf_op jit(solution)/shard_map/all_to_all | solution.py:334
  130.3 0.0 collective-permute-done.5.below_ref
  130.3 0.0 collective-permute-done.6.above_ref
  130.4 1.0 copy-done.2
  131.4 1.4 add_arrived.1
  132.8 7.5 %all-to-all-done.4 = bf16[8,16,512]{2,1,0:T(8,128)(2,1)S(1)} async-done(((bf16[8,16,512]{2,1,0:T(8,128)(2,1)}), bf16[8,16,512]{2,1,0:T(8,128)(2,1)S(1)}, u32[]{:S(2)}, u32[]{:S(2)}) %all-to-all-start.4) | async-done | bytes 131104 | tf_op jit(solution)/shard_map/all_to_all | solution.py:334
  140.3 0.6 maximum_multiply_fusion
  (10 shorter events, 0.0 us)
Async XLA Ops:
  0.6 46.5 %copy-start = (bf16[1,2,128,1024]{3,2,1,0:T(8,128)(2,1)S(1)}, bf16[1,2,128,1024]{3,2,1,0:T(8,128)(2,1)}, u32[]{:S(2)}) copy-start(bf16[1,2,128,1024]{3,2,1,0:T(8,128)(2,1)} %param.12) | copy-start | bytes 1572868
  2.6 32.3 %collective-permute-start.3 = (bf16[2,256,512]{2,1,0:T(8,128)(2,1)}, bf16[2,256,512]{2,1,0:T(8,128)(2,1)S(1)}, u32[]{:S(2)}, u32[]{:S(2)}) collective-permute-start(bf16[2,256,512]{2,1,0:T(8,128)(2,1)} %stack_half.3), channel_id=1, source_target_pairs={{1,0},{2,1},{3,2},{4,3},{5,4},{6,5},{7,6},{8,7},{9,8},{10,9},{11,1... | collective-permute-start | bytes 1572872 | tf_op jit(solution)/shard_map/ppermute | solution.py:322
  5.8 29.1 %collective-permute-start.2 = (bf16[2,256,512]{2,1,0:T(8,128)(2,1)}, bf16[2,256,512]{2,1,0:T(8,128)(2,1)S(1)}, u32[]{:S(2)}, u32[]{:S(2)}) collective-permute-start(bf16[2,256,512]{2,1,0:T(8,128)(2,1)} %stack_half.3), channel_id=1, source_target_pairs={{0,1},{1,2},{2,3},{3,4},{4,5},{5,6},{6,7},{7,8},{8,9},{9,10},{10,1... | collective-permute-start | bytes 1572872 | tf_op jit(solution)/shard_map/ppermute | solution.py:322
  9.9 19.1 %all-to-all-start = ((bf16[16,16,512]{2,1,0:T(8,128)(2,1)}), bf16[16,16,512]{2,1,0:T(8,128)(2,1)S(1)}, u32[]{:S(2)}, u32[]{:S(2)}) async-start(bf16[16,16,512]{2,1,0:T(8,128)(2,1)} %broadcast_in_dim.8), calls=%async_computation | async-start | bytes 524288 | tf_op jit(solution)/shard_map/all_to_all | solution.py:334
  21.3 19.8 %collective-permute-start.1 = (bf16[2,256,512]{2,1,0:T(8,128)(2,1)}, bf16[2,256,512]{2,1,0:T(8,128)(2,1)S(1)}, u32[]{:S(2)}, u32[]{:S(2)}) collective-permute-start(bf16[2,256,512]{2,1,0:T(8,128)(2,1)} %stack_half.2), channel_id=1, source_target_pairs={{1,0},{2,1},{3,2},{4,3},{5,4},{6,5},{7,6},{8,7},{9,8},{10,9},{11,1... | collective-permute-start | bytes 1572872 | tf_op jit(solution)/shard_map/ppermute | solution.py:322
  24.7 16.5 %collective-permute-start = (bf16[2,256,512]{2,1,0:T(8,128)(2,1)}, bf16[2,256,512]{2,1,0:T(8,128)(2,1)}, u32[]{:S(2)}, u32[]{:S(2)}) collective-permute-start(bf16[2,256,512]{2,1,0:T(8,128)(2,1)} %stack_half.2), channel_id=1, source_target_pairs={{0,1},{1,2},{2,3},{3,4},{4,5},{5,6},{6,7},{7,8},{8,9},{9,10},{10,1... | collective-permute-start | bytes 1572872 | tf_op jit(solution)/shard_map/ppermute | solution.py:322
  30.1 19.7 %all-to-all-start.1 = ((bf16[4,256,512]{2,1,0:T(8,128)(2,1)}), bf16[4,256,512]{2,1,0:T(8,128)(2,1)S(1)}, u32[]{:S(2)}, u32[]{:S(2)}) async-start(bf16[4,256,512]{2,1,0:T(8,128)(2,1)} %broadcast_in_dim.10), calls=%async_computation.1 | async-start | bytes 2097152 | tf_op jit(solution)/shard_map/all_to_all | solution.py:363
  34.9 0.8 copy-start.4
  34.9 1.0 copy-start.5
  41.1 0.8 copy-start.6
  47.2 7.3 %copy-start.3 = (bf16[256,1024]{1,0:T(8,128)(2,1)S(1)}, bf16[256,1024]{1,0:T(8,128)(2,1)}, u32[]{:S(2)}) copy-start(bf16[256,1024]{1,0:T(8,128)(2,1)} %get-tuple-element.22.o_ref) | copy-start | bytes 1572868
  49.7 4.8 %collective-permute-start.7 = (bf16[1024,512]{1,0:T(8,128)(2,1)}, bf16[1024,512]{1,0:T(8,128)(2,1)S(1)}, u32[]{:S(2)}, u32[]{:S(2)}) collective-permute-start(bf16[1024,512]{1,0:T(8,128)(2,1)} %convolution_convert_fusion), channel_id=1, source_target_pairs={{0,64},{64,0},{1,65},{65,1},{2,66},{66,2},{3,67},{67,3},{4,68},{68... | collective-permute-start | bytes 3145736 | tf_op jit(solution)/shard_map/ppermute | solution.py:326
  51.7 9.6 %collective-permute-start.4 = (bf16[1024,512]{1,0:T(8,128)(2,1)S(1)}, bf16[1024,512]{1,0:T(8,128)(2,1)S(1)}, u32[]{:S(2)}, u32[]{:S(2)}) collective-permute-start(bf16[1024,512]{1,0:T(8,128)(2,1)S(1)} %bitcast.36), channel_id=1, source_target_pairs={{0,64},{64,0},{1,65},{65,1},{2,66},{66,2},{3,67},{67,3},{4,68},{68... | collective-permute-start | bytes 3145736 | tf_op jit(solution)/shard_map/ppermute | solution.py:326
  56.0 22.7 %all-to-all-start.2 = ((bf16[4,256,512]{2,1,0:T(8,128)(2,1)}), bf16[4,256,512]{2,1,0:T(8,128)(2,1)}, u32[]{:S(2)}, u32[]{:S(2)}) async-start(bf16[4,256,512]{2,1,0:T(8,128)(2,1)} %bitcast.10), calls=%async_computation.2 | async-start | bytes 2097152 | tf_op jit(solution)/shard_map/all_to_all | solution.py:340
  72.5 57.8 %copy-start.1 = (bf16[256,1024]{1,0:T(8,128)(2,1)S(1)}, bf16[256,1024]{1,0:T(8,128)(2,1)}, u32[]{:S(2)}) copy-start(bf16[256,1024]{1,0:T(8,128)(2,1)} %get-tuple-element.29.own_key_ref) | copy-start | bytes 1572868
  72.5 57.8 %collective-permute-start.5 = (bf16[2,256,1024]{2,1,0:T(8,128)(2,1)}, bf16[2,256,1024]{2,1,0:T(8,128)(2,1)S(1)}, u32[]{:S(2)}, u32[]{:S(2)}) collective-permute-start(bf16[2,256,1024]{2,1,0:T(8,128)(2,1)} %get-tuple-element.27), channel_id=1, source_target_pairs={{0,1},{1,2},{2,3},{3,4},{4,5},{5,6},{6,7},{7,8},{8,9},{9,10},{10,1... | collective-permute-start | bytes 3145736 | tf_op jit(solution)/shard_map/ppermute | solution.py:322
  76.8 53.6 %collective-permute-start.6 = (bf16[2,256,1024]{2,1,0:T(8,128)(2,1)}, bf16[2,256,1024]{2,1,0:T(8,128)(2,1)S(1)}, u32[]{:S(2)}, u32[]{:S(2)}) collective-permute-start(bf16[2,256,1024]{2,1,0:T(8,128)(2,1)} %get-tuple-element.28), channel_id=1, source_target_pairs={{1,0},{2,1},{3,2},{4,3},{5,4},{6,5},{7,6},{8,7},{9,8},{10,9},{11,1... | collective-permute-start | bytes 3145736 | tf_op jit(solution)/shard_map/ppermute | solution.py:322
  120.9 19.3 %all-to-all-start.4 = ((bf16[8,16,512]{2,1,0:T(8,128)(2,1)}), bf16[8,16,512]{2,1,0:T(8,128)(2,1)S(1)}, u32[]{:S(2)}, u32[]{:S(2)}) async-start(bf16[8,16,512]{2,1,0:T(8,128)(2,1)} %broadcast_in_dim.22), calls=%async_computation.4 | async-start | bytes 262144 | tf_op jit(solution)/shard_map/all_to_all | solution.py:334
  130.4 1.0 copy-start.2

commit v7 on v4

--- a/solution.py
+++ b/solution.py
@@ -328,7 +328,6 @@
     grad_mine = lax.dynamic_slice_in_dim(grad_flat, mine, half_width, axis=1)
     grad_other = lax.dynamic_slice_in_dim(grad_flat, others, half_width, axis=1)
     sent = dot(attended, grad_other, ((0,), (0,))).astype(BF)
-    proj, sent = lax.optimization_barrier((proj, sent))
     received = core_swap(sent)
     proj_other = core_swap(proj)
     partial = (dot(attended, grad_mine, ((0,), (0,))) + received.astype(F32)).astype(BF)
@@ -344,8 +343,9 @@
 
     partial = scatter_sum(partial, "x").astype(BF)
     arrived = [(lat_shift(edges[0][1], 1), lat_shift(edges[0][0], -1))]
-    partial, arrived[0], edges[1] = lax.optimization_barrier((partial, arrived[0], edges[1]))
+    partial, edges[1] = lax.optimization_barrier((partial, edges[1]))
     partial = scatter_sum(partial, ZY).astype(BF)
+    partial, arrived[0] = lax.optimization_barrier((partial, arrived[0]))
     arrived.append((lat_shift(edges[1][1], 1), lat_shift(edges[1][0], -1)))
     samples = lax.axis_size(DP)
     gathered = spread(partial, DP).reshape((samples // 2, 2) + partial.shape)

time: 132 us -> 123 us (0.932)
  waiting for transfers between devices: 21.4 us -> 10.3 us
  starting transfers between devices: 64.9 us -> 68.2 us
    ppermute x8, waiting for transfers between devices: 5.56 us -> 0.02 us  [lat_shift(): return lax.ppermute(value, LAT, pairs)]
    all_to_all x1, waiting for transfers between devices: 6.29 us -> 0.8 us  [local(): proj = lax.all_to_all(proj, 'x', 0, 0, tiled=True).reshape(-1, half_width)]
    ppermute x2, starting transfers between devices: 4.32 us -> 7.82 us  [core_swap(): return lax.ppermute(value, 'core', [(0, 1), (1, 0)])]
    ppermute x8, starting transfers between devices: 18.9 us -> 21.9 us  [lat_shift(): return lax.ppermute(value, LAT, pairs)]
    all_to_all x2, starting transfers between devices: 12.1 us -> 9.18 us  [scatter_sum(): received = lax.all_to_all(blocks, axes, 0, 0, tiled=True)]
  transfers between devices with their start and end apart: 15 -> 15, of which waited for: 7 -> 4; matrix products, arithmetic and copies ran while one was open for 10% -> 9% of each run, Pallas kernels for 20% -> 21%
where the time goes in v7:
time: 123 us; the launch traced here: 122 us
  starting transfers between devices  68.2 us (55%)
  Pallas kernels  25.7 us (21%)
  waiting for transfers between devices  10.3 us (8%)
  matrix products  7.1 us (6%)
  local copies, waits for them, and re-layouts  6.59 us (5%)
  other arithmetic  3.29 us (3%)
    all_to_all x2, starting transfers between devices, spread(): return lax.all_to_all(copies_of(value, axes), axes, 0, 0, tiled=True)  25 us
    ppermute x8, starting transfers between devices, lat_shift(): return lax.ppermute(value, LAT, pairs)  21.9 us
    pallas_call x2, Pallas kernels, backward(): pl.pallas_call(backward_kernel, grid=(steps,), in_specs=specs + [pl.Block...  10.9 us
    pallas_call x2, Pallas kernels, forward(): pl.pallas_call(forward_kernel, grid=(steps,), in_specs=specs + [pl.BlockS...  10.6 us
    all_to_all x2, starting transfers between devices, scatter_sum(): received = lax.all_to_all(blocks, axes, 0, 0, tiled=True)  9.18 us
    ppermute x2, starting transfers between devices, core_swap(): return lax.ppermute(value, 'core', [(0, 1), (1, 0)])  7.82 us
    dot_general x4, matrix products, dot(): return lax.dot_general(a, b, (dims, ((), ())), preferred_element_type=F32)  7.1 us
    all_to_all x2, waiting for transfers between devices, spread(): return lax.all_to_all(copies_of(value, axes), axes, 0, 0, tiled=True)  6.26 us
  transfers between devices with their start and end apart: 15, of which 4 were waited for; matrix products, arithmetic and copies ran while one was open for 9% of the time, Pallas kernels for 21%

profile of v7, /device:TPU:1, one launch (start us, length us, event | category | flops | bytes accessed | tf_op | source)
XLA Modules:
  0.0 122.2 jit_solution(1717081671486157774)
XLA Ops:
  0.6 0.0 copy-start
  0.7 1.3 %slice_bitcast_fusion = (bf16[1,256,512]{2,1,0:T(8,128)(2,1)S(1)}, bf16[1,256,512]{2,1,0:T(8,128)(2,1)S(1)}, bf16[1,256,512]{2,1,0:T(8,128)(2,1)S(1)}, bf16[1,256,512]{2,1,0:T(8,128)(2,1)S(1)}) fusion(bf16[256,1024]{1,0:T(8,128)(2,1)} %bitcast.34, bf16[256,1024]{1,0:T(8,128)(2,1)} %bitcast.39), kind=kLoop, calls=%fused_computation.6 | loop fusion | bytes 2097152 | tf_op jit(solution)/shard_map/stack | solution.py:306
  2.0 0.8 pad_maximum_fusion.1
  2.8 4.0 %collective-permute-start.3 = (bf16[2,256,512]{2,1,0:T(8,128)(2,1)}, bf16[2,256,512]{2,1,0:T(8,128)(2,1)S(1)}, u32[]{:S(2)}, u32[]{:S(2)}) collective-permute-start(bf16[2,256,512]{2,1,0:T(8,128)(2,1)} %pad_maximum_fusion.1), channel_id=1, source_target_pairs={{0,1},{1,2},{2,3},{3,4},{4,5},{5,6},{6,7},{7,8},{8,9},{9,10},{10,1... | collective-permute-start | bytes 1572872 | tf_op jit(solution)/shard_map/ppermute | solution.py:271
  6.9 1.3 %collective-permute-start.4 = (bf16[2,256,512]{2,1,0:T(8,128)(2,1)}, bf16[2,256,512]{2,1,0:T(8,128)(2,1)S(1)}, u32[]{:S(2)}, u32[]{:S(2)}) collective-permute-start(bf16[2,256,512]{2,1,0:T(8,128)(2,1)} %pad_maximum_fusion.1), channel_id=1, source_target_pairs={{1,0},{2,1},{3,2},{4,3},{5,4},{6,5},{7,6},{8,7},{9,8},{10,9},{11,1... | collective-permute-start | bytes 1572872 | tf_op jit(solution)/shard_map/ppermute | solution.py:271
  8.2 0.7 broadcast_in_dim.8
  8.9 10.7 %all-to-all-start = ((bf16[16,16,512]{2,1,0:T(8,128)(2,1)}), bf16[16,16,512]{2,1,0:T(8,128)(2,1)S(1)}, u32[]{:S(2)}, u32[]{:S(2)}) async-start(bf16[16,16,512]{2,1,0:T(8,128)(2,1)} %broadcast_in_dim.8), calls=%async_computation | async-start | bytes 524288 | tf_op jit(solution)/shard_map/all_to_all | solution.py:283
  19.7 0.8 pad_maximum_fusion
  20.5 3.3 %collective-permute-start.1 = (bf16[2,256,512]{2,1,0:T(8,128)(2,1)}, bf16[2,256,512]{2,1,0:T(8,128)(2,1)S(1)}, u32[]{:S(2)}, u32[]{:S(2)}) collective-permute-start(bf16[2,256,512]{2,1,0:T(8,128)(2,1)} %pad_maximum_fusion), channel_id=1, source_target_pairs={{0,1},{1,2},{2,3},{3,4},{4,5},{5,6},{6,7},{7,8},{8,9},{9,10},{10,1... | collective-permute-start | bytes 1572872 | tf_op jit(solution)/shard_map/ppermute | solution.py:271
  23.8 1.3 %collective-permute-start.2 = (bf16[2,256,512]{2,1,0:T(8,128)(2,1)}, bf16[2,256,512]{2,1,0:T(8,128)(2,1)}, u32[]{:S(2)}, u32[]{:S(2)}) collective-permute-start(bf16[2,256,512]{2,1,0:T(8,128)(2,1)} %pad_maximum_fusion), channel_id=1, source_target_pairs={{1,0},{2,1},{3,2},{4,3},{5,4},{6,5},{7,6},{8,7},{9,8},{10,9},{11,1... | collective-permute-start | bytes 1572872 | tf_op jit(solution)/shard_map/ppermute | solution.py:271
  25.1 3.5 %all-to-all-done = bf16[16,16,512]{2,1,0:T(8,128)(2,1)S(1)} async-done(((bf16[16,16,512]{2,1,0:T(8,128)(2,1)}), bf16[16,16,512]{2,1,0:T(8,128)(2,1)S(1)}, u32[]{:S(2)}, u32[]{:S(2)}) %all-to-all-start) | async-done | bytes 262176 | tf_op jit(solution)/shard_map/all_to_all | solution.py:283
  28.6 1.1 broadcast_in_dim.10
  29.6 4.3 %all-to-all-start.1 = ((bf16[4,256,512]{2,1,0:T(8,128)(2,1)}), bf16[4,256,512]{2,1,0:T(8,128)(2,1)S(1)}, u32[]{:S(2)}, u32[]{:S(2)}) async-start(bf16[4,256,512]{2,1,0:T(8,128)(2,1)} %broadcast_in_dim.10), calls=%async_computation.1 | async-start | bytes 2097152 | tf_op jit(solution)/shard_map/all_to_all | solution.py:315
  34.0 0.0 collective-permute-done.3.kp_ref.vp_ref
  34.0 0.8 copy-done.2
  34.7 0.2 copy-done.3
  35.0 5.3 %attention_forward.2 = (bf16[256,1024]{1,0:T(8,128)(2,1)}, bf16[4,2,640,256]{3,2,1,0:T(8,128)(2,1)}) custom-call(s32[1]{0:T(128)} %bitcast.4.first_ref, s32[128]{0:T(128)} %lo_ref.3, s32[128]{0:T(128)} %hi_ref.3, s32[128]{0:T(128)} %half_ref.3, f32[128]{0:T(128)} %constant.41.clone.logw_ref, bf16[256,1024]{1,0:T(8,128)(2,1)} %bitcast.48, ...), custom_call_target="tpu_custom_call" | custom-call | flops 20000000000 | bytes 40000000 | tf_op jit(solution)/shard_map/attention_forward/pallas_call | solution.py:204
  40.2 0.0 collective-permute-done.1.kp_ref.vp_ref
  40.2 0.0 collective-permute-done.2.kn_ref.vn_ref
  40.2 0.8 copy-done.4
  41.0 5.3 %attention_forward.3 = (bf16[256,1024]{1,0:T(8,128)(2,1)}, bf16[4,2,640,256]{3,2,1,0:T(8,128)(2,1)}) custom-call(s32[1]{0:T(128)} %bitcast.4.first_ref, s32[128]{0:T(128)} %lo_ref.3, s32[128]{0:T(128)} %hi_ref.3, s32[128]{0:T(128)} %half_ref.3, f32[128]{0:T(128)} %constant.41.clone.logw_ref, ...), custom_call_target="tpu_custom_call", output_to_operand_aliasing={{0}: (12, {})} | custom-call | flops 20000000000 | bytes 40000000 | tf_op jit(solution)/shard_map/attention_forward/pallas_call | solution.py:204
  46.4 2.7 %convolution_convert_fusion = bf16[1024,512]{1,0:T(8,128)(2,1)} fusion(bf16[256,1024]{1,0:T(8,128)(2,1)} %get-tuple-element.33.o_ref, bf16[256,1024]{1,0:T(8,128)(2,1)S(1)} %bitcast.32, s32[]{:T(128)S(6)} %select_n.8), kind=kOutput, calls=%fused_computation.1 | convolution fusion | flops 268959744 | bytes 1835012 | tf_op jit(solution)/shard_map/dot_general | solution.py:31
  49.0 5.4 %collective-permute-start.5 = (bf16[1024,512]{1,0:T(8,128)(2,1)}, bf16[1024,512]{1,0:T(8,128)(2,1)S(1)}, u32[]{:S(2)}, u32[]{:S(2)}) collective-permute-start(bf16[1024,512]{1,0:T(8,128)(2,1)} %convolution_convert_fusion), channel_id=1, source_target_pairs={{0,64},{64,0},{1,65},{65,1},{2,66},{66,2},{3,67},{67,3},{4,68},{68... | collective-permute-start | bytes 3145736 | tf_op jit(solution)/shard_map/ppermute | solution.py:275
  54.4 0.8 all-to-all-done.1
  55.2 2.4 %collective-permute-start = (bf16[1024,512]{1,0:T(8,128)(2,1)S(1)}, bf16[1024,512]{1,0:T(8,128)(2,1)}, u32[]{:S(2)}, u32[]{:S(2)}) collective-permute-start(bf16[1024,512]{1,0:T(8,128)(2,1)S(1)} %bitcast.46), channel_id=1, source_target_pairs={{0,64},{64,0},{1,65},{65,1},{2,66},{66,2},{3,67},{67,3},{4,68},{68... | collective-permute-start | bytes 3145736 | tf_op jit(solution)/shard_map/ppermute | solution.py:275
  57.7 1.5 %add_convert_fusion = bf16[1024,512]{1,0:T(8,128)(2,1)} fusion(bf16[1024,512]{1,0:T(8,128)(2,1)S(1)} %collective-permute-done.5, bf16[256,1024]{1,0:T(8,128)(2,1)S(1)} %copy-done.1, bf16[256,1024]{1,0:T(8,128)(2,1)S(1)} %bitcast.33, s32[]{:T(128)S(6)} %select_n.7), kind=kOutput, calls=%fused_computation | convolution fusion | flops 270008320 | bytes 2883588 | tf_op jit(solution)/shard_map/dot_general | solution.py:31
  59.1 3.8 %all-to-all-start.2 = ((bf16[4,256,512]{2,1,0:T(8,128)(2,1)}), bf16[4,256,512]{2,1,0:T(8,128)(2,1)S(1)}, u32[]{:S(2)}, u32[]{:S(2)}) async-start(bf16[4,256,512]{2,1,0:T(8,128)(2,1)} %bitcast.12), calls=%async_computation.2 | async-start | bytes 2097152 | tf_op jit(solution)/shard_map/all_to_all | solution.py:289
  62.9 0.5 fusion.4
  63.4 2.5 %fusion.g_ref = bf16[256,1024]{1,0:T(8,128)(2,1)} fusion(f32[256,1024]{1,0:T(8,128)S(1)} %fusion.4, bf16[1024,512]{1,0:T(8,128)(2,1)} %collective-permute-done, bf16[256,1024]{1,0:T(8,128)(2,1)S(1)} %bitcast.31, s32[]{:T(128)S(6)} %select_n.8), kind=kOutput, calls=%fused_computation.3 | convolution fusion | flops 268959744 | bytes 2883588 | tf_op jit(solution)/shard_map/dot_general | solution.py:31
  65.9 5.4 %attention_backward.2 = (bf16[256,1024]{1,0:T(8,128)(2,1)}, bf16[256,1024]{1,0:T(8,128)(2,1)}, bf16[256,1024]{1,0:T(8,128)(2,1)}, bf16[2,256,512]{2,1,0:T(8,128)(2,1)}, bf16[2,256,512]{2,1,0:T(8,128)(2,1)}) custom-call(bf16[256,1024]{1,0:T(8,128)(2,1)} %bitcast.50, bf16[256,1024]{1,0:T(8,128)(2,1)} %fusion.g_ref, bf16[256,1024]{1,0:T(8,128)(2,1)} %get-tuple-element.33.o_ref, ...), custom_call_target="tpu_custom_call" | custom-call | flops 1000000 | bytes 100000 | tf_op jit(solution)/shard_map/attention_backward/pallas_call | solution.py:232
  71.3 6.1 %collective-permute-start.8 = (bf16[2,256,512]{2,1,0:T(8,128)(2,1)}, bf16[2,256,512]{2,1,0:T(8,128)(2,1)S(1)}, u32[]{:S(2)}, u32[]{:S(2)}) collective-permute-start(bf16[2,256,512]{2,1,0:T(8,128)(2,1)} %get-tuple-element.45), channel_id=1, source_target_pairs={{0,1},{1,2},{2,3},{3,4},{4,5},{5,6},{6,7},{7,8},{8,9},{9,10},{10,1... | collective-permute-start | bytes 1572872 | tf_op jit(solution)/shard_map/ppermute | solution.py:271
  77.4 1.3 %collective-permute-start.9 = (bf16[2,256,512]{2,1,0:T(8,128)(2,1)}, bf16[2,256,512]{2,1,0:T(8,128)(2,1)S(1)}, u32[]{:S(2)}, u32[]{:S(2)}) collective-permute-start(bf16[2,256,512]{2,1,0:T(8,128)(2,1)} %get-tuple-element.46), channel_id=1, source_target_pairs={{1,0},{2,1},{3,2},{4,3},{5,4},{6,5},{7,6},{8,7},{9,8},{10,9},{11,1... | collective-permute-start | bytes 1572872 | tf_op jit(solution)/shard_map/ppermute | solution.py:271
  78.7 5.5 %attention_backward.3 = (bf16[256,1024]{1,0:T(8,128)(2,1)}, bf16[256,1024]{1,0:T(8,128)(2,1)}, bf16[256,1024]{1,0:T(8,128)(2,1)}, bf16[2,256,512]{2,1,0:T(8,128)(2,1)}, bf16[2,256,512]{2,1,0:T(8,128)(2,1)}) custom-call(bf16[256,1024]{1,0:T(8,128)(2,1)} %bitcast.51, ...), custom_call_target="tpu_custom_call", output_to_operand_aliasing={{0}: (10, {}), {1}: (11, {}), {2}: (12, {})} | custom-call | flops 1000000 | bytes 100000 | tf_op jit(solution)/shard_map/attention_backward/pallas_call | solution.py:232
  84.2 0.0 all-to-all-done.2
  84.2 0.9 reduce_sum.33
  85.1 5.4 %all-to-all-start.3 = ((bf16[16,16,512]{2,1,0:T(8,128)(2,1)}), bf16[16,16,512]{2,1,0:T(8,128)(2,1)S(1)}, u32[]{:S(2)}, u32[]{:S(2)}) async-start(bf16[16,16,512]{2,1,0:T(8,128)(2,1)} %bitcast.13), calls=%async_computation.3 | async-start | bytes 524288 | tf_op jit(solution)/shard_map/all_to_all | solution.py:289
  90.6 3.3 %collective-permute-start.6 = (bf16[2,256,512]{2,1,0:T(8,128)(2,1)}, bf16[2,256,512]{2,1,0:T(8,128)(2,1)S(1)}, u32[]{:S(2)}, u32[]{:S(2)}) collective-permute-start(bf16[2,256,512]{2,1,0:T(8,128)(2,1)} %get-tuple-element.42), channel_id=1, source_target_pairs={{0,1},{1,2},{2,3},{3,4},{4,5},{5,6},{6,7},{7,8},{8,9},{9,10},{10,1... | collective-permute-start | bytes 1572872 | tf_op jit(solution)/shard_map/ppermute | solution.py:271
  93.9 1.3 %collective-permute-start.7 = (bf16[2,256,512]{2,1,0:T(8,128)(2,1)}, bf16[2,256,512]{2,1,0:T(8,128)(2,1)S(1)}, u32[]{:S(2)}, u32[]{:S(2)}) collective-permute-start(bf16[2,256,512]{2,1,0:T(8,128)(2,1)} %get-tuple-element.43), channel_id=1, source_target_pairs={{1,0},{2,1},{3,2},{4,3},{5,4},{6,5},{7,6},{8,7},{9,8},{10,9},{11,1... | collective-permute-start | bytes 1572872 | tf_op jit(solution)/shard_map/ppermute | solution.py:271
  95.2 3.2 %all-to-all-done.3 = bf16[16,16,512]{2,1,0:T(8,128)(2,1)S(1)} async-done(((bf16[16,16,512]{2,1,0:T(8,128)(2,1)}), bf16[16,16,512]{2,1,0:T(8,128)(2,1)S(1)}, u32[]{:S(2)}, u32[]{:S(2)}) %all-to-all-start.3) | async-done | bytes 262176 | tf_op jit(solution)/shard_map/all_to_all | solution.py:289
  98.4 0.0 collective-permute-done.8.below_ref
  98.5 0.7 broadcast_in_dim.22
  99.2 14.3 %all-to-all-start.4 = ((bf16[8,16,512]{2,1,0:T(8,128)(2,1)}), bf16[8,16,512]{2,1,0:T(8,128)(2,1)S(1)}, u32[]{:S(2)}, u32[]{:S(2)}) async-start(bf16[8,16,512]{2,1,0:T(8,128)(2,1)} %broadcast_in_dim.22), calls=%async_computation.4 | async-start | bytes 262144 | tf_op jit(solution)/shard_map/all_to_all | solution.py:283
  113.5 2.1 %add_arrived.2 = (bf16[256,1024]{1,0:T(8,128)(2,1)}, bf16[256,1024]{1,0:T(8,128)(2,1)}) custom-call(bf16[2,256,512]{2,1,0:T(8,128)(2,1)} %copy-done.5, bf16[2,256,512]{2,1,0:T(8,128)(2,1)} %copy-done.6, bf16[256,1024]{1,0:T(8,128)(2,1)} %get-tuple-element.49.own_key_ref, ...), custom_call_target="tpu_custom_call", output_to_operand_aliasing={{0}: (2, {}), {1}: (3, {})} | custom-call | flops 1000000 | bytes 100000 | tf_op jit(solution)/shard_map/add_arrived/pallas_call | solution.py:256
  115.6 0.8 copy-done.7
  116.4 0.2 copy-done.8
  116.6 2.1 %add_arrived.3 = (bf16[256,1024]{1,0:T(8,128)(2,1)}, bf16[256,1024]{1,0:T(8,128)(2,1)}) custom-call(bf16[2,256,512]{2,1,0:T(8,128)(2,1)} %copy-done.7, bf16[2,256,512]{2,1,0:T(8,128)(2,1)} %copy-done.8, bf16[256,1024]{1,0:T(8,128)(2,1)} %get-tuple-element.51.own_key_ref, ...), custom_call_target="tpu_custom_call", output_to_operand_aliasing={{0}: (2, {}), {1}: (3, {})} | custom-call | flops 1000000 | bytes 100000 | tf_op jit(solution)/shard_map/add_arrived/pallas_call | solution.py:256
  118.7 2.8 %all-to-all-done.4 = bf16[8,16,512]{2,1,0:T(8,128)(2,1)S(1)} async-done(((bf16[8,16,512]{2,1,0:T(8,128)(2,1)}), bf16[8,16,512]{2,1,0:T(8,128)(2,1)S(1)}, u32[]{:S(2)}, u32[]{:S(2)}) %all-to-all-start.4) | async-done | bytes 131104 | tf_op jit(solution)/shard_map/all_to_all | solution.py:283
  121.5 0.6 maximum_multiply_fusion
  (24 shorter events, 0.1 us)
Async XLA Ops:
  0.6 45.7 %copy-start = (bf16[1,2,128,1024]{3,2,1,0:T(8,128)(2,1)S(1)}, bf16[1,2,128,1024]{3,2,1,0:T(8,128)(2,1)}, u32[]{:S(2)}) copy-start(bf16[1,2,128,1024]{3,2,1,0:T(8,128)(2,1)} %param.12) | copy-start | bytes 1572868
  0.6 7.5 %copy-start.9 = (bf16[16,1024]{1,0:T(8,128)(2,1)S(1)}, bf16[16,1024]{1,0:T(8,128)(2,1)}, u32[]{:S(2)}) copy-start(bf16[16,1024]{1,0:T(8,128)(2,1)} %param.13) | copy-start | bytes 98308
  2.8 31.1 %collective-permute-start.3 = (bf16[2,256,512]{2,1,0:T(8,128)(2,1)}, bf16[2,256,512]{2,1,0:T(8,128)(2,1)S(1)}, u32[]{:S(2)}, u32[]{:S(2)}) collective-permute-start(bf16[2,256,512]{2,1,0:T(8,128)(2,1)} %pad_maximum_fusion.1), channel_id=1, source_target_pairs={{0,1},{1,2},{2,3},{3,4},{4,5},{5,6},{6,7},{7,8},{8,9},{9,10},{10,1... | collective-permute-start | bytes 1572872 | tf_op jit(solution)/shard_map/ppermute | solution.py:271
  6.9 27.1 %collective-permute-start.4 = (bf16[2,256,512]{2,1,0:T(8,128)(2,1)}, bf16[2,256,512]{2,1,0:T(8,128)(2,1)S(1)}, u32[]{:S(2)}, u32[]{:S(2)}) collective-permute-start(bf16[2,256,512]{2,1,0:T(8,128)(2,1)} %pad_maximum_fusion.1), channel_id=1, source_target_pairs={{1,0},{2,1},{3,2},{4,3},{5,4},{6,5},{7,6},{8,7},{9,8},{10,9},{11,1... | collective-permute-start | bytes 1572872 | tf_op jit(solution)/shard_map/ppermute | solution.py:271
  8.9 19.6 %all-to-all-start = ((bf16[16,16,512]{2,1,0:T(8,128)(2,1)}), bf16[16,16,512]{2,1,0:T(8,128)(2,1)S(1)}, u32[]{:S(2)}, u32[]{:S(2)}) async-start(bf16[16,16,512]{2,1,0:T(8,128)(2,1)} %broadcast_in_dim.8), calls=%async_computation | async-start | bytes 524288 | tf_op jit(solution)/shard_map/all_to_all | solution.py:283
  20.5 19.7 %collective-permute-start.1 = (bf16[2,256,512]{2,1,0:T(8,128)(2,1)}, bf16[2,256,512]{2,1,0:T(8,128)(2,1)S(1)}, u32[]{:S(2)}, u32[]{:S(2)}) collective-permute-start(bf16[2,256,512]{2,1,0:T(8,128)(2,1)} %pad_maximum_fusion), channel_id=1, source_target_pairs={{0,1},{1,2},{2,3},{3,4},{4,5},{5,6},{6,7},{7,8},{8,9},{9,10},{10,1... | collective-permute-start | bytes 1572872 | tf_op jit(solution)/shard_map/ppermute | solution.py:271
  23.8 16.4 %collective-permute-start.2 = (bf16[2,256,512]{2,1,0:T(8,128)(2,1)}, bf16[2,256,512]{2,1,0:T(8,128)(2,1)}, u32[]{:S(2)}, u32[]{:S(2)}) collective-permute-start(bf16[2,256,512]{2,1,0:T(8,128)(2,1)} %pad_maximum_fusion), channel_id=1, source_target_pairs={{1,0},{2,1},{3,2},{4,3},{5,4},{6,5},{7,6},{8,7},{9,8},{10,9},{11,1... | collective-permute-start | bytes 1572872 | tf_op jit(solution)/shard_map/ppermute | solution.py:271
  29.6 25.6 %all-to-all-start.1 = ((bf16[4,256,512]{2,1,0:T(8,128)(2,1)}), bf16[4,256,512]{2,1,0:T(8,128)(2,1)S(1)}, u32[]{:S(2)}, u32[]{:S(2)}) async-start(bf16[4,256,512]{2,1,0:T(8,128)(2,1)} %broadcast_in_dim.10), calls=%async_computation.1 | async-start | bytes 2097152 | tf_op jit(solution)/shard_map/all_to_all | solution.py:315
  34.0 0.8 copy-start.2
  34.0 1.0 copy-start.3
  40.2 0.8 copy-start.4
  46.3 11.3 %copy-start.1 = (bf16[256,1024]{1,0:T(8,128)(2,1)S(1)}, bf16[256,1024]{1,0:T(8,128)(2,1)}, u32[]{:S(2)}) copy-start(bf16[256,1024]{1,0:T(8,128)(2,1)} %get-tuple-element.33.o_ref) | copy-start | bytes 1572868
  49.0 8.6 %collective-permute-start.5 = (bf16[1024,512]{1,0:T(8,128)(2,1)}, bf16[1024,512]{1,0:T(8,128)(2,1)S(1)}, u32[]{:S(2)}, u32[]{:S(2)}) collective-permute-start(bf16[1024,512]{1,0:T(8,128)(2,1)} %convolution_convert_fusion), channel_id=1, source_target_pairs={{0,64},{64,0},{1,65},{65,1},{2,66},{66,2},{3,67},{67,3},{4,68},{68... | collective-permute-start | bytes 3145736 | tf_op jit(solution)/shard_map/ppermute | solution.py:275
  55.2 8.1 %collective-permute-start = (bf16[1024,512]{1,0:T(8,128)(2,1)S(1)}, bf16[1024,512]{1,0:T(8,128)(2,1)}, u32[]{:S(2)}, u32[]{:S(2)}) collective-permute-start(bf16[1024,512]{1,0:T(8,128)(2,1)S(1)} %bitcast.46), channel_id=1, source_target_pairs={{0,64},{64,0},{1,65},{65,1},{2,66},{66,2},{3,67},{67,3},{4,68},{68... | collective-permute-start | bytes 3145736 | tf_op jit(solution)/shard_map/ppermute | solution.py:275
  59.1 25.1 %all-to-all-start.2 = ((bf16[4,256,512]{2,1,0:T(8,128)(2,1)}), bf16[4,256,512]{2,1,0:T(8,128)(2,1)S(1)}, u32[]{:S(2)}, u32[]{:S(2)}) async-start(bf16[4,256,512]{2,1,0:T(8,128)(2,1)} %bitcast.12), calls=%async_computation.2 | async-start | bytes 2097152 | tf_op jit(solution)/shard_map/all_to_all | solution.py:289
  71.3 27.1 %collective-permute-start.8 = (bf16[2,256,512]{2,1,0:T(8,128)(2,1)}, bf16[2,256,512]{2,1,0:T(8,128)(2,1)S(1)}, u32[]{:S(2)}, u32[]{:S(2)}) collective-permute-start(bf16[2,256,512]{2,1,0:T(8,128)(2,1)} %get-tuple-element.45), channel_id=1, source_target_pairs={{0,1},{1,2},{2,3},{3,4},{4,5},{5,6},{6,7},{7,8},{8,9},{9,10},{10,1... | collective-permute-start | bytes 1572872 | tf_op jit(solution)/shard_map/ppermute | solution.py:271
  77.4 21.0 %collective-permute-start.9 = (bf16[2,256,512]{2,1,0:T(8,128)(2,1)}, bf16[2,256,512]{2,1,0:T(8,128)(2,1)S(1)}, u32[]{:S(2)}, u32[]{:S(2)}) collective-permute-start(bf16[2,256,512]{2,1,0:T(8,128)(2,1)} %get-tuple-element.46), channel_id=1, source_target_pairs={{1,0},{2,1},{3,2},{4,3},{5,4},{6,5},{7,6},{8,7},{9,8},{10,9},{11,1... | collective-permute-start | bytes 1572872 | tf_op jit(solution)/shard_map/ppermute | solution.py:271
  85.1 13.3 %all-to-all-start.3 = ((bf16[16,16,512]{2,1,0:T(8,128)(2,1)}), bf16[16,16,512]{2,1,0:T(8,128)(2,1)S(1)}, u32[]{:S(2)}, u32[]{:S(2)}) async-start(bf16[16,16,512]{2,1,0:T(8,128)(2,1)} %bitcast.13), calls=%async_computation.3 | async-start | bytes 524288 | tf_op jit(solution)/shard_map/all_to_all | solution.py:289
  90.6 25.0 %collective-permute-start.6 = (bf16[2,256,512]{2,1,0:T(8,128)(2,1)}, bf16[2,256,512]{2,1,0:T(8,128)(2,1)S(1)}, u32[]{:S(2)}, u32[]{:S(2)}) collective-permute-start(bf16[2,256,512]{2,1,0:T(8,128)(2,1)} %get-tuple-element.42), channel_id=1, source_target_pairs={{0,1},{1,2},{2,3},{3,4},{4,5},{5,6},{6,7},{7,8},{8,9},{9,10},{10,1... | collective-permute-start | bytes 1572872 | tf_op jit(solution)/shard_map/ppermute | solution.py:271
  93.9 21.8 %collective-permute-start.7 = (bf16[2,256,512]{2,1,0:T(8,128)(2,1)}, bf16[2,256,512]{2,1,0:T(8,128)(2,1)S(1)}, u32[]{:S(2)}, u32[]{:S(2)}) collective-permute-start(bf16[2,256,512]{2,1,0:T(8,128)(2,1)} %get-tuple-element.43), channel_id=1, source_target_pairs={{1,0},{2,1},{3,2},{4,3},{5,4},{6,5},{7,6},{8,7},{9,8},{10,9},{11,1... | collective-permute-start | bytes 1572872 | tf_op jit(solution)/shard_map/ppermute | solution.py:271
  98.4 15.0 %copy-start.5 = (bf16[2,256,512]{2,1,0:T(8,128)(2,1)}, bf16[2,256,512]{2,1,0:T(8,128)(2,1)S(1)}, u32[]{:S(2)}) copy-start(bf16[2,256,512]{2,1,0:T(8,128)(2,1)S(1)} %collective-permute-done.8.below_ref) | copy-start | bytes 1572868
  98.5 15.0 %copy-start.6 = (bf16[2,256,512]{2,1,0:T(8,128)(2,1)}, bf16[2,256,512]{2,1,0:T(8,128)(2,1)S(1)}, u32[]{:S(2)}) copy-start(bf16[2,256,512]{2,1,0:T(8,128)(2,1)S(1)} %collective-permute-done.9.above_ref) | copy-start | bytes 1572868
  99.2 22.3 %all-to-all-start.4 = ((bf16[8,16,512]{2,1,0:T(8,128)(2,1)}), bf16[8,16,512]{2,1,0:T(8,128)(2,1)S(1)}, u32[]{:S(2)}, u32[]{:S(2)}) async-start(bf16[8,16,512]{2,1,0:T(8,128)(2,1)} %broadcast_in_dim.22), calls=%async_computation.4 | async-start | bytes 262144 | tf_op jit(solution)/shard_map/all_to_all | solution.py:283
  115.6 0.8 copy-start.7
  115.6 1.0 copy-start.8

commit v8 on v7

--- a/solution.py
+++ b/solution.py
@@ -343,7 +343,6 @@
 
     partial = scatter_sum(partial, "x").astype(BF)
     arrived = [(lat_shift(edges[0][1], 1), lat_shift(edges[0][0], -1))]
-    partial, edges[1] = lax.optimization_barrier((partial, edges[1]))
     partial = scatter_sum(partial, ZY).astype(BF)
     partial, arrived[0] = lax.optimization_barrier((partial, arrived[0]))
     arrived.append((lat_shift(edges[1][1], 1), lat_shift(edges[1][0], -1)))

time: 123 us -> 122 us (level)
  the two profiles are of different devices: /device:TPU:1 before, /device:TPU:59 now
where the time goes in v8:
time: 122 us; the launch traced here: 121 us
  starting transfers between devices  66.2 us (54%)
  Pallas kernels  25.6 us (21%)
  waiting for transfers between devices  11.6 us (10%)
  matrix products  7.08 us (6%)
  local copies, waits for them, and re-layouts  6.59 us (5%)
  other arithmetic  3.29 us (3%)
    all_to_all x2, starting transfers between devices, spread(): return lax.all_to_all(copies_of(value, axes), axes, 0, 0, tiled=True)  22.2 us
    ppermute x8, starting transfers between devices, lat_shift(): return lax.ppermute(value, LAT, pairs)  21.1 us
    all_to_all x2, starting transfers between devices, scatter_sum(): received = lax.all_to_all(blocks, axes, 0, 0, tiled=True)  11.6 us
    all_to_all x2, waiting for transfers between devices, spread(): return lax.all_to_all(copies_of(value, axes), axes, 0, 0, tiled=True)  11 us
    pallas_call x2, Pallas kernels, backward(): pl.pallas_call(backward_kernel, grid=(steps,), in_specs=specs + [pl.Block...  10.9 us
    pallas_call x2, Pallas kernels, forward(): pl.pallas_call(forward_kernel, grid=(steps,), in_specs=specs + [pl.BlockS...  10.5 us
    ppermute x2, starting transfers between devices, core_swap(): return lax.ppermute(value, 'core', [(0, 1), (1, 0)])  7.08 us
    dot_general x4, matrix products, dot(): return lax.dot_general(a, b, (dims, ((), ())), preferred_element_type=F32)  7.08 us
  transfers between devices with their start and end apart: 15, of which 3 were waited for; matrix products, arithmetic and copies ran while one was open for 9% of the time, Pallas kernels for 21%

profile of v8, /device:TPU:59, one launch (start us, length us, event | category | flops | bytes accessed | tf_op | source)
XLA Modules:
  0.0 121.4 jit_solution(9560559728113873554)
XLA Ops:
  0.6 0.0 copy-start
  0.7 1.3 %slice_bitcast_fusion = (bf16[1,256,512]{2,1,0:T(8,128)(2,1)S(1)}, bf16[1,256,512]{2,1,0:T(8,128)(2,1)S(1)}, bf16[1,256,512]{2,1,0:T(8,128)(2,1)S(1)}, bf16[1,256,512]{2,1,0:T(8,128)(2,1)S(1)}) fusion(bf16[256,1024]{1,0:T(8,128)(2,1)} %bitcast.34, bf16[256,1024]{1,0:T(8,128)(2,1)} %bitcast.39), kind=kLoop, calls=%fused_computation.6 | loop fusion | bytes 2097152 | tf_op jit(solution)/shard_map/stack | solution.py:306
  2.0 0.8 pad_maximum_fusion.1
  2.8 3.2 %collective-permute-start.3 = (bf16[2,256,512]{2,1,0:T(8,128)(2,1)}, bf16[2,256,512]{2,1,0:T(8,128)(2,1)S(1)}, u32[]{:S(2)}, u32[]{:S(2)}) collective-permute-start(bf16[2,256,512]{2,1,0:T(8,128)(2,1)} %pad_maximum_fusion.1), channel_id=1, source_target_pairs={{0,1},{1,2},{2,3},{3,4},{4,5},{5,6},{6,7},{7,8},{8,9},{9,10},{10,1... | collective-permute-start | bytes 1572872 | tf_op jit(solution)/shard_map/ppermute | solution.py:271
  6.0 2.1 %collective-permute-start.4 = (bf16[2,256,512]{2,1,0:T(8,128)(2,1)}, bf16[2,256,512]{2,1,0:T(8,128)(2,1)S(1)}, u32[]{:S(2)}, u32[]{:S(2)}) collective-permute-start(bf16[2,256,512]{2,1,0:T(8,128)(2,1)} %pad_maximum_fusion.1), channel_id=1, source_target_pairs={{1,0},{2,1},{3,2},{4,3},{5,4},{6,5},{7,6},{8,7},{9,8},{10,9},{11,1... | collective-permute-start | bytes 1572872 | tf_op jit(solution)/shard_map/ppermute | solution.py:271
  8.1 0.7 broadcast_in_dim.8
  8.9 9.3 %all-to-all-start = ((bf16[16,16,512]{2,1,0:T(8,128)(2,1)}), bf16[16,16,512]{2,1,0:T(8,128)(2,1)S(1)}, u32[]{:S(2)}, u32[]{:S(2)}) async-start(bf16[16,16,512]{2,1,0:T(8,128)(2,1)} %broadcast_in_dim.8), calls=%async_computation | async-start | bytes 524288 | tf_op jit(solution)/shard_map/all_to_all | solution.py:283
  18.2 0.8 pad_maximum_fusion
  19.1 3.1 %collective-permute-start.1 = (bf16[2,256,512]{2,1,0:T(8,128)(2,1)}, bf16[2,256,512]{2,1,0:T(8,128)(2,1)S(1)}, u32[]{:S(2)}, u32[]{:S(2)}) collective-permute-start(bf16[2,256,512]{2,1,0:T(8,128)(2,1)} %pad_maximum_fusion), channel_id=1, source_target_pairs={{0,1},{1,2},{2,3},{3,4},{4,5},{5,6},{6,7},{7,8},{8,9},{9,10},{10,1... | collective-permute-start | bytes 1572872 | tf_op jit(solution)/shard_map/ppermute | solution.py:271
  22.1 2.2 %collective-permute-start.2 = (bf16[2,256,512]{2,1,0:T(8,128)(2,1)}, bf16[2,256,512]{2,1,0:T(8,128)(2,1)}, u32[]{:S(2)}, u32[]{:S(2)}) collective-permute-start(bf16[2,256,512]{2,1,0:T(8,128)(2,1)} %pad_maximum_fusion), channel_id=1, source_target_pairs={{1,0},{2,1},{3,2},{4,3},{5,4},{6,5},{7,6},{8,7},{9,8},{10,9},{11,1... | collective-permute-start | bytes 1572872 | tf_op jit(solution)/shard_map/ppermute | solution.py:271
  24.4 3.8 %all-to-all-done = bf16[16,16,512]{2,1,0:T(8,128)(2,1)S(1)} async-done(((bf16[16,16,512]{2,1,0:T(8,128)(2,1)}), bf16[16,16,512]{2,1,0:T(8,128)(2,1)S(1)}, u32[]{:S(2)}, u32[]{:S(2)}) %all-to-all-start) | async-done | bytes 262176 | tf_op jit(solution)/shard_map/all_to_all | solution.py:283
  28.1 1.1 broadcast_in_dim.10
  29.2 4.3 %all-to-all-start.1 = ((bf16[4,256,512]{2,1,0:T(8,128)(2,1)}), bf16[4,256,512]{2,1,0:T(8,128)(2,1)S(1)}, u32[]{:S(2)}, u32[]{:S(2)}) async-start(bf16[4,256,512]{2,1,0:T(8,128)(2,1)} %broadcast_in_dim.10), calls=%async_computation.1 | async-start | bytes 2097152 | tf_op jit(solution)/shard_map/all_to_all | solution.py:315
  33.5 0.0 collective-permute-done.3.kp_ref.vp_ref
  33.5 0.0 collective-permute-done.4.kn_ref.vn_ref
  33.5 0.8 copy-done.2
  34.3 0.2 copy-done.3
  34.5 5.3 %attention_forward.2 = (bf16[256,1024]{1,0:T(8,128)(2,1)}, bf16[4,2,640,256]{3,2,1,0:T(8,128)(2,1)}) custom-call(s32[1]{0:T(128)} %bitcast.4.first_ref, s32[128]{0:T(128)} %lo_ref.3, s32[128]{0:T(128)} %hi_ref.3, s32[128]{0:T(128)} %half_ref.3, f32[128]{0:T(128)} %constant.41.clone.logw_ref, bf16[256,1024]{1,0:T(8,128)(2,1)} %bitcast.48, ...), custom_call_target="tpu_custom_call" | custom-call | flops 20000000000 | bytes 40000000 | tf_op jit(solution)/shard_map/attention_forward/pallas_call | solution.py:204
  39.8 0.8 copy-done.4
  40.6 5.2 %attention_forward.3 = (bf16[256,1024]{1,0:T(8,128)(2,1)}, bf16[4,2,640,256]{3,2,1,0:T(8,128)(2,1)}) custom-call(s32[1]{0:T(128)} %bitcast.4.first_ref, s32[128]{0:T(128)} %lo_ref.3, s32[128]{0:T(128)} %hi_ref.3, s32[128]{0:T(128)} %half_ref.3, f32[128]{0:T(128)} %constant.41.clone.logw_ref, ...), custom_call_target="tpu_custom_call", output_to_operand_aliasing={{0}: (12, {})} | custom-call | flops 20000000000 | bytes 40000000 | tf_op jit(solution)/shard_map/attention_forward/pallas_call | solution.py:204
  45.8 2.7 %convolution_convert_fusion = bf16[1024,512]{1,0:T(8,128)(2,1)} fusion(bf16[256,1024]{1,0:T(8,128)(2,1)} %get-tuple-element.30.o_ref, bf16[256,1024]{1,0:T(8,128)(2,1)S(1)} %bitcast.32, s32[]{:T(128)S(6)} %select_n.8), kind=kOutput, calls=%fused_computation.1 | convolution fusion | flops 268959744 | bytes 1835012 | tf_op jit(solution)/shard_map/dot_general | solution.py:31
  48.5 5.2 %collective-permute-start.7 = (bf16[1024,512]{1,0:T(8,128)(2,1)}, bf16[1024,512]{1,0:T(8,128)(2,1)S(1)}, u32[]{:S(2)}, u32[]{:S(2)}) collective-permute-start(bf16[1024,512]{1,0:T(8,128)(2,1)} %convolution_convert_fusion), channel_id=1, source_target_pairs={{0,64},{64,0},{1,65},{65,1},{2,66},{66,2},{3,67},{67,3},{4,68},{68... | collective-permute-start | bytes 3145736 | tf_op jit(solution)/shard_map/ppermute | solution.py:275
  53.7 1.9 %collective-permute-start = (bf16[1024,512]{1,0:T(8,128)(2,1)S(1)}, bf16[1024,512]{1,0:T(8,128)(2,1)}, u32[]{:S(2)}, u32[]{:S(2)}) collective-permute-start(bf16[1024,512]{1,0:T(8,128)(2,1)S(1)} %bitcast.46), channel_id=1, source_target_pairs={{0,64},{64,0},{1,65},{65,1},{2,66},{66,2},{3,67},{67,3},{4,68},{68... | collective-permute-start | bytes 3145736 | tf_op jit(solution)/shard_map/ppermute | solution.py:275
  55.6 0.5 collective-permute-done.7
  56.1 1.5 %add_convert_fusion = bf16[1024,512]{1,0:T(8,128)(2,1)} fusion(bf16[1024,512]{1,0:T(8,128)(2,1)S(1)} %collective-permute-done.7, bf16[256,1024]{1,0:T(8,128)(2,1)S(1)} %copy-done.1, bf16[256,1024]{1,0:T(8,128)(2,1)S(1)} %bitcast.33, s32[]{:T(128)S(6)} %select_n.7), kind=kOutput, calls=%fused_computation | convolution fusion | flops 270008320 | bytes 2883588 | tf_op jit(solution)/shard_map/dot_general | solution.py:31
  57.6 4.2 %all-to-all-start.2 = ((bf16[4,256,512]{2,1,0:T(8,128)(2,1)}), bf16[4,256,512]{2,1,0:T(8,128)(2,1)S(1)}, u32[]{:S(2)}, u32[]{:S(2)}) async-start(bf16[4,256,512]{2,1,0:T(8,128)(2,1)} %bitcast.12), calls=%async_computation.2 | async-start | bytes 2097152 | tf_op jit(solution)/shard_map/all_to_all | solution.py:289
  61.8 0.5 fusion.4
  62.3 0.0 collective-permute-done
  62.3 2.5 %fusion.g_ref = bf16[256,1024]{1,0:T(8,128)(2,1)} fusion(f32[256,1024]{1,0:T(8,128)S(1)} %fusion.4, bf16[1024,512]{1,0:T(8,128)(2,1)} %collective-permute-done, bf16[256,1024]{1,0:T(8,128)(2,1)S(1)} %bitcast.31, s32[]{:T(128)S(6)} %select_n.8), kind=kOutput, calls=%fused_computation.3 | convolution fusion | flops 268959744 | bytes 2883588 | tf_op jit(solution)/shard_map/dot_general | solution.py:31
  64.8 5.4 %attention_backward.2 = (bf16[256,1024]{1,0:T(8,128)(2,1)}, bf16[256,1024]{1,0:T(8,128)(2,1)}, bf16[256,1024]{1,0:T(8,128)(2,1)}, bf16[2,256,512]{2,1,0:T(8,128)(2,1)}, bf16[2,256,512]{2,1,0:T(8,128)(2,1)}) custom-call(bf16[256,1024]{1,0:T(8,128)(2,1)} %bitcast.50, bf16[256,1024]{1,0:T(8,128)(2,1)} %fusion.g_ref, bf16[256,1024]{1,0:T(8,128)(2,1)} %get-tuple-element.30.o_ref, ...), custom_call_target="tpu_custom_call" | custom-call | flops 1000000 | bytes 100000 | tf_op jit(solution)/shard_map/attention_backward/pallas_call | solution.py:232
  70.2 1.9 %collective-permute-start.8 = (bf16[2,256,512]{2,1,0:T(8,128)(2,1)}, bf16[2,256,512]{2,1,0:T(8,128)(2,1)S(1)}, u32[]{:S(2)}, u32[]{:S(2)}) collective-permute-start(bf16[2,256,512]{2,1,0:T(8,128)(2,1)} %get-tuple-element.39), channel_id=1, source_target_pairs={{0,1},{1,2},{2,3},{3,4},{4,5},{5,6},{6,7},{7,8},{8,9},{9,10},{10,1... | collective-permute-start | bytes 1572872 | tf_op jit(solution)/shard_map/ppermute | solution.py:271
  72.2 3.3 %collective-permute-start.9 = (bf16[2,256,512]{2,1,0:T(8,128)(2,1)}, bf16[2,256,512]{2,1,0:T(8,128)(2,1)S(1)}, u32[]{:S(2)}, u32[]{:S(2)}) collective-permute-start(bf16[2,256,512]{2,1,0:T(8,128)(2,1)} %get-tuple-element.40), channel_id=1, source_target_pairs={{1,0},{2,1},{3,2},{4,3},{5,4},{6,5},{7,6},{8,7},{9,8},{10,9},{11,1... | collective-permute-start | bytes 1572872 | tf_op jit(solution)/shard_map/ppermute | solution.py:271
  75.5 0.0 all-to-all-done.2
  75.5 0.9 reduce_sum.33
  76.5 7.4 %all-to-all-start.3 = ((bf16[16,16,512]{2,1,0:T(8,128)(2,1)}), bf16[16,16,512]{2,1,0:T(8,128)(2,1)S(1)}, u32[]{:S(2)}, u32[]{:S(2)}) async-start(bf16[16,16,512]{2,1,0:T(8,128)(2,1)} %bitcast.13), calls=%async_computation.3 | async-start | bytes 524288 | tf_op jit(solution)/shard_map/all_to_all | solution.py:289
  83.8 5.5 %attention_backward.3 = (bf16[256,1024]{1,0:T(8,128)(2,1)}, bf16[256,1024]{1,0:T(8,128)(2,1)}, bf16[256,1024]{1,0:T(8,128)(2,1)}, bf16[2,256,512]{2,1,0:T(8,128)(2,1)}, bf16[2,256,512]{2,1,0:T(8,128)(2,1)}) custom-call(bf16[256,1024]{1,0:T(8,128)(2,1)} %bitcast.51, ...), custom_call_target="tpu_custom_call", output_to_operand_aliasing={{0}: (10, {}), {1}: (11, {}), {2}: (12, {})} | custom-call | flops 1000000 | bytes 100000 | tf_op jit(solution)/shard_map/attention_backward/pallas_call | solution.py:232
  89.3 3.1 %collective-permute-start.5 = (bf16[2,256,512]{2,1,0:T(8,128)(2,1)}, bf16[2,256,512]{2,1,0:T(8,128)(2,1)S(1)}, u32[]{:S(2)}, u32[]{:S(2)}) collective-permute-start(bf16[2,256,512]{2,1,0:T(8,128)(2,1)} %get-tuple-element.37), channel_id=1, source_target_pairs={{0,1},{1,2},{2,3},{3,4},{4,5},{5,6},{6,7},{7,8},{8,9},{9,10},{10,1... | collective-permute-start | bytes 1572872 | tf_op jit(solution)/shard_map/ppermute | solution.py:271
  92.4 2.2 %collective-permute-start.6 = (bf16[2,256,512]{2,1,0:T(8,128)(2,1)}, bf16[2,256,512]{2,1,0:T(8,128)(2,1)S(1)}, u32[]{:S(2)}, u32[]{:S(2)}) collective-permute-start(bf16[2,256,512]{2,1,0:T(8,128)(2,1)} %get-tuple-element.38), channel_id=1, source_target_pairs={{1,0},{2,1},{3,2},{4,3},{5,4},{6,5},{7,6},{8,7},{9,8},{10,9},{11,1... | collective-permute-start | bytes 1572872 | tf_op jit(solution)/shard_map/ppermute | solution.py:271
  94.6 0.0 all-to-all-done.3
  94.7 0.0 collective-permute-done.8.below_ref
  94.7 0.7 broadcast_in_dim.22
  95.4 12.8 %all-to-all-start.4 = ((bf16[8,16,512]{2,1,0:T(8,128)(2,1)}), bf16[8,16,512]{2,1,0:T(8,128)(2,1)S(1)}, u32[]{:S(2)}, u32[]{:S(2)}) async-start(bf16[8,16,512]{2,1,0:T(8,128)(2,1)} %broadcast_in_dim.22), calls=%async_computation.4 | async-start | bytes 262144 | tf_op jit(solution)/shard_map/all_to_all | solution.py:283
  108.2 2.1 %add_arrived.2 = (bf16[256,1024]{1,0:T(8,128)(2,1)}, bf16[256,1024]{1,0:T(8,128)(2,1)}) custom-call(bf16[2,256,512]{2,1,0:T(8,128)(2,1)} %copy-done.5, bf16[2,256,512]{2,1,0:T(8,128)(2,1)} %copy-done.6, bf16[256,1024]{1,0:T(8,128)(2,1)} %get-tuple-element.43.own_key_ref, ...), custom_call_target="tpu_custom_call", output_to_operand_aliasing={{0}: (2, {}), {1}: (3, {})} | custom-call | flops 1000000 | bytes 100000 | tf_op jit(solution)/shard_map/add_arrived/pallas_call | solution.py:256
  110.4 0.8 copy-done.7
  111.2 0.2 copy-done.8
  111.4 2.1 %add_arrived.3 = (bf16[256,1024]{1,0:T(8,128)(2,1)}, bf16[256,1024]{1,0:T(8,128)(2,1)}) custom-call(bf16[2,256,512]{2,1,0:T(8,128)(2,1)} %copy-done.7, bf16[2,256,512]{2,1,0:T(8,128)(2,1)} %copy-done.8, bf16[256,1024]{1,0:T(8,128)(2,1)} %get-tuple-element.45.own_key_ref, ...), custom_call_target="tpu_custom_call", output_to_operand_aliasing={{0}: (2, {}), {1}: (3, {})} | custom-call | flops 1000000 | bytes 100000 | tf_op jit(solution)/shard_map/add_arrived/pallas_call | solution.py:256
  113.5 7.2 %all-to-all-done.4 = bf16[8,16,512]{2,1,0:T(8,128)(2,1)S(1)} async-done(((bf16[8,16,512]{2,1,0:T(8,128)(2,1)}), bf16[8,16,512]{2,1,0:T(8,128)(2,1)S(1)}, u32[]{:S(2)}, u32[]{:S(2)}) %all-to-all-start.4) | async-done | bytes 131104 | tf_op jit(solution)/shard_map/all_to_all | solution.py:283
  120.7 0.6 maximum_multiply_fusion
  (24 shorter events, 0.1 us)
Async XLA Ops:
  0.6 45.2 %copy-start = (bf16[1,2,128,1024]{3,2,1,0:T(8,128)(2,1)S(1)}, bf16[1,2,128,1024]{3,2,1,0:T(8,128)(2,1)}, u32[]{:S(2)}) copy-start(bf16[1,2,128,1024]{3,2,1,0:T(8,128)(2,1)} %param.12) | copy-start | bytes 1572868
  0.6 7.5 %copy-start.9 = (bf16[16,1024]{1,0:T(8,128)(2,1)S(1)}, bf16[16,1024]{1,0:T(8,128)(2,1)}, u32[]{:S(2)}) copy-start(bf16[16,1024]{1,0:T(8,128)(2,1)} %param.13) | copy-start | bytes 98308
  2.8 30.7 %collective-permute-start.3 = (bf16[2,256,512]{2,1,0:T(8,128)(2,1)}, bf16[2,256,512]{2,1,0:T(8,128)(2,1)S(1)}, u32[]{:S(2)}, u32[]{:S(2)}) collective-permute-start(bf16[2,256,512]{2,1,0:T(8,128)(2,1)} %pad_maximum_fusion.1), channel_id=1, source_target_pairs={{0,1},{1,2},{2,3},{3,4},{4,5},{5,6},{6,7},{7,8},{8,9},{9,10},{10,1... | collective-permute-start | bytes 1572872 | tf_op jit(solution)/shard_map/ppermute | solution.py:271
  6.0 27.5 %collective-permute-start.4 = (bf16[2,256,512]{2,1,0:T(8,128)(2,1)}, bf16[2,256,512]{2,1,0:T(8,128)(2,1)S(1)}, u32[]{:S(2)}, u32[]{:S(2)}) collective-permute-start(bf16[2,256,512]{2,1,0:T(8,128)(2,1)} %pad_maximum_fusion.1), channel_id=1, source_target_pairs={{1,0},{2,1},{3,2},{4,3},{5,4},{6,5},{7,6},{8,7},{9,8},{10,9},{11,1... | collective-permute-start | bytes 1572872 | tf_op jit(solution)/shard_map/ppermute | solution.py:271
  8.9 19.3 %all-to-all-start = ((bf16[16,16,512]{2,1,0:T(8,128)(2,1)}), bf16[16,16,512]{2,1,0:T(8,128)(2,1)S(1)}, u32[]{:S(2)}, u32[]{:S(2)}) async-start(bf16[16,16,512]{2,1,0:T(8,128)(2,1)} %broadcast_in_dim.8), calls=%async_computation | async-start | bytes 524288 | tf_op jit(solution)/shard_map/all_to_all | solution.py:283
  19.1 20.7 %collective-permute-start.1 = (bf16[2,256,512]{2,1,0:T(8,128)(2,1)}, bf16[2,256,512]{2,1,0:T(8,128)(2,1)S(1)}, u32[]{:S(2)}, u32[]{:S(2)}) collective-permute-start(bf16[2,256,512]{2,1,0:T(8,128)(2,1)} %pad_maximum_fusion), channel_id=1, source_target_pairs={{0,1},{1,2},{2,3},{3,4},{4,5},{5,6},{6,7},{7,8},{8,9},{9,10},{10,1... | collective-permute-start | bytes 1572872 | tf_op jit(solution)/shard_map/ppermute | solution.py:271
  22.1 17.6 %collective-permute-start.2 = (bf16[2,256,512]{2,1,0:T(8,128)(2,1)}, bf16[2,256,512]{2,1,0:T(8,128)(2,1)}, u32[]{:S(2)}, u32[]{:S(2)}) collective-permute-start(bf16[2,256,512]{2,1,0:T(8,128)(2,1)} %pad_maximum_fusion), channel_id=1, source_target_pairs={{1,0},{2,1},{3,2},{4,3},{5,4},{6,5},{7,6},{8,7},{9,8},{10,9},{11,1... | collective-permute-start | bytes 1572872 | tf_op jit(solution)/shard_map/ppermute | solution.py:271
  29.2 24.4 %all-to-all-start.1 = ((bf16[4,256,512]{2,1,0:T(8,128)(2,1)}), bf16[4,256,512]{2,1,0:T(8,128)(2,1)S(1)}, u32[]{:S(2)}, u32[]{:S(2)}) async-start(bf16[4,256,512]{2,1,0:T(8,128)(2,1)} %broadcast_in_dim.10), calls=%async_computation.1 | async-start | bytes 2097152 | tf_op jit(solution)/shard_map/all_to_all | solution.py:315
  33.5 0.8 copy-start.2
  33.5 1.0 copy-start.3
  39.8 0.8 copy-start.4
  45.8 10.3 %copy-start.1 = (bf16[256,1024]{1,0:T(8,128)(2,1)S(1)}, bf16[256,1024]{1,0:T(8,128)(2,1)}, u32[]{:S(2)}) copy-start(bf16[256,1024]{1,0:T(8,128)(2,1)} %get-tuple-element.30.o_ref) | copy-start | bytes 1572868
  48.5 7.6 %collective-permute-start.7 = (bf16[1024,512]{1,0:T(8,128)(2,1)}, bf16[1024,512]{1,0:T(8,128)(2,1)S(1)}, u32[]{:S(2)}, u32[]{:S(2)}) collective-permute-start(bf16[1024,512]{1,0:T(8,128)(2,1)} %convolution_convert_fusion), channel_id=1, source_target_pairs={{0,64},{64,0},{1,65},{65,1},{2,66},{66,2},{3,67},{67,3},{4,68},{68... | collective-permute-start | bytes 3145736 | tf_op jit(solution)/shard_map/ppermute | solution.py:275
  53.7 8.6 %collective-permute-start = (bf16[1024,512]{1,0:T(8,128)(2,1)S(1)}, bf16[1024,512]{1,0:T(8,128)(2,1)}, u32[]{:S(2)}, u32[]{:S(2)}) collective-permute-start(bf16[1024,512]{1,0:T(8,128)(2,1)S(1)} %bitcast.46), channel_id=1, source_target_pairs={{0,64},{64,0},{1,65},{65,1},{2,66},{66,2},{3,67},{67,3},{4,68},{68... | collective-permute-start | bytes 3145736 | tf_op jit(solution)/shard_map/ppermute | solution.py:275
  57.6 18.0 %all-to-all-start.2 = ((bf16[4,256,512]{2,1,0:T(8,128)(2,1)}), bf16[4,256,512]{2,1,0:T(8,128)(2,1)S(1)}, u32[]{:S(2)}, u32[]{:S(2)}) async-start(bf16[4,256,512]{2,1,0:T(8,128)(2,1)} %bitcast.12), calls=%async_computation.2 | async-start | bytes 2097152 | tf_op jit(solution)/shard_map/all_to_all | solution.py:289
  70.2 24.4 %collective-permute-start.8 = (bf16[2,256,512]{2,1,0:T(8,128)(2,1)}, bf16[2,256,512]{2,1,0:T(8,128)(2,1)S(1)}, u32[]{:S(2)}, u32[]{:S(2)}) collective-permute-start(bf16[2,256,512]{2,1,0:T(8,128)(2,1)} %get-tuple-element.39), channel_id=1, source_target_pairs={{0,1},{1,2},{2,3},{3,4},{4,5},{5,6},{6,7},{7,8},{8,9},{9,10},{10,1... | collective-permute-start | bytes 1572872 | tf_op jit(solution)/shard_map/ppermute | solution.py:271
  72.2 22.5 %collective-permute-start.9 = (bf16[2,256,512]{2,1,0:T(8,128)(2,1)}, bf16[2,256,512]{2,1,0:T(8,128)(2,1)S(1)}, u32[]{:S(2)}, u32[]{:S(2)}) collective-permute-start(bf16[2,256,512]{2,1,0:T(8,128)(2,1)} %get-tuple-element.40), channel_id=1, source_target_pairs={{1,0},{2,1},{3,2},{4,3},{5,4},{6,5},{7,6},{8,7},{9,8},{10,9},{11,1... | collective-permute-start | bytes 1572872 | tf_op jit(solution)/shard_map/ppermute | solution.py:271
  76.5 18.1 %all-to-all-start.3 = ((bf16[16,16,512]{2,1,0:T(8,128)(2,1)}), bf16[16,16,512]{2,1,0:T(8,128)(2,1)S(1)}, u32[]{:S(2)}, u32[]{:S(2)}) async-start(bf16[16,16,512]{2,1,0:T(8,128)(2,1)} %bitcast.13), calls=%async_computation.3 | async-start | bytes 524288 | tf_op jit(solution)/shard_map/all_to_all | solution.py:289
  89.3 21.1 %collective-permute-start.5 = (bf16[2,256,512]{2,1,0:T(8,128)(2,1)}, bf16[2,256,512]{2,1,0:T(8,128)(2,1)S(1)}, u32[]{:S(2)}, u32[]{:S(2)}) collective-permute-start(bf16[2,256,512]{2,1,0:T(8,128)(2,1)} %get-tuple-element.37), channel_id=1, source_target_pairs={{0,1},{1,2},{2,3},{3,4},{4,5},{5,6},{6,7},{7,8},{8,9},{9,10},{10,1... | collective-permute-start | bytes 1572872 | tf_op jit(solution)/shard_map/ppermute | solution.py:271
  92.4 18.0 %collective-permute-start.6 = (bf16[2,256,512]{2,1,0:T(8,128)(2,1)}, bf16[2,256,512]{2,1,0:T(8,128)(2,1)S(1)}, u32[]{:S(2)}, u32[]{:S(2)}) collective-permute-start(bf16[2,256,512]{2,1,0:T(8,128)(2,1)} %get-tuple-element.38), channel_id=1, source_target_pairs={{1,0},{2,1},{3,2},{4,3},{5,4},{6,5},{7,6},{8,7},{9,8},{10,9},{11,1... | collective-permute-start | bytes 1572872 | tf_op jit(solution)/shard_map/ppermute | solution.py:271
  94.7 13.6 %copy-start.5 = (bf16[2,256,512]{2,1,0:T(8,128)(2,1)}, bf16[2,256,512]{2,1,0:T(8,128)(2,1)S(1)}, u32[]{:S(2)}) copy-start(bf16[2,256,512]{2,1,0:T(8,128)(2,1)S(1)} %collective-permute-done.8.below_ref) | copy-start | bytes 1572868
  94.7 13.5 %copy-start.6 = (bf16[2,256,512]{2,1,0:T(8,128)(2,1)}, bf16[2,256,512]{2,1,0:T(8,128)(2,1)S(1)}, u32[]{:S(2)}) copy-start(bf16[2,256,512]{2,1,0:T(8,128)(2,1)S(1)} %collective-permute-done.9.above_ref) | copy-start | bytes 1572868
  95.4 25.3 %all-to-all-start.4 = ((bf16[8,16,512]{2,1,0:T(8,128)(2,1)}), bf16[8,16,512]{2,1,0:T(8,128)(2,1)S(1)}, u32[]{:S(2)}, u32[]{:S(2)}) async-start(bf16[8,16,512]{2,1,0:T(8,128)(2,1)} %broadcast_in_dim.22), calls=%async_computation.4 | async-start | bytes 262144 | tf_op jit(solution)/shard_map/all_to_all | solution.py:283
  110.4 0.8 copy-start.7
  110.4 1.0 copy-start.8

commit v9 on v8

--- a/solution.py
+++ b/solution.py
@@ -15,6 +15,7 @@
 PAIR = 2 * HEAD_DIM
 PPS = 2
 HALVES = 2
+SPLIT = 3
 SCALE = 1.0 / math.sqrt(HEAD_DIM)
 SPAN = 2 * REACH + 1
 DP = ("zh", "core")
@@ -183,9 +184,15 @@
                 high_ref[which, lon:, c] = far[4 * lon :].astype(BF)
 
 
-def half_specs(rows, steps, half):
+def part_pairs(width):
+    pairs = width // PAIR
+    first = pairs * SPLIT // 4
+    return ((0, first), (first, pairs - first))
+
+
+def half_specs(rows, begin, half):
     width = PPS * PAIR
-    flat = pl.BlockSpec((rows, width), lambda p: (0, p + half * steps))
+    flat = pl.BlockSpec((rows, width), lambda p: (0, p + begin // PPS))
     key = pl.BlockSpec((1, rows, width), lambda p: (0, 0, p))
     value = pl.BlockSpec((1, rows, width), lambda p: (1, 0, p))
     both = pl.BlockSpec((2, rows, width), lambda p: (0, 0, p))
@@ -195,10 +202,10 @@
 def forward(half, band, q, k, v, below, above, lon, previous):
     rows, width = q.shape
     cycles = rows // lon
-    pairs = width // PAIR // HALVES
+    begin, pairs = part_pairs(width)[half]
     steps = pairs // PPS
     smem = pl.BlockSpec(memory_space=pltpu.SMEM)
-    flat, key, value, _ = half_specs(rows, steps, half)
+    flat, key, value, _ = half_specs(rows, begin, half)
     operands = [*band, q, below, k, above, below, v, above]
     specs = [smem] * len(band) + [flat, key, flat, key, value, flat, value]
     return pl.pallas_call(
@@ -221,12 +228,12 @@
 def backward(half, q, g, o, probs, k, v, below, above, lon, previous):
     rows, width = q.shape
     cycles = rows // lon
-    pairs = width // PAIR // HALVES
+    begin, pairs = part_pairs(width)[half]
     steps = pairs // PPS
-    flat, key, value, both = half_specs(rows, steps, half)
+    flat, key, value, both = half_specs(rows, begin, half)
     prob = pl.BlockSpec((PPS, cycles, SPAN * lon, 2 * lon), lambda p: (p, 0, 0, 0))
     whole = jax.ShapeDtypeStruct((rows, width), BF)
-    edge = jax.ShapeDtypeStruct((2, rows, width // HALVES), BF)
+    edge = jax.ShapeDtypeStruct((2, rows, pairs * PAIR), BF)
     operands = [q, g, o, probs, below, k, above, below, v, above]
     specs = [flat, flat, flat, prob, key, flat, key, value, flat, value]
     return pl.pallas_call(
@@ -250,8 +257,9 @@
 
 def add_arrived(half, own_key, own_value, from_below, from_above):
     rows, width = own_key.shape
-    steps = width // HALVES // (PPS * PAIR)
-    flat, _, _, both = half_specs(rows, steps, half)
+    begin, pairs = part_pairs(width)[half]
+    steps = pairs // PPS
+    flat, _, _, both = half_specs(rows, begin, half)
     whole = jax.ShapeDtypeStruct((rows, width), BF)
     return pl.pallas_call(
         total_kernel,
@@ -303,8 +311,8 @@
     mine, others = core * half_width, (1 - core) * half_width
 
     parts = [
-        jnp.stack([k[:, n : n + width // HALVES], v[:, n : n + width // HALVES]])
-        for n in range(0, width, width // HALVES)
+        jnp.stack([k[:, n * PAIR : (n + m) * PAIR], v[:, n * PAIR : (n + m) * PAIR]])
+        for n, m in part_pairs(width)
     ]
     below = [lat_shift(part, 1) for part in parts]
     above = [lat_shift(part, -1) for part in parts]

time: 122 us -> 135 us (1.11)
  the two profiles are of different devices: /device:TPU:59 before, /device:TPU:1 now
where the time goes in v9:
time: 135 us; the launch traced here: 134 us
  starting transfers between devices  68.4 us (51%)
  Pallas kernels  26.7 us (20%)
  waiting for transfers between devices  19.9 us (15%)
  local copies, waits for them, and re-layouts  7.24 us (5%)
  matrix products  7.14 us (5%)
  other arithmetic  3.29 us (2%)
    all_to_all x2, starting transfers between devices, spread(): return lax.all_to_all(copies_of(value, axes), axes, 0, 0, tiled=True)  24.3 us
    ppermute x8, starting transfers between devices, lat_shift(): return lax.ppermute(value, LAT, pairs)  22 us
    pallas_call x2, Pallas kernels, backward(): pl.pallas_call(backward_kernel, grid=(steps,), in_specs=specs + [pl.Block...  11 us
    pallas_call x2, Pallas kernels, forward(): pl.pallas_call(forward_kernel, grid=(steps,), in_specs=specs + [pl.BlockS...  10.5 us
    all_to_all x2, waiting for transfers between devices, spread(): return lax.all_to_all(copies_of(value, axes), axes, 0, 0, tiled=True)  10.3 us
    all_to_all x2, starting transfers between devices, scatter_sum(): received = lax.all_to_all(blocks, axes, 0, 0, tiled=True)  9.92 us
    all_to_all x2, waiting for transfers between devices, scatter_sum(): received = lax.all_to_all(blocks, axes, 0, 0, tiled=True)  9.05 us
    ppermute x2, starting transfers between devices, core_swap(): return lax.ppermute(value, 'core', [(0, 1), (1, 0)])  7.88 us
  transfers between devices with their start and end apart: 15, of which 4 were waited for; matrix products, arithmetic and copies ran while one was open for 9% of the time, Pallas kernels for 20%

profile of v9, /device:TPU:1, one launch (start us, length us, event | category | flops | bytes accessed | tf_op | source)
XLA Modules:
  0.0 133.5 jit_solution(4585741694468719318)
XLA Ops:
  0.6 0.0 copy-start
  0.7 1.2 slice_bitcast_fusion
  1.9 1.0 pad_maximum_fusion
  2.8 4.1 %collective-permute-start.3 = (bf16[2,256,768]{2,1,0:T(8,128)(2,1)}, bf16[2,256,768]{2,1,0:T(8,128)(2,1)S(1)}, u32[]{:S(2)}, u32[]{:S(2)}) collective-permute-start(bf16[2,256,768]{2,1,0:T(8,128)(2,1)} %pad_maximum_fusion), channel_id=1, source_target_pairs={{0,1},{1,2},{2,3},{3,4},{4,5},{5,6},{6,7},{7,8},{8,9},{9,10},{10,1... | collective-permute-start | bytes 2359304 | tf_op jit(solution)/shard_map/ppermute | solution.py:279
  6.9 1.3 collective-permute-start.4
  8.3 0.7 broadcast_in_dim.8
  9.0 10.7 %all-to-all-start = ((bf16[16,16,512]{2,1,0:T(8,128)(2,1)}), bf16[16,16,512]{2,1,0:T(8,128)(2,1)S(1)}, u32[]{:S(2)}, u32[]{:S(2)}) async-start(bf16[16,16,512]{2,1,0:T(8,128)(2,1)} %broadcast_in_dim.8), calls=%async_computation | async-start | bytes 524288 | tf_op jit(solution)/shard_map/all_to_all | solution.py:291
  19.7 1.0 slice_bitcast_fusion.2
  20.7 0.7 pad_maximum_fusion.1
  21.4 3.3 %collective-permute-start.1 = (bf16[2,256,256]{2,1,0:T(8,128)(2,1)}, bf16[2,256,256]{2,1,0:T(8,128)(2,1)S(1)}, u32[]{:S(2)}, u32[]{:S(2)}) collective-permute-start(bf16[2,256,256]{2,1,0:T(8,128)(2,1)} %pad_maximum_fusion.1), channel_id=1, source_target_pairs={{0,1},{1,2},{2,3},{3,4},{4,5},{5,6},{6,7},{7,8},{8,9},{9,10},{10,1... | collective-permute-start | bytes 786440 | tf_op jit(solution)/shard_map/ppermute | solution.py:279
  24.7 1.3 collective-permute-start.2
  26.0 8.2 %all-to-all-done = bf16[16,16,512]{2,1,0:T(8,128)(2,1)S(1)} async-done(((bf16[16,16,512]{2,1,0:T(8,128)(2,1)}), bf16[16,16,512]{2,1,0:T(8,128)(2,1)S(1)}, u32[]{:S(2)}, u32[]{:S(2)}) %all-to-all-start) | async-done | bytes 262176 | tf_op jit(solution)/shard_map/all_to_all | solution.py:291
  34.2 1.1 broadcast_in_dim.10
  35.3 4.2 %all-to-all-start.1 = ((bf16[4,256,512]{2,1,0:T(8,128)(2,1)}), bf16[4,256,512]{2,1,0:T(8,128)(2,1)S(1)}, u32[]{:S(2)}, u32[]{:S(2)}) async-start(bf16[4,256,512]{2,1,0:T(8,128)(2,1)} %broadcast_in_dim.10), calls=%async_computation.1 | async-start | bytes 2097152 | tf_op jit(solution)/shard_map/all_to_all | solution.py:323
  39.5 0.0 collective-permute-done.4.kn_ref.vn_ref
  39.5 0.9 copy-done.2
  40.4 6.8 %attention_forward.2 = (bf16[256,1024]{1,0:T(8,128)(2,1)}, bf16[6,2,640,256]{3,2,1,0:T(8,128)(2,1)}) custom-call(s32[1]{0:T(128)} %bitcast.4.first_ref, s32[128]{0:T(128)} %lo_ref.3, s32[128]{0:T(128)} %hi_ref.3, s32[128]{0:T(128)} %half_ref.3, f32[128]{0:T(128)} %constant.41.clone.logw_ref, bf16[256,1024]{1,0:T(8,128)(2,1)} %bitcast.50, ...), custom_call_target="tpu_custom_call" | custom-call | flops 20000000000 | bytes 40000000 | tf_op jit(solution)/shard_map/attention_forward/pallas_call | solution.py:211
  47.2 0.0 collective-permute-done.1.kp_ref.vp_ref
  47.3 0.7 copy-done.3
  48.0 0.1 copy-done.4
  48.1 3.6 %attention_forward.3 = (bf16[256,1024]{1,0:T(8,128)(2,1)}, bf16[2,2,640,256]{3,2,1,0:T(8,128)(2,1)}) custom-call(s32[1]{0:T(128)} %bitcast.4.first_ref, s32[128]{0:T(128)} %lo_ref.3, s32[128]{0:T(128)} %hi_ref.3, s32[128]{0:T(128)} %half_ref.3, f32[128]{0:T(128)} %constant.41.clone.logw_ref, ...), custom_call_target="tpu_custom_call", output_to_operand_aliasing={{0}: (12, {})} | custom-call | flops 20000000000 | bytes 40000000 | tf_op jit(solution)/shard_map/attention_forward/pallas_call | solution.py:211
  51.7 2.7 %convolution_convert_fusion = bf16[1024,512]{1,0:T(8,128)(2,1)} fusion(bf16[256,1024]{1,0:T(8,128)(2,1)} %get-tuple-element.30.o_ref, bf16[256,1024]{1,0:T(8,128)(2,1)S(1)} %bitcast.32, s32[]{:T(128)S(6)} %select_n.8), kind=kOutput, calls=%fused_computation.1 | convolution fusion | flops 268959744 | bytes 1835012 | tf_op jit(solution)/shard_map/dot_general | solution.py:32
  54.4 6.0 %collective-permute-start.7 = (bf16[1024,512]{1,0:T(8,128)(2,1)}, bf16[1024,512]{1,0:T(8,128)(2,1)S(1)}, u32[]{:S(2)}, u32[]{:S(2)}) collective-permute-start(bf16[1024,512]{1,0:T(8,128)(2,1)} %convolution_convert_fusion), channel_id=1, source_target_pairs={{0,64},{64,0},{1,65},{65,1},{2,66},{66,2},{3,67},{67,3},{4,68},{68... | collective-permute-start | bytes 3145736 | tf_op jit(solution)/shard_map/ppermute | solution.py:283
  60.3 0.0 all-to-all-done.1
  60.4 1.9 %collective-permute-start = (bf16[1024,512]{1,0:T(8,128)(2,1)S(1)}, bf16[1024,512]{1,0:T(8,128)(2,1)}, u32[]{:S(2)}, u32[]{:S(2)}) collective-permute-start(bf16[1024,512]{1,0:T(8,128)(2,1)S(1)} %bitcast.48), channel_id=1, source_target_pairs={{0,64},{64,0},{1,65},{65,1},{2,66},{66,2},{3,67},{67,3},{4,68},{68... | collective-permute-start | bytes 3145736 | tf_op jit(solution)/shard_map/ppermute | solution.py:283
  62.3 0.5 collective-permute-done.7
  62.8 1.5 %add_convert_fusion = bf16[1024,512]{1,0:T(8,128)(2,1)} fusion(bf16[1024,512]{1,0:T(8,128)(2,1)S(1)} %collective-permute-done.7, bf16[256,1024]{1,0:T(8,128)(2,1)S(1)} %copy-done.1, bf16[256,1024]{1,0:T(8,128)(2,1)S(1)} %bitcast.33, s32[]{:T(128)S(6)} %select_n.7), kind=kOutput, calls=%fused_computation | convolution fusion | flops 270008320 | bytes 2883588 | tf_op jit(solution)/shard_map/dot_general | solution.py:32
  64.3 4.5 %all-to-all-start.2 = ((bf16[4,256,512]{2,1,0:T(8,128)(2,1)}), bf16[4,256,512]{2,1,0:T(8,128)(2,1)S(1)}, u32[]{:S(2)}, u32[]{:S(2)}) async-start(bf16[4,256,512]{2,1,0:T(8,128)(2,1)} %bitcast.12), calls=%async_computation.2 | async-start | bytes 2097152 | tf_op jit(solution)/shard_map/all_to_all | solution.py:297
  68.8 0.5 fusion.4
  69.3 0.0 collective-permute-done
  69.3 2.6 %fusion.g_ref = bf16[256,1024]{1,0:T(8,128)(2,1)} fusion(f32[256,1024]{1,0:T(8,128)S(1)} %fusion.4, bf16[1024,512]{1,0:T(8,128)(2,1)} %collective-permute-done, bf16[256,1024]{1,0:T(8,128)(2,1)S(1)} %bitcast.31, s32[]{:T(128)S(6)} %select_n.8), kind=kOutput, calls=%fused_computation.3 | convolution fusion | flops 268959744 | bytes 2883588 | tf_op jit(solution)/shard_map/dot_general | solution.py:32
  71.8 7.2 %attention_backward.2 = (bf16[256,1024]{1,0:T(8,128)(2,1)}, bf16[256,1024]{1,0:T(8,128)(2,1)}, bf16[256,1024]{1,0:T(8,128)(2,1)}, bf16[2,256,768]{2,1,0:T(8,128)(2,1)}, bf16[2,256,768]{2,1,0:T(8,128)(2,1)}) custom-call(bf16[256,1024]{1,0:T(8,128)(2,1)} %bitcast.52, bf16[256,1024]{1,0:T(8,128)(2,1)} %fusion.g_ref, bf16[256,1024]{1,0:T(8,128)(2,1)} %get-tuple-element.30.o_ref, ...), custom_call_target="tpu_custom_call" | custom-call | flops 1000000 | bytes 100000 | tf_op jit(solution)/shard_map/attention_backward/pallas_call | solution.py:239
  79.0 6.3 %collective-permute-start.8 = (bf16[2,256,768]{2,1,0:T(8,128)(2,1)}, bf16[2,256,768]{2,1,0:T(8,128)(2,1)S(1)}, u32[]{:S(2)}, u32[]{:S(2)}) collective-permute-start(bf16[2,256,768]{2,1,0:T(8,128)(2,1)} %get-tuple-element.39), channel_id=1, source_target_pairs={{0,1},{1,2},{2,3},{3,4},{4,5},{5,6},{6,7},{7,8},{8,9},{9,10},{10,1... | collective-permute-start | bytes 2359304 | tf_op jit(solution)/shard_map/ppermute | solution.py:279
  85.3 1.3 collective-permute-start.9
  86.6 0.9 reduce_sum.33
  87.5 5.4 %all-to-all-start.3 = ((bf16[16,16,512]{2,1,0:T(8,128)(2,1)}), bf16[16,16,512]{2,1,0:T(8,128)(2,1)S(1)}, u32[]{:S(2)}, u32[]{:S(2)}) async-start(bf16[16,16,512]{2,1,0:T(8,128)(2,1)} %bitcast.13), calls=%async_computation.3 | async-start | bytes 524288 | tf_op jit(solution)/shard_map/all_to_all | solution.py:297
  92.9 3.8 %attention_backward.3 = (bf16[256,1024]{1,0:T(8,128)(2,1)}, bf16[256,1024]{1,0:T(8,128)(2,1)}, bf16[256,1024]{1,0:T(8,128)(2,1)}, bf16[2,256,256]{2,1,0:T(8,128)(2,1)}, bf16[2,256,256]{2,1,0:T(8,128)(2,1)}) custom-call(bf16[256,1024]{1,0:T(8,128)(2,1)} %bitcast.53, ...), custom_call_target="tpu_custom_call", output_to_operand_aliasing={{0}: (10, {}), {1}: (11, {}), {2}: (12, {})} | custom-call | flops 1000000 | bytes 100000 | tf_op jit(solution)/shard_map/attention_backward/pallas_call | solution.py:239
  96.8 3.3 %collective-permute-start.5 = (bf16[2,256,256]{2,1,0:T(8,128)(2,1)}, bf16[2,256,256]{2,1,0:T(8,128)(2,1)S(1)}, u32[]{:S(2)}, u32[]{:S(2)}) collective-permute-start(bf16[2,256,256]{2,1,0:T(8,128)(2,1)} %get-tuple-element.37), channel_id=1, source_target_pairs={{0,1},{1,2},{2,3},{3,4},{4,5},{5,6},{6,7},{7,8},{8,9},{9,10},{10,1... | collective-permute-start | bytes 786440 | tf_op jit(solution)/shard_map/ppermute | solution.py:279
  100.0 1.3 collective-permute-start.6
  101.3 9.0 %all-to-all-done.3 = bf16[16,16,512]{2,1,0:T(8,128)(2,1)S(1)} async-done(((bf16[16,16,512]{2,1,0:T(8,128)(2,1)}), bf16[16,16,512]{2,1,0:T(8,128)(2,1)S(1)}, u32[]{:S(2)}, u32[]{:S(2)}) %all-to-all-start.3) | async-done | bytes 262176 | tf_op jit(solution)/shard_map/all_to_all | solution.py:297
  110.5 0.7 broadcast_in_dim.22
  111.2 13.6 %all-to-all-start.4 = ((bf16[8,16,512]{2,1,0:T(8,128)(2,1)}), bf16[8,16,512]{2,1,0:T(8,128)(2,1)S(1)}, u32[]{:S(2)}, u32[]{:S(2)}) async-start(bf16[8,16,512]{2,1,0:T(8,128)(2,1)} %broadcast_in_dim.22), calls=%async_computation.4 | async-start | bytes 262144 | tf_op jit(solution)/shard_map/all_to_all | solution.py:291
  124.8 3.3 %add_arrived.2 = (bf16[256,1024]{1,0:T(8,128)(2,1)}, bf16[256,1024]{1,0:T(8,128)(2,1)}) custom-call(bf16[2,256,768]{2,1,0:T(8,128)(2,1)} %copy-done.5, bf16[2,256,768]{2,1,0:T(8,128)(2,1)} %collective-permute-done.9.above_ref, bf16[256,1024]{1,0:T(8,128)(2,1)} %get-tuple-element.43.own_key_ref, ...), custom_call_target="tpu_custom_call", output_to_operand_aliasing={{0}: (2, {}), {1}: (3, {})} | custom-call | flops 1000000 | bytes 100000 | tf_op jit(solution)/shard_map/add_arrived/pallas_call | solution.py:264
  128.1 0.7 copy-done.6
  128.8 0.1 copy-done.7
  128.9 1.9 %add_arrived.3 = (bf16[256,1024]{1,0:T(8,128)(2,1)}, bf16[256,1024]{1,0:T(8,128)(2,1)}) custom-call(bf16[2,256,256]{2,1,0:T(8,128)(2,1)} %copy-done.6, bf16[2,256,256]{2,1,0:T(8,128)(2,1)} %copy-done.7, bf16[256,1024]{1,0:T(8,128)(2,1)} %get-tuple-element.45.own_key_ref, ...), custom_call_target="tpu_custom_call", output_to_operand_aliasing={{0}: (2, {}), {1}: (3, {})} | custom-call | flops 1000000 | bytes 100000 | tf_op jit(solution)/shard_map/add_arrived/pallas_call | solution.py:264
  130.8 2.1 %all-to-all-done.4 = bf16[8,16,512]{2,1,0:T(8,128)(2,1)S(1)} async-done(((bf16[8,16,512]{2,1,0:T(8,128)(2,1)}), bf16[8,16,512]{2,1,0:T(8,128)(2,1)S(1)}, u32[]{:S(2)}, u32[]{:S(2)}) %all-to-all-start.4) | async-done | bytes 131104 | tf_op jit(solution)/shard_map/all_to_all | solution.py:291
  132.9 0.6 maximum_multiply_fusion
  (23 shorter events, 0.1 us)
Async XLA Ops:
  0.6 51.1 %copy-start = (bf16[1,2,128,1024]{3,2,1,0:T(8,128)(2,1)S(1)}, bf16[1,2,128,1024]{3,2,1,0:T(8,128)(2,1)}, u32[]{:S(2)}) copy-start(bf16[1,2,128,1024]{3,2,1,0:T(8,128)(2,1)} %param.12) | copy-start | bytes 1572868
  0.6 7.6 %copy-start.8 = (bf16[16,1024]{1,0:T(8,128)(2,1)S(1)}, bf16[16,1024]{1,0:T(8,128)(2,1)}, u32[]{:S(2)}) copy-start(bf16[16,1024]{1,0:T(8,128)(2,1)} %param.13) | copy-start | bytes 98308
  2.8 36.7 %collective-permute-start.3 = (bf16[2,256,768]{2,1,0:T(8,128)(2,1)}, bf16[2,256,768]{2,1,0:T(8,128)(2,1)S(1)}, u32[]{:S(2)}, u32[]{:S(2)}) collective-permute-start(bf16[2,256,768]{2,1,0:T(8,128)(2,1)} %pad_maximum_fusion), channel_id=1, source_target_pairs={{0,1},{1,2},{2,3},{3,4},{4,5},{5,6},{6,7},{7,8},{8,9},{9,10},{10,1... | collective-permute-start | bytes 2359304 | tf_op jit(solution)/shard_map/ppermute | solution.py:279
  6.9 32.6 %collective-permute-start.4 = (bf16[2,256,768]{2,1,0:T(8,128)(2,1)}, bf16[2,256,768]{2,1,0:T(8,128)(2,1)}, u32[]{:S(2)}, u32[]{:S(2)}) collective-permute-start(bf16[2,256,768]{2,1,0:T(8,128)(2,1)} %pad_maximum_fusion), channel_id=1, source_target_pairs={{1,0},{2,1},{3,2},{4,3},{5,4},{6,5},{7,6},{8,7},{9,8},{10,9},{11,1... | collective-permute-start | bytes 2359304 | tf_op jit(solution)/shard_map/ppermute | solution.py:279
  9.0 25.2 %all-to-all-start = ((bf16[16,16,512]{2,1,0:T(8,128)(2,1)}), bf16[16,16,512]{2,1,0:T(8,128)(2,1)S(1)}, u32[]{:S(2)}, u32[]{:S(2)}) async-start(bf16[16,16,512]{2,1,0:T(8,128)(2,1)} %broadcast_in_dim.8), calls=%async_computation | async-start | bytes 524288 | tf_op jit(solution)/shard_map/all_to_all | solution.py:291
  21.4 25.8 %collective-permute-start.1 = (bf16[2,256,256]{2,1,0:T(8,128)(2,1)}, bf16[2,256,256]{2,1,0:T(8,128)(2,1)S(1)}, u32[]{:S(2)}, u32[]{:S(2)}) collective-permute-start(bf16[2,256,256]{2,1,0:T(8,128)(2,1)} %pad_maximum_fusion.1), channel_id=1, source_target_pairs={{0,1},{1,2},{2,3},{3,4},{4,5},{5,6},{6,7},{7,8},{8,9},{9,10},{10,1... | collective-permute-start | bytes 786440 | tf_op jit(solution)/shard_map/ppermute | solution.py:279
  24.7 22.6 %collective-permute-start.2 = (bf16[2,256,256]{2,1,0:T(8,128)(2,1)}, bf16[2,256,256]{2,1,0:T(8,128)(2,1)S(1)}, u32[]{:S(2)}, u32[]{:S(2)}) collective-permute-start(bf16[2,256,256]{2,1,0:T(8,128)(2,1)} %pad_maximum_fusion.1), channel_id=1, source_target_pairs={{1,0},{2,1},{3,2},{4,3},{5,4},{6,5},{7,6},{8,7},{9,8},{10,9},{11,1... | collective-permute-start | bytes 786440 | tf_op jit(solution)/shard_map/ppermute | solution.py:279
  35.3 25.1 %all-to-all-start.1 = ((bf16[4,256,512]{2,1,0:T(8,128)(2,1)}), bf16[4,256,512]{2,1,0:T(8,128)(2,1)S(1)}, u32[]{:S(2)}, u32[]{:S(2)}) async-start(bf16[4,256,512]{2,1,0:T(8,128)(2,1)} %broadcast_in_dim.10), calls=%async_computation.1 | async-start | bytes 2097152 | tf_op jit(solution)/shard_map/all_to_all | solution.py:323
  39.5 0.9 copy-start.2
  47.3 0.7 copy-start.3
  47.3 0.8 copy-start.4
  51.7 11.1 %copy-start.1 = (bf16[256,1024]{1,0:T(8,128)(2,1)S(1)}, bf16[256,1024]{1,0:T(8,128)(2,1)}, u32[]{:S(2)}) copy-start(bf16[256,1024]{1,0:T(8,128)(2,1)} %get-tuple-element.30.o_ref) | copy-start | bytes 1572868
  54.4 8.4 %collective-permute-start.7 = (bf16[1024,512]{1,0:T(8,128)(2,1)}, bf16[1024,512]{1,0:T(8,128)(2,1)S(1)}, u32[]{:S(2)}, u32[]{:S(2)}) collective-permute-start(bf16[1024,512]{1,0:T(8,128)(2,1)} %convolution_convert_fusion), channel_id=1, source_target_pairs={{0,64},{64,0},{1,65},{65,1},{2,66},{66,2},{3,67},{67,3},{4,68},{68... | collective-permute-start | bytes 3145736 | tf_op jit(solution)/shard_map/ppermute | solution.py:283
  60.4 8.9 %collective-permute-start = (bf16[1024,512]{1,0:T(8,128)(2,1)S(1)}, bf16[1024,512]{1,0:T(8,128)(2,1)}, u32[]{:S(2)}, u32[]{:S(2)}) collective-permute-start(bf16[1024,512]{1,0:T(8,128)(2,1)S(1)} %bitcast.48), channel_id=1, source_target_pairs={{0,64},{64,0},{1,65},{65,1},{2,66},{66,2},{3,67},{67,3},{4,68},{68... | collective-permute-start | bytes 3145736 | tf_op jit(solution)/shard_map/ppermute | solution.py:283
  64.3 22.3 %all-to-all-start.2 = ((bf16[4,256,512]{2,1,0:T(8,128)(2,1)}), bf16[4,256,512]{2,1,0:T(8,128)(2,1)S(1)}, u32[]{:S(2)}, u32[]{:S(2)}) async-start(bf16[4,256,512]{2,1,0:T(8,128)(2,1)} %bitcast.12), calls=%async_computation.2 | async-start | bytes 2097152 | tf_op jit(solution)/shard_map/all_to_all | solution.py:297
  79.0 31.4 %collective-permute-start.8 = (bf16[2,256,768]{2,1,0:T(8,128)(2,1)}, bf16[2,256,768]{2,1,0:T(8,128)(2,1)S(1)}, u32[]{:S(2)}, u32[]{:S(2)}) collective-permute-start(bf16[2,256,768]{2,1,0:T(8,128)(2,1)} %get-tuple-element.39), channel_id=1, source_target_pairs={{0,1},{1,2},{2,3},{3,4},{4,5},{5,6},{6,7},{7,8},{8,9},{9,10},{10,1... | collective-permute-start | bytes 2359304 | tf_op jit(solution)/shard_map/ppermute | solution.py:279
  85.3 25.1 %collective-permute-start.9 = (bf16[2,256,768]{2,1,0:T(8,128)(2,1)}, bf16[2,256,768]{2,1,0:T(8,128)(2,1)}, u32[]{:S(2)}, u32[]{:S(2)}) collective-permute-start(bf16[2,256,768]{2,1,0:T(8,128)(2,1)} %get-tuple-element.40), channel_id=1, source_target_pairs={{1,0},{2,1},{3,2},{4,3},{5,4},{6,5},{7,6},{8,7},{9,8},{10,9},{11,1... | collective-permute-start | bytes 2359304 | tf_op jit(solution)/shard_map/ppermute | solution.py:279
  87.5 22.9 %all-to-all-start.3 = ((bf16[16,16,512]{2,1,0:T(8,128)(2,1)}), bf16[16,16,512]{2,1,0:T(8,128)(2,1)S(1)}, u32[]{:S(2)}, u32[]{:S(2)}) async-start(bf16[16,16,512]{2,1,0:T(8,128)(2,1)} %bitcast.13), calls=%async_computation.3 | async-start | bytes 524288 | tf_op jit(solution)/shard_map/all_to_all | solution.py:297
  96.8 31.3 %collective-permute-start.5 = (bf16[2,256,256]{2,1,0:T(8,128)(2,1)}, bf16[2,256,256]{2,1,0:T(8,128)(2,1)S(1)}, u32[]{:S(2)}, u32[]{:S(2)}) collective-permute-start(bf16[2,256,256]{2,1,0:T(8,128)(2,1)} %get-tuple-element.37), channel_id=1, source_target_pairs={{0,1},{1,2},{2,3},{3,4},{4,5},{5,6},{6,7},{7,8},{8,9},{9,10},{10,1... | collective-permute-start | bytes 786440 | tf_op jit(solution)/shard_map/ppermute | solution.py:279
  100.0 28.1 %collective-permute-start.6 = (bf16[2,256,256]{2,1,0:T(8,128)(2,1)}, bf16[2,256,256]{2,1,0:T(8,128)(2,1)S(1)}, u32[]{:S(2)}, u32[]{:S(2)}) collective-permute-start(bf16[2,256,256]{2,1,0:T(8,128)(2,1)} %get-tuple-element.38), channel_id=1, source_target_pairs={{1,0},{2,1},{3,2},{4,3},{5,4},{6,5},{7,6},{8,7},{9,8},{10,9},{11,1... | collective-permute-start | bytes 786440 | tf_op jit(solution)/shard_map/ppermute | solution.py:279
  110.4 14.4 %copy-start.5 = (bf16[2,256,768]{2,1,0:T(8,128)(2,1)}, bf16[2,256,768]{2,1,0:T(8,128)(2,1)S(1)}, u32[]{:S(2)}) copy-start(bf16[2,256,768]{2,1,0:T(8,128)(2,1)S(1)} %collective-permute-done.8.below_ref) | copy-start | bytes 2359300
  111.2 21.7 %all-to-all-start.4 = ((bf16[8,16,512]{2,1,0:T(8,128)(2,1)}), bf16[8,16,512]{2,1,0:T(8,128)(2,1)S(1)}, u32[]{:S(2)}, u32[]{:S(2)}) async-start(bf16[8,16,512]{2,1,0:T(8,128)(2,1)} %broadcast_in_dim.22), calls=%async_computation.4 | async-start | bytes 262144 | tf_op jit(solution)/shard_map/all_to_all | solution.py:291
  128.1 0.7 copy-start.6
  128.1 0.8 copy-start.7

commit v10 on v8

--- a/solution.py
+++ b/solution.py
@@ -22,7 +22,7 @@
 LAT = ("x", "zl", "y")
 BF = jnp.bfloat16
 F32 = jnp.float32
-VMEM_LIMIT = 60*1024*1024
+VMEM_LIMIT = 32 * 1024 * 1024
 LARGE = pl.CostEstimate(flops=2*10**10, bytes_accessed=4*10**7, transcendentals=0)
 SMALL = pl.CostEstimate(flops=10**6, bytes_accessed=10**5, transcendentals=0)
 

time: 122 us -> 125 us (1.025)
  local copies, waits for them, and re-layouts: 6.59 us -> 10.7 us
  Pallas kernels: 25.6 us -> 21.6 us
  waiting for transfers between devices: 11.6 us -> 13.4 us
  other arithmetic: 3.29 us -> 4.54 us
    unnamed x20 -> x38, local copies, waits for them, and re-layouts: 2.75 us -> 6.94 us
    pallas_call x2, Pallas kernels: 10.5 us -> 8.21 us  [forward(): pl.pallas_call(forward_kernel, grid=(steps,), in_specs=specs + [pl.BlockS...]
    pallas_call x2, Pallas kernels: 10.9 us -> 9.16 us  [backward(): pl.pallas_call(backward_kernel, grid=(steps,), in_specs=specs + [pl.Block...]
    all_to_all x2, waiting for transfers between devices: 11 us -> 12.5 us  [spread(): return lax.all_to_all(copies_of(value, axes), axes, 0, 0, tiled=True)]
    all_to_all x2, starting transfers between devices: 22.2 us -> 20.7 us  [spread(): return lax.all_to_all(copies_of(value, axes), axes, 0, 0, tiled=True)]
  transfers between devices with their start and end apart: 15 -> 15, of which waited for: 3 -> 4; matrix products, arithmetic and copies ran while one was open for 9% -> 11% of each run, Pallas kernels for 21% -> 17%
where the time goes in v10:
time: 125 us; the launch traced here: 124 us
  starting transfers between devices  65.1 us (52%)
  Pallas kernels  21.6 us (17%)
  waiting for transfers between devices  13.4 us (11%)
  local copies, waits for them, and re-layouts  10.7 us (9%)
  matrix products  7.84 us (6%)
  other arithmetic  4.54 us (4%)
    ppermute x8, starting transfers between devices, lat_shift(): return lax.ppermute(value, LAT, pairs)  21.2 us
    all_to_all x2, starting transfers between devices, spread(): return lax.all_to_all(copies_of(value, axes), axes, 0, 0, tiled=True)  20.7 us
    all_to_all x2, waiting for transfers between devices, spread(): return lax.all_to_all(copies_of(value, axes), axes, 0, 0, tiled=True)  12.5 us
    all_to_all x2, starting transfers between devices, scatter_sum(): received = lax.all_to_all(blocks, axes, 0, 0, tiled=True)  11.8 us
    pallas_call x2, Pallas kernels, backward(): pl.pallas_call(backward_kernel, grid=(steps,), in_specs=specs + [pl.Block...  9.16 us
    pallas_call x2, Pallas kernels, forward(): pl.pallas_call(forward_kernel, grid=(steps,), in_specs=specs + [pl.BlockS...  8.21 us
    dot_general x4, matrix products, dot(): return lax.dot_general(a, b, (dims, ((), ())), preferred_element_type=F32)  7.84 us
    unnamed x38, local copies, waits for them, and re-layouts  6.94 us
  transfers between devices with their start and end apart: 15, of which 4 were waited for; matrix products, arithmetic and copies ran while one was open for 11% of the time, Pallas kernels for 17%

profile of v10, /device:TPU:59, one launch (start us, length us, event | category | flops | bytes accessed | tf_op | source)
XLA Modules:
  0.0 124.3 jit_solution(1929261646829870453)
XLA Ops:
  0.6 0.0 copy-start
  0.7 1.3 %slice_bitcast_fusion = (bf16[1,256,512]{2,1,0:T(8,128)(2,1)S(1)}, bf16[1,256,512]{2,1,0:T(8,128)(2,1)S(1)}, bf16[1,256,512]{2,1,0:T(8,128)(2,1)S(1)}, bf16[1,256,512]{2,1,0:T(8,128)(2,1)S(1)}) fusion(bf16[256,1024]{1,0:T(8,128)(2,1)} %bitcast.34, bf16[256,1024]{1,0:T(8,128)(2,1)} %bitcast.39), kind=kLoop, calls=%fused_computation.6 | loop fusion | bytes 2097152 | tf_op jit(solution)/shard_map/stack | solution.py:306
  2.0 0.8 pad_maximum_fusion.1
  2.8 3.2 %collective-permute-start.3 = (bf16[2,256,512]{2,1,0:T(8,128)(2,1)}, bf16[2,256,512]{2,1,0:T(8,128)(2,1)S(1)}, u32[]{:S(2)}, u32[]{:S(2)}) collective-permute-start(bf16[2,256,512]{2,1,0:T(8,128)(2,1)} %pad_maximum_fusion.1), channel_id=1, source_target_pairs={{0,1},{1,2},{2,3},{3,4},{4,5},{5,6},{6,7},{7,8},{8,9},{9,10},{10,1... | collective-permute-start | bytes 1572872 | tf_op jit(solution)/shard_map/ppermute | solution.py:271
  6.0 2.1 %collective-permute-start.4 = (bf16[2,256,512]{2,1,0:T(8,128)(2,1)}, bf16[2,256,512]{2,1,0:T(8,128)(2,1)S(1)}, u32[]{:S(2)}, u32[]{:S(2)}) collective-permute-start(bf16[2,256,512]{2,1,0:T(8,128)(2,1)} %pad_maximum_fusion.1), channel_id=1, source_target_pairs={{1,0},{2,1},{3,2},{4,3},{5,4},{6,5},{7,6},{8,7},{9,8},{10,9},{11,1... | collective-permute-start | bytes 1572872 | tf_op jit(solution)/shard_map/ppermute | solution.py:271
  8.2 0.7 broadcast_in_dim.8
  8.9 9.3 %all-to-all-start = ((bf16[16,16,512]{2,1,0:T(8,128)(2,1)}), bf16[16,16,512]{2,1,0:T(8,128)(2,1)S(1)}, u32[]{:S(2)}, u32[]{:S(2)}) async-start(bf16[16,16,512]{2,1,0:T(8,128)(2,1)} %broadcast_in_dim.8), calls=%async_computation | async-start | bytes 524288 | tf_op jit(solution)/shard_map/all_to_all | solution.py:283
  18.2 0.0 copy-start.12
  18.3 0.0 copy-start.13
  18.3 0.0 copy-start.15
  18.3 0.8 pad_maximum_fusion
  19.1 3.1 %collective-permute-start.1 = (bf16[2,256,512]{2,1,0:T(8,128)(2,1)}, bf16[2,256,512]{2,1,0:T(8,128)(2,1)}, u32[]{:S(2)}, u32[]{:S(2)}) collective-permute-start(bf16[2,256,512]{2,1,0:T(8,128)(2,1)} %pad_maximum_fusion), channel_id=1, source_target_pairs={{0,1},{1,2},{2,3},{3,4},{4,5},{5,6},{6,7},{7,8},{8,9},{9,10},{10,1... | collective-permute-start | bytes 1572872 | tf_op jit(solution)/shard_map/ppermute | solution.py:271
  22.2 2.2 %collective-permute-start.2 = (bf16[2,256,512]{2,1,0:T(8,128)(2,1)}, bf16[2,256,512]{2,1,0:T(8,128)(2,1)}, u32[]{:S(2)}, u32[]{:S(2)}) collective-permute-start(bf16[2,256,512]{2,1,0:T(8,128)(2,1)} %pad_maximum_fusion), channel_id=1, source_target_pairs={{1,0},{2,1},{3,2},{4,3},{5,4},{6,5},{7,6},{8,7},{9,8},{10,9},{11,1... | collective-permute-start | bytes 1572872 | tf_op jit(solution)/shard_map/ppermute | solution.py:271
  24.4 3.7 %all-to-all-done = bf16[16,16,512]{2,1,0:T(8,128)(2,1)S(1)} async-done(((bf16[16,16,512]{2,1,0:T(8,128)(2,1)}), bf16[16,16,512]{2,1,0:T(8,128)(2,1)S(1)}, u32[]{:S(2)}, u32[]{:S(2)}) %all-to-all-start) | async-done | bytes 262176 | tf_op jit(solution)/shard_map/all_to_all | solution.py:283
  28.2 1.0 broadcast_in_dim.10
  29.2 4.5 %all-to-all-start.1 = ((bf16[4,256,512]{2,1,0:T(8,128)(2,1)}), bf16[4,256,512]{2,1,0:T(8,128)(2,1)}, u32[]{:S(2)}, u32[]{:S(2)}) async-start(bf16[4,256,512]{2,1,0:T(8,128)(2,1)} %broadcast_in_dim.10), calls=%async_computation.1 | async-start | bytes 2097152 | tf_op jit(solution)/shard_map/all_to_all | solution.py:315
  33.7 0.0 copy-start.9
  33.7 1.2 copy-done.9
  34.9 3.9 %attention_forward.2 = (bf16[256,1024]{1,0:T(8,128)(2,1)S(1)}, bf16[4,2,640,256]{3,2,1,0:T(8,128)(2,1)S(1)}) custom-call(s32[1]{0:T(128)} %bitcast.4.first_ref, s32[128]{0:T(128)S(1)} %copy-done.12, s32[128]{0:T(128)S(1)} %copy-done.13, s32[128]{0:T(128)S(1)} %copy-done.14, f32[128]{0:T(128)S(1)} %copy-done.15, bf16[256,1024]{1,0:T(8,128)(2,1)S(1)} %bitcast.44, ...), custom_call_target="tpu_custom_call" | custom-call | flops 20000000000 | bytes 40000000 | tf_op jit(solution)/shard_map/attention_forward/pallas_call | solution.py:204
  38.8 1.5 %copy-done.3 = bf16[4,2,640,256]{3,2,1,0:T(8,128)(2,1)} copy-done((bf16[4,2,640,256]{3,2,1,0:T(8,128)(2,1)}, bf16[4,2,640,256]{3,2,1,0:T(8,128)(2,1)S(1)}, u32[]{:S(2)}) %copy-start.3) | copy-done | bytes 2621464
  40.3 4.3 %attention_forward.3 = (bf16[256,1024]{1,0:T(8,128)(2,1)S(1)}, bf16[4,2,640,256]{3,2,1,0:T(8,128)(2,1)S(1)}) custom-call(s32[1]{0:T(128)} %bitcast.4.first_ref, s32[128]{0:T(128)S(1)} %copy-done.12, s32[128]{0:T(128)S(1)} %copy-done.13, s32[128]{0:T(128)S(1)} %copy-done.14, f32[128]{0:T(128)S(1)} %copy-done.15, ...), custom_call_target="tpu_custom_call", output_to_operand_aliasing={{0}: (12, {})} | custom-call | flops 20000000000 | bytes 40000000 | tf_op jit(solution)/shard_map/attention_forward/pallas_call | solution.py:204
  44.7 1.5 %copy-done.5 = bf16[4,2,640,256]{3,2,1,0:T(8,128)(2,1)} copy-done((bf16[4,2,640,256]{3,2,1,0:T(8,128)(2,1)}, bf16[4,2,640,256]{3,2,1,0:T(8,128)(2,1)S(1)}, u32[]{:S(2)}) %copy-start.5) | copy-done | bytes 2621464
  46.2 1.5 %convolution_convert_fusion = bf16[1024,512]{1,0:T(8,128)(2,1)} fusion(bf16[256,1024]{1,0:T(8,128)(2,1)S(1)} %get-tuple-element.30.o_ref, bf16[256,1024]{1,0:T(8,128)(2,1)S(1)} %bitcast.32, s32[]{:T(128)S(6)} %select_n.8), kind=kOutput, calls=%fused_computation.1 | convolution fusion | flops 268959744 | bytes 1835012 | tf_op jit(solution)/shard_map/dot_general | solution.py:31
  47.7 4.9 %collective-permute-start.7 = (bf16[1024,512]{1,0:T(8,128)(2,1)}, bf16[1024,512]{1,0:T(8,128)(2,1)}, u32[]{:S(2)}, u32[]{:S(2)}) collective-permute-start(bf16[1024,512]{1,0:T(8,128)(2,1)} %convolution_convert_fusion), channel_id=1, source_target_pairs={{0,64},{64,0},{1,65},{65,1},{2,66},{66,2},{3,67},{67,3},{4,68},{68... | collective-permute-start | bytes 3145736 | tf_op jit(solution)/shard_map/ppermute | solution.py:275
  52.7 1.9 %collective-permute-start = (bf16[1024,512]{1,0:T(8,128)(2,1)}, bf16[1024,512]{1,0:T(8,128)(2,1)}, u32[]{:S(2)}, u32[]{:S(2)}) collective-permute-start(bf16[1024,512]{1,0:T(8,128)(2,1)} %bitcast.3), channel_id=1, source_target_pairs={{0,64},{64,0},{1,65},{65,1},{2,66},{66,2},{3,67},{67,3},{4,68},{68... | collective-permute-start | bytes 3145736 | tf_op jit(solution)/shard_map/ppermute | solution.py:275
  54.6 0.7 collective-permute-done.7
  55.3 2.8 %add_convert_fusion = bf16[1024,512]{1,0:T(8,128)(2,1)} fusion(bf16[1024,512]{1,0:T(8,128)(2,1)} %collective-permute-done.7, bf16[256,1024]{1,0:T(8,128)(2,1)S(1)} %get-tuple-element.30.o_ref, bf16[256,1024]{1,0:T(8,128)(2,1)S(1)} %bitcast.33, s32[]{:T(128)S(6)} %select_n.7), kind=kOutput, calls=%fused_computation | convolution fusion | flops 270008320 | bytes 2883588 | tf_op jit(solution)/shard_map/dot_general | solution.py:31
  58.0 4.2 %all-to-all-start.2 = ((bf16[4,256,512]{2,1,0:T(8,128)(2,1)}), bf16[4,256,512]{2,1,0:T(8,128)(2,1)}, u32[]{:S(2)}, u32[]{:S(2)}) async-start(bf16[4,256,512]{2,1,0:T(8,128)(2,1)} %bitcast.50), calls=%async_computation.2 | async-start | bytes 2097152 | tf_op jit(solution)/shard_map/all_to_all | solution.py:289
  62.3 1.8 %fusion.4 = f32[256,1024]{1,0:T(8,128)S(1)} fusion(bf16[1024,512]{1,0:T(8,128)(2,1)} %bitcast.3, bf16[256,1024]{1,0:T(8,128)(2,1)S(1)} %bitcast.30, s32[]{:T(128)S(6)} %select_n.7), kind=kOutput, calls=%fused_computation.14 | convolution fusion | flops 268435456 | bytes 2359300 | tf_op jit(solution)/shard_map/dot_general | solution.py:31
  64.2 1.7 %fusion.g_ref = bf16[256,1024]{1,0:T(8,128)(2,1)S(1)} fusion(f32[256,1024]{1,0:T(8,128)S(1)} %fusion.4, bf16[1024,512]{1,0:T(8,128)(2,1)} %collective-permute-done, bf16[256,1024]{1,0:T(8,128)(2,1)S(1)} %bitcast.31, s32[]{:T(128)S(6)} %select_n.8), kind=kOutput, calls=%fused_computation.3 | convolution fusion | flops 268959744 | bytes 2883588 | tf_op jit(solution)/shard_map/dot_general | solution.py:31
  65.9 4.2 %attention_backward.2 = (bf16[256,1024]{1,0:T(8,128)(2,1)}, bf16[256,1024]{1,0:T(8,128)(2,1)}, bf16[256,1024]{1,0:T(8,128)(2,1)}, bf16[2,256,512]{2,1,0:T(8,128)(2,1)}, bf16[2,256,512]{2,1,0:T(8,128)(2,1)}) custom-call(bf16[256,1024]{1,0:T(8,128)(2,1)S(1)} %bitcast.46, bf16[256,1024]{1,0:T(8,128)(2,1)S(1)} %fusion.g_ref, ...), custom_call_target="tpu_custom_call" | custom-call | flops 1000000 | bytes 100000 | tf_op jit(solution)/shard_map/attention_backward/pallas_call | solution.py:232
  70.1 2.1 %collective-permute-start.8 = (bf16[2,256,512]{2,1,0:T(8,128)(2,1)}, bf16[2,256,512]{2,1,0:T(8,128)(2,1)}, u32[]{:S(2)}, u32[]{:S(2)}) collective-permute-start(bf16[2,256,512]{2,1,0:T(8,128)(2,1)} %get-tuple-element.39), channel_id=1, source_target_pairs={{0,1},{1,2},{2,3},{3,4},{4,5},{5,6},{6,7},{7,8},{8,9},{9,10},{10,1... | collective-permute-start | bytes 1572872 | tf_op jit(solution)/shard_map/ppermute | solution.py:271
  72.2 3.3 %collective-permute-start.9 = (bf16[2,256,512]{2,1,0:T(8,128)(2,1)}, bf16[2,256,512]{2,1,0:T(8,128)(2,1)}, u32[]{:S(2)}, u32[]{:S(2)}) collective-permute-start(bf16[2,256,512]{2,1,0:T(8,128)(2,1)} %get-tuple-element.40), channel_id=1, source_target_pairs={{1,0},{2,1},{3,2},{4,3},{5,4},{6,5},{7,6},{8,7},{9,8},{10,9},{11,1... | collective-permute-start | bytes 1572872 | tf_op jit(solution)/shard_map/ppermute | solution.py:271
  75.5 0.2 all-to-all-done.2
  75.7 2.2 %reduce_sum.33 = bf16[256,512]{1,0:T(8,128)(2,1)} reduce(bf16[4,256,512]{2,1,0:T(8,128)(2,1)} %all-to-all-done.2, bf16[]{:T(256)} %constant.38.clone.1), dimensions={0}, to_apply=%region_0.0 | reduce | flops 393216 | bytes 1310722 | tf_op jit(solution)/shard_map/reduce_sum | solution.py:290
  77.9 7.5 %all-to-all-start.3 = ((bf16[16,16,512]{2,1,0:T(8,128)(2,1)}), bf16[16,16,512]{2,1,0:T(8,128)(2,1)S(1)}, u32[]{:S(2)}, u32[]{:S(2)}) async-start(bf16[16,16,512]{2,1,0:T(8,128)(2,1)} %bitcast.13), calls=%async_computation.3 | async-start | bytes 524288 | tf_op jit(solution)/shard_map/all_to_all | solution.py:289
  85.4 1.7 %copy-done.6 = bf16[4,2,640,256]{3,2,1,0:T(8,128)(2,1)S(1)} copy-done((bf16[4,2,640,256]{3,2,1,0:T(8,128)(2,1)S(1)}, bf16[4,2,640,256]{3,2,1,0:T(8,128)(2,1)}, u32[]{:S(2)}) %copy-start.6) | copy-done | bytes 2621464
  87.2 5.0 %attention_backward.3 = (bf16[256,1024]{1,0:T(8,128)(2,1)}, bf16[256,1024]{1,0:T(8,128)(2,1)}, bf16[256,1024]{1,0:T(8,128)(2,1)}, bf16[2,256,512]{2,1,0:T(8,128)(2,1)}, bf16[2,256,512]{2,1,0:T(8,128)(2,1)}) custom-call(bf16[256,1024]{1,0:T(8,128)(2,1)S(1)} %bitcast.47, ...), custom_call_target="tpu_custom_call", output_to_operand_aliasing={{0}: (10, {}), {1}: (11, {}), {2}: (12, {})} | custom-call | flops 1000000 | bytes 100000 | tf_op jit(solution)/shard_map/attention_backward/pallas_call | solution.py:232
  92.1 3.1 %collective-permute-start.5 = (bf16[2,256,512]{2,1,0:T(8,128)(2,1)}, bf16[2,256,512]{2,1,0:T(8,128)(2,1)S(1)}, u32[]{:S(2)}, u32[]{:S(2)}) collective-permute-start(bf16[2,256,512]{2,1,0:T(8,128)(2,1)} %get-tuple-element.37), channel_id=1, source_target_pairs={{0,1},{1,2},{2,3},{3,4},{4,5},{5,6},{6,7},{7,8},{8,9},{9,10},{10,1... | collective-permute-start | bytes 1572872 | tf_op jit(solution)/shard_map/ppermute | solution.py:271
  95.2 2.2 %collective-permute-start.6 = (bf16[2,256,512]{2,1,0:T(8,128)(2,1)}, bf16[2,256,512]{2,1,0:T(8,128)(2,1)S(1)}, u32[]{:S(2)}, u32[]{:S(2)}) collective-permute-start(bf16[2,256,512]{2,1,0:T(8,128)(2,1)} %get-tuple-element.38), channel_id=1, source_target_pairs={{1,0},{2,1},{3,2},{4,3},{5,4},{6,5},{7,6},{8,7},{9,8},{10,9},{11,1... | collective-permute-start | bytes 1572872 | tf_op jit(solution)/shard_map/ppermute | solution.py:271
  97.5 0.7 broadcast_in_dim.22
  98.2 11.4 %all-to-all-start.4 = ((bf16[8,16,512]{2,1,0:T(8,128)(2,1)}), bf16[8,16,512]{2,1,0:T(8,128)(2,1)S(1)}, u32[]{:S(2)}, u32[]{:S(2)}) async-start(bf16[8,16,512]{2,1,0:T(8,128)(2,1)} %broadcast_in_dim.22), calls=%async_computation.4 | async-start | bytes 262144 | tf_op jit(solution)/shard_map/all_to_all | solution.py:283
  109.6 2.1 %add_arrived.2 = (bf16[256,1024]{1,0:T(8,128)(2,1)}, bf16[256,1024]{1,0:T(8,128)(2,1)}) custom-call(bf16[2,256,512]{2,1,0:T(8,128)(2,1)} %collective-permute-done.8.below_ref, bf16[2,256,512]{2,1,0:T(8,128)(2,1)} %collective-permute-done.9.above_ref, bf16[256,1024]{1,0:T(8,128)(2,1)} %get-tuple-element.43.own_key_ref, ...), custom_call_target="tpu_custom_call", output_to_operand_aliasing={{0}: (2, {}), {1}: (3, {})} | custom-call | flops 1000000 | bytes 100000 | tf_op jit(solution)/shard_map/add_arrived/pallas_call | solution.py:256
  111.7 0.8 copy-done.16
  112.5 0.2 copy-done.17
  112.7 2.1 %add_arrived.3 = (bf16[256,1024]{1,0:T(8,128)(2,1)}, bf16[256,1024]{1,0:T(8,128)(2,1)}) custom-call(bf16[2,256,512]{2,1,0:T(8,128)(2,1)} %copy-done.16, bf16[2,256,512]{2,1,0:T(8,128)(2,1)} %copy-done.17, bf16[256,1024]{1,0:T(8,128)(2,1)} %get-tuple-element.45.own_key_ref, ...), custom_call_target="tpu_custom_call", output_to_operand_aliasing={{0}: (2, {}), {1}: (3, {})} | custom-call | flops 1000000 | bytes 100000 | tf_op jit(solution)/shard_map/add_arrived/pallas_call | solution.py:256
  114.8 8.8 %all-to-all-done.4 = bf16[8,16,512]{2,1,0:T(8,128)(2,1)S(1)} async-done(((bf16[8,16,512]{2,1,0:T(8,128)(2,1)}), bf16[8,16,512]{2,1,0:T(8,128)(2,1)S(1)}, u32[]{:S(2)}, u32[]{:S(2)}) %all-to-all-start.4) | async-done | bytes 131104 | tf_op jit(solution)/shard_map/all_to_all | solution.py:283
  123.6 0.6 maximum_multiply_fusion
  (42 shorter events, 0.2 us)
Async XLA Ops:
  0.6 45.6 %copy-start = (bf16[1,2,128,1024]{3,2,1,0:T(8,128)(2,1)S(1)}, bf16[1,2,128,1024]{3,2,1,0:T(8,128)(2,1)}, u32[]{:S(2)}) copy-start(bf16[1,2,128,1024]{3,2,1,0:T(8,128)(2,1)} %param.12) | copy-start | bytes 1572868
  0.6 7.5 %copy-start.18 = (bf16[16,1024]{1,0:T(8,128)(2,1)S(1)}, bf16[16,1024]{1,0:T(8,128)(2,1)}, u32[]{:S(2)}) copy-start(bf16[16,1024]{1,0:T(8,128)(2,1)} %param.13) | copy-start | bytes 98308
  2.8 30.8 %collective-permute-start.3 = (bf16[2,256,512]{2,1,0:T(8,128)(2,1)}, bf16[2,256,512]{2,1,0:T(8,128)(2,1)S(1)}, u32[]{:S(2)}, u32[]{:S(2)}) collective-permute-start(bf16[2,256,512]{2,1,0:T(8,128)(2,1)} %pad_maximum_fusion.1), channel_id=1, source_target_pairs={{0,1},{1,2},{2,3},{3,4},{4,5},{5,6},{6,7},{7,8},{8,9},{9,10},{10,1... | collective-permute-start | bytes 1572872 | tf_op jit(solution)/shard_map/ppermute | solution.py:271
  6.0 27.6 %collective-permute-start.4 = (bf16[2,256,512]{2,1,0:T(8,128)(2,1)}, bf16[2,256,512]{2,1,0:T(8,128)(2,1)S(1)}, u32[]{:S(2)}, u32[]{:S(2)}) collective-permute-start(bf16[2,256,512]{2,1,0:T(8,128)(2,1)} %pad_maximum_fusion.1), channel_id=1, source_target_pairs={{1,0},{2,1},{3,2},{4,3},{5,4},{6,5},{7,6},{8,7},{9,8},{10,9},{11,1... | collective-permute-start | bytes 1572872 | tf_op jit(solution)/shard_map/ppermute | solution.py:271
  8.9 19.3 %all-to-all-start = ((bf16[16,16,512]{2,1,0:T(8,128)(2,1)}), bf16[16,16,512]{2,1,0:T(8,128)(2,1)S(1)}, u32[]{:S(2)}, u32[]{:S(2)}) async-start(bf16[16,16,512]{2,1,0:T(8,128)(2,1)} %broadcast_in_dim.8), calls=%async_computation | async-start | bytes 524288 | tf_op jit(solution)/shard_map/all_to_all | solution.py:283
  18.2 15.4 %copy-start.1 = (bf16[1,2,128,1024]{3,2,1,0:T(8,128)(2,1)S(1)}, bf16[1,2,128,1024]{3,2,1,0:T(8,128)(2,1)}, u32[]{:S(2)}) copy-start(bf16[1,2,128,1024]{3,2,1,0:T(8,128)(2,1)} %param.11) | copy-start | bytes 1572868
  18.2 15.5 %copy-start.2 = (bf16[1,2,128,1024]{3,2,1,0:T(8,128)(2,1)S(1)}, bf16[1,2,128,1024]{3,2,1,0:T(8,128)(2,1)}, u32[]{:S(2)}) copy-start(bf16[1,2,128,1024]{3,2,1,0:T(8,128)(2,1)} %param.10) | copy-start | bytes 1572868
  18.2 15.4 %copy-start.12 = (s32[128]{0:T(128)S(1)}, s32[128]{0:T(128)}, u32[]{:S(2)}) copy-start(s32[128]{0:T(128)} %lo_ref.3) | copy-start | bytes 1540
  18.3 15.4 %copy-start.13 = (s32[128]{0:T(128)S(1)}, s32[128]{0:T(128)}, u32[]{:S(2)}) copy-start(s32[128]{0:T(128)} %hi_ref.3) | copy-start | bytes 1540
  18.3 15.4 %copy-start.14 = (s32[128]{0:T(128)S(1)}, s32[128]{0:T(128)}, u32[]{:S(2)}) copy-start(s32[128]{0:T(128)} %half_ref.3) | copy-start | bytes 1540
  18.3 15.4 %copy-start.15 = (f32[128]{0:T(128)S(1)}, f32[128]{0:T(128)}, u32[]{:S(2)}) copy-start(f32[128]{0:T(128)} %constant.41.clone.logw_ref) | copy-start | bytes 1540
  19.1 21.2 %collective-permute-start.1 = (bf16[2,256,512]{2,1,0:T(8,128)(2,1)}, bf16[2,256,512]{2,1,0:T(8,128)(2,1)}, u32[]{:S(2)}, u32[]{:S(2)}) collective-permute-start(bf16[2,256,512]{2,1,0:T(8,128)(2,1)} %pad_maximum_fusion), channel_id=1, source_target_pairs={{0,1},{1,2},{2,3},{3,4},{4,5},{5,6},{6,7},{7,8},{8,9},{9,10},{10,1... | collective-permute-start | bytes 1572872 | tf_op jit(solution)/shard_map/ppermute | solution.py:271
  22.2 18.1 %collective-permute-start.2 = (bf16[2,256,512]{2,1,0:T(8,128)(2,1)}, bf16[2,256,512]{2,1,0:T(8,128)(2,1)}, u32[]{:S(2)}, u32[]{:S(2)}) collective-permute-start(bf16[2,256,512]{2,1,0:T(8,128)(2,1)} %pad_maximum_fusion), channel_id=1, source_target_pairs={{1,0},{2,1},{3,2},{4,3},{5,4},{6,5},{7,6},{8,7},{9,8},{10,9},{11,1... | collective-permute-start | bytes 1572872 | tf_op jit(solution)/shard_map/ppermute | solution.py:271
  29.2 23.4 %all-to-all-start.1 = ((bf16[4,256,512]{2,1,0:T(8,128)(2,1)}), bf16[4,256,512]{2,1,0:T(8,128)(2,1)}, u32[]{:S(2)}, u32[]{:S(2)}) async-start(bf16[4,256,512]{2,1,0:T(8,128)(2,1)} %broadcast_in_dim.10), calls=%async_computation.1 | async-start | bytes 2097152 | tf_op jit(solution)/shard_map/all_to_all | solution.py:315
  33.7 5.1 %copy-start.7 = (bf16[2,256,512]{2,1,0:T(8,128)(2,1)}, bf16[2,256,512]{2,1,0:T(8,128)(2,1)S(1)}, u32[]{:S(2)}) copy-start(bf16[2,256,512]{2,1,0:T(8,128)(2,1)S(1)} %collective-permute-done.4.kn_ref.vn_ref) | copy-start | bytes 1572868
  33.7 1.2 copy-start.9
  38.8 1.5 %copy-start.3 = (bf16[4,2,640,256]{3,2,1,0:T(8,128)(2,1)}, bf16[4,2,640,256]{3,2,1,0:T(8,128)(2,1)S(1)}, u32[]{:S(2)}) copy-start(bf16[4,2,640,256]{3,2,1,0:T(8,128)(2,1)S(1)} %get-tuple-element.32.prob_ref) | copy-start | bytes 7864324
  44.7 1.5 %copy-start.5 = (bf16[4,2,640,256]{3,2,1,0:T(8,128)(2,1)}, bf16[4,2,640,256]{3,2,1,0:T(8,128)(2,1)S(1)}, u32[]{:S(2)}) copy-start(bf16[4,2,640,256]{3,2,1,0:T(8,128)(2,1)S(1)} %get-tuple-element.31.prob_ref) | copy-start | bytes 7864324
  47.7 7.5 %collective-permute-start.7 = (bf16[1024,512]{1,0:T(8,128)(2,1)}, bf16[1024,512]{1,0:T(8,128)(2,1)}, u32[]{:S(2)}, u32[]{:S(2)}) collective-permute-start(bf16[1024,512]{1,0:T(8,128)(2,1)} %convolution_convert_fusion), channel_id=1, source_target_pairs={{0,64},{64,0},{1,65},{65,1},{2,66},{66,2},{3,67},{67,3},{4,68},{68... | collective-permute-start | bytes 3145736 | tf_op jit(solution)/shard_map/ppermute | solution.py:275
  52.7 11.5 %collective-permute-start = (bf16[1024,512]{1,0:T(8,128)(2,1)}, bf16[1024,512]{1,0:T(8,128)(2,1)}, u32[]{:S(2)}, u32[]{:S(2)}) collective-permute-start(bf16[1024,512]{1,0:T(8,128)(2,1)} %bitcast.3), channel_id=1, source_target_pairs={{0,64},{64,0},{1,65},{65,1},{2,66},{66,2},{3,67},{67,3},{4,68},{68... | collective-permute-start | bytes 3145736 | tf_op jit(solution)/shard_map/ppermute | solution.py:275
  58.0 17.7 %all-to-all-start.2 = ((bf16[4,256,512]{2,1,0:T(8,128)(2,1)}), bf16[4,256,512]{2,1,0:T(8,128)(2,1)}, u32[]{:S(2)}, u32[]{:S(2)}) async-start(bf16[4,256,512]{2,1,0:T(8,128)(2,1)} %bitcast.50), calls=%async_computation.2 | async-start | bytes 2097152 | tf_op jit(solution)/shard_map/all_to_all | solution.py:289
  62.3 3.6 %copy-start.4 = (bf16[4,2,640,256]{3,2,1,0:T(8,128)(2,1)S(1)}, bf16[4,2,640,256]{3,2,1,0:T(8,128)(2,1)}, u32[]{:S(2)}) copy-start(bf16[4,2,640,256]{3,2,1,0:T(8,128)(2,1)} %copy-done.3) | copy-start | bytes 7864324
  62.3 3.6 %copy-start.8 = (bf16[2,256,512]{2,1,0:T(8,128)(2,1)S(1)}, bf16[2,256,512]{2,1,0:T(8,128)(2,1)}, u32[]{:S(2)}) copy-start(bf16[2,256,512]{2,1,0:T(8,128)(2,1)} %copy-done.7) | copy-start | bytes 1572868
  62.3 3.6 %copy-start.10 = (bf16[1,2,128,1024]{3,2,1,0:T(8,128)(2,1)S(1)}, bf16[1,2,128,1024]{3,2,1,0:T(8,128)(2,1)}, u32[]{:S(2)}) copy-start(bf16[1,2,128,1024]{3,2,1,0:T(8,128)(2,1)} %param.9) | copy-start | bytes 1572868
  70.1 15.3 %copy-start.11 = (bf16[1,2,128,1024]{3,2,1,0:T(8,128)(2,1)S(1)}, bf16[1,2,128,1024]{3,2,1,0:T(8,128)(2,1)}, u32[]{:S(2)}) copy-start(bf16[1,2,128,1024]{3,2,1,0:T(8,128)(2,1)} %param.9) | copy-start | bytes 1572868
  70.1 27.4 %collective-permute-start.8 = (bf16[2,256,512]{2,1,0:T(8,128)(2,1)}, bf16[2,256,512]{2,1,0:T(8,128)(2,1)}, u32[]{:S(2)}, u32[]{:S(2)}) collective-permute-start(bf16[2,256,512]{2,1,0:T(8,128)(2,1)} %get-tuple-element.39), channel_id=1, source_target_pairs={{0,1},{1,2},{2,3},{3,4},{4,5},{5,6},{6,7},{7,8},{8,9},{9,10},{10,1... | collective-permute-start | bytes 1572872 | tf_op jit(solution)/shard_map/ppermute | solution.py:271
  72.2 25.3 %collective-permute-start.9 = (bf16[2,256,512]{2,1,0:T(8,128)(2,1)}, bf16[2,256,512]{2,1,0:T(8,128)(2,1)}, u32[]{:S(2)}, u32[]{:S(2)}) collective-permute-start(bf16[2,256,512]{2,1,0:T(8,128)(2,1)} %get-tuple-element.40), channel_id=1, source_target_pairs={{1,0},{2,1},{3,2},{4,3},{5,4},{6,5},{7,6},{8,7},{9,8},{10,9},{11,1... | collective-permute-start | bytes 1572872 | tf_op jit(solution)/shard_map/ppermute | solution.py:271
  77.9 19.6 %all-to-all-start.3 = ((bf16[16,16,512]{2,1,0:T(8,128)(2,1)}), bf16[16,16,512]{2,1,0:T(8,128)(2,1)S(1)}, u32[]{:S(2)}, u32[]{:S(2)}) async-start(bf16[16,16,512]{2,1,0:T(8,128)(2,1)} %bitcast.13), calls=%async_computation.3 | async-start | bytes 524288 | tf_op jit(solution)/shard_map/all_to_all | solution.py:289
  85.4 1.7 %copy-start.6 = (bf16[4,2,640,256]{3,2,1,0:T(8,128)(2,1)S(1)}, bf16[4,2,640,256]{3,2,1,0:T(8,128)(2,1)}, u32[]{:S(2)}) copy-start(bf16[4,2,640,256]{3,2,1,0:T(8,128)(2,1)} %copy-done.5) | copy-start | bytes 7864324
  92.1 19.6 %collective-permute-start.5 = (bf16[2,256,512]{2,1,0:T(8,128)(2,1)}, bf16[2,256,512]{2,1,0:T(8,128)(2,1)S(1)}, u32[]{:S(2)}, u32[]{:S(2)}) collective-permute-start(bf16[2,256,512]{2,1,0:T(8,128)(2,1)} %get-tuple-element.37), channel_id=1, source_target_pairs={{0,1},{1,2},{2,3},{3,4},{4,5},{5,6},{6,7},{7,8},{8,9},{9,10},{10,1... | collective-permute-start | bytes 1572872 | tf_op jit(solution)/shard_map/ppermute | solution.py:271
  95.2 16.5 %collective-permute-start.6 = (bf16[2,256,512]{2,1,0:T(8,128)(2,1)}, bf16[2,256,512]{2,1,0:T(8,128)(2,1)S(1)}, u32[]{:S(2)}, u32[]{:S(2)}) collective-permute-start(bf16[2,256,512]{2,1,0:T(8,128)(2,1)} %get-tuple-element.38), channel_id=1, source_target_pairs={{1,0},{2,1},{3,2},{4,3},{5,4},{6,5},{7,6},{8,7},{9,8},{10,9},{11,1... | collective-permute-start | bytes 1572872 | tf_op jit(solution)/shard_map/ppermute | solution.py:271
  98.2 25.4 %all-to-all-start.4 = ((bf16[8,16,512]{2,1,0:T(8,128)(2,1)}), bf16[8,16,512]{2,1,0:T(8,128)(2,1)S(1)}, u32[]{:S(2)}, u32[]{:S(2)}) async-start(bf16[8,16,512]{2,1,0:T(8,128)(2,1)} %broadcast_in_dim.22), calls=%async_computation.4 | async-start | bytes 262144 | tf_op jit(solution)/shard_map/all_to_all | solution.py:283
  111.7 0.8 copy-start.16
  111.7 1.0 copy-start.17
